TPU v7x, 32 devices: a whole 2x2x4 slice. The times are simulated.
32 devices in a mesh: row: 2 (over x), col: 16 (over z, y, core).
Axes of the slice: x: 2, y: 2, z: 4, core: 2. Of those that a mesh axis runs over, the one named last changes fastest.
Arguments:
- density: float32 [2048, 1216], P(('row', 'col')), as said below
- pattern: int32 [32, 19], P(('row', 'col')), may hold values from 0 to 1, as said below
Outputs:
- purified: float32 [2048, 1216], P(('row', 'col'))
Inputs may be any that keep to these rules, and one draw needn't show every extreme that they name: pattern[i, s] equals pattern[i + s - 9, 18 - s]; pattern[i, 9] is 1; pattern[i, s] is 0 where i + s - 9 lies outside 0 to 31. `density`: block (i, s) is zero where pattern is 0.
All inputs are finite; a program needn't handle non-finite values.
Results may differ from a plain program's by a relative error of at most 0.007.
Values may be sent and summed in bfloat16 or wider, within the bound.
No kernel may reach another device: no remote copies, remote signals or barrier semaphores. Data moves between devices by JAX's collectives and lax.ppermute only.
A program may use at most 64 MiB of HBM per device.

v0:
```python
import jax
import jax.numpy as jnp
from jax import lax
from jax.sharding import PartitionSpec as P

STEPS = 2


def from_behind(value, axis, steps):
    count = lax.axis_size(axis)
    first, last = (max(0, -steps), min(count, count - steps))
    return lax.ppermute(value, axis, [(source, source + steps) for source in range(first, last)])


def apply_mask(values, pattern_rows, block_size):
    rows_total, full_width = values.shape
    blocks = rows_total // block_size
    slot_count = pattern_rows.shape[1]
    shaped = values.reshape(blocks, block_size, slot_count, block_size)
    factor = pattern_rows.astype(jnp.float32)[:, None, :, None]
    return (shaped * factor).reshape(rows_total, full_width)


def band_product(left_rows, far_rows, half_band, block_size):
    rows_total = left_rows.shape[0]
    blocks = rows_total // block_size
    slot_count = 2 * half_band + 1
    outputs = []
    for out_slot in range(slot_count):
        first_slot = max(0, out_slot - half_band)
        last_slot = min(2 * half_band, out_slot + half_band)
        slot_span = last_slot - first_slot + 1
        shift_start = first_slot - out_slot + half_band
        left_part = left_rows[:, first_slot * block_size : (last_slot + 1) * block_size].reshape(
            blocks, block_size, slot_span * block_size
        )
        right_part = far_rows[
            out_slot * block_size : out_slot * block_size + rows_total,
            shift_start * block_size : (shift_start + slot_span) * block_size,
        ].reshape(blocks, block_size, slot_span * block_size)
        outputs.append(
            jnp.einsum("iax,ibx->iab", left_part, right_part, preferred_element_type=jnp.float32)
        )
    return jnp.stack(outputs, axis=2).reshape(rows_total, slot_count * block_size)


def local(density, pattern):
    rows_local, full_width = density.shape
    blocks_local, slot_count = pattern.shape
    block_size = rows_local // blocks_local
    half_band = (slot_count - 1) // 2
    reach_count = (half_band + blocks_local - 1) // blocks_local
    halo_rows = half_band * block_size
    current = density
    for iteration in range(STEPS):
        lowered = current.astype(jnp.bfloat16)
        lower_list = [
            from_behind(lowered, ("row", "col"), distance) for distance in range(reach_count, 0, -1)
        ]
        upper_list = [
            from_behind(lowered, ("row", "col"), -distance)
            for distance in range(1, reach_count + 1)
        ]
        lower_part = jnp.concatenate(lower_list, axis=0)
        upper_part = jnp.concatenate(upper_list, axis=0)
        far_rows = jnp.concatenate([lower_part, lowered, upper_part], axis=0)
        square = apply_mask(
            band_product(lowered, far_rows, half_band, block_size), pattern, block_size
        )
        square_low = square.astype(jnp.bfloat16)
        cube_term = band_product(square_low, far_rows, half_band, block_size)
        current = apply_mask(3.0 * square - 2.0 * cube_term, pattern, block_size)
    return current


def solution(mesh):
    placed = (P(("row", "col"), None), P(("row", "col"), None))
    return jax.shard_map(
        local, mesh=mesh, in_specs=placed, out_specs=P(("row", "col"), None), check_vma=False
    )
```

profile of v0, /device:TPU:0, one launch (start us, length us, event | category | flops | bytes accessed | tf_op | source)
XLA Modules:
  0.0 219.3 jit_solution(4818672890876887022)
XLA Ops:
  1.0 5.4 %collective-permute-start = (bf16[64,1216]{1,0:T(8,128)(2,1)S(1)}, bf16[64,1216]{1,0:T(8,128)(2,1)S(1)}, u32[]{:S(2)}, u32[]{:S(2)}) collective-permute-start(bf16[64,1216]{1,0:T(8,128)(2,1)S(1)} %convert_element_type.51), channel_id=1, source_target_pairs={{0,9},{1,10},{2,11},{3,12},{4,13},{5,14},{6,15},{7,16},{8,17},{9,1... | collective-permute-start | bytes 466952 | tf_op jit(solution)/shard_map/ppermute | solution.py:12
  6.4 3.2 %collective-permute-start.1 = (bf16[64,1216]{1,0:T(8,128)(2,1)S(1)}, bf16[64,1216]{1,0:T(8,128)(2,1)S(1)}, u32[]{:S(2)}, u32[]{:S(2)}) collective-permute-start(bf16[64,1216]{1,0:T(8,128)(2,1)S(1)} %convert_element_type.51), channel_id=1, source_target_pairs={{0,8},{1,9},{2,10},{3,11},{4,12},{5,13},{6,14},{7,15},{8,16},{9,17... | collective-permute-start | bytes 466952 | tf_op jit(solution)/shard_map/ppermute | solution.py:12
  9.6 4.5 %collective-permute-start.2 = (bf16[64,1216]{1,0:T(8,128)(2,1)S(1)}, bf16[64,1216]{1,0:T(8,128)(2,1)S(1)}, u32[]{:S(2)}, u32[]{:S(2)}) collective-permute-start(bf16[64,1216]{1,0:T(8,128)(2,1)S(1)} %convert_element_type.51), channel_id=1, source_target_pairs={{0,7},{1,8},{2,9},{3,10},{4,11},{5,12},{6,13},{7,14},{8,15},{9,16}... | collective-permute-start | bytes 466952 | tf_op jit(solution)/shard_map/ppermute | solution.py:12
  14.1 5.3 %collective-permute-start.3 = (bf16[64,1216]{1,0:T(8,128)(2,1)S(1)}, bf16[64,1216]{1,0:T(8,128)(2,1)S(1)}, u32[]{:S(2)}, u32[]{:S(2)}) collective-permute-start(bf16[64,1216]{1,0:T(8,128)(2,1)S(1)} %convert_element_type.51), channel_id=1, source_target_pairs={{0,6},{1,7},{2,8},{3,9},{4,10},{5,11},{6,12},{7,13},{8,14},{9,15},... | collective-permute-start | bytes 466952 | tf_op jit(solution)/shard_map/ppermute | solution.py:12
  19.4 1.3 collective-permute-start.4
  20.9 2.1 collective-permute-start.5
  23.3 3.4 %collective-permute-start.6 = (bf16[64,1216]{1,0:T(8,128)(2,1)S(1)}, bf16[64,1216]{1,0:T(8,128)(2,1)S(1)}, u32[]{:S(2)}, u32[]{:S(2)}) collective-permute-start(bf16[64,1216]{1,0:T(8,128)(2,1)S(1)} %convert_element_type.51), channel_id=1, source_target_pairs={{0,3},{1,4},{2,5},{3,6},{4,7},{5,8},{6,9},{7,10},{8,11},{9,12},{10... | collective-permute-start | bytes 466952 | tf_op jit(solution)/shard_map/ppermute | solution.py:12
  26.9 13.2 %collective-permute-start.7 = (bf16[64,1216]{1,0:T(8,128)(2,1)S(1)}, bf16[64,1216]{1,0:T(8,128)(2,1)S(1)}, u32[]{:S(2)}, u32[]{:S(2)}) collective-permute-start(bf16[64,1216]{1,0:T(8,128)(2,1)S(1)} %convert_element_type.51), channel_id=1, source_target_pairs={{0,2},{1,3},{2,4},{3,5},{4,6},{5,7},{6,8},{7,9},{8,10},{9,11},{10,... | collective-permute-start | bytes 466952 | tf_op jit(solution)/shard_map/ppermute | solution.py:12
  40.4 1.3 collective-permute-start.8
  41.9 1.3 collective-permute-start.9
  45.5 1.3 collective-permute-start.11
  52.2 1.3 collective-permute-start.14
  58.6 3.9 %collective-permute-done.12 = bf16[64,1216]{1,0:T(8,128)(2,1)S(1)} collective-permute-done((bf16[64,1216]{1,0:T(8,128)(2,1)S(1)}, bf16[64,1216]{1,0:T(8,128)(2,1)S(1)}, u32[]{:S(2)}, u32[]{:S(2)}) %collective-permute-start.12) | collective-permute-done | bytes 155680 | tf_op jit(solution)/shard_map/ppermute | solution.py:12
  64.8 4.0 %collective-permute-done.14 = bf16[64,1216]{1,0:T(8,128)(2,1)S(1)} collective-permute-done((bf16[64,1216]{1,0:T(8,128)(2,1)S(1)}, bf16[64,1216]{1,0:T(8,128)(2,1)S(1)}, u32[]{:S(2)}, u32[]{:S(2)}) %collective-permute-start.14) | collective-permute-done | bytes 155680 | tf_op jit(solution)/shard_map/ppermute | solution.py:12
  71.0 23.7 %collective-permute-done.16 = bf16[64,1216]{1,0:T(8,128)(2,1)S(1)} collective-permute-done((bf16[64,1216]{1,0:T(8,128)(2,1)S(1)}, bf16[64,1216]{1,0:T(8,128)(2,1)S(1)}, u32[]{:S(2)}, u32[]{:S(2)}) %collective-permute-start.16) | collective-permute-done | bytes 155680 | tf_op jit(solution)/shard_map/ppermute | solution.py:12
  106.2 1.3 collective-permute-start.18
  107.5 12.7 %collective-permute-start.19 = (bf16[64,1216]{1,0:T(8,128)(2,1)S(1)}, bf16[64,1216]{1,0:T(8,128)(2,1)S(1)}, u32[]{:S(2)}, u32[]{:S(2)}) collective-permute-start(bf16[64,1216]{1,0:T(8,128)(2,1)S(1)} %multiply_convert_fusion.2), channel_id=1, source_target_pairs={{0,8},{1,9},{2,10},{3,11},{4,12},{5,13},{6,14},{7,15},{8,16},{9,17... | collective-permute-start | bytes 466952 | tf_op jit(solution)/shard_map/ppermute | solution.py:12
  120.2 2.4 %collective-permute-start.20 = (bf16[64,1216]{1,0:T(8,128)(2,1)S(1)}, bf16[64,1216]{1,0:T(8,128)(2,1)S(1)}, u32[]{:S(2)}, u32[]{:S(2)}) collective-permute-start(bf16[64,1216]{1,0:T(8,128)(2,1)S(1)} %multiply_convert_fusion.2), channel_id=1, source_target_pairs={{0,7},{1,8},{2,9},{3,10},{4,11},{5,12},{6,13},{7,14},{8,15},{9,16}... | collective-permute-start | bytes 466952 | tf_op jit(solution)/shard_map/ppermute | solution.py:12
  122.6 1.3 collective-permute-start.21
  123.9 2.4 %collective-permute-start.22 = (bf16[64,1216]{1,0:T(8,128)(2,1)S(1)}, bf16[64,1216]{1,0:T(8,128)(2,1)S(1)}, u32[]{:S(2)}, u32[]{:S(2)}) collective-permute-start(bf16[64,1216]{1,0:T(8,128)(2,1)S(1)} %multiply_convert_fusion.2), channel_id=1, source_target_pairs={{0,5},{1,6},{2,7},{3,8},{4,9},{5,10},{6,11},{7,12},{8,13},{9,14},{... | collective-permute-start | bytes 466952 | tf_op jit(solution)/shard_map/ppermute | solution.py:12
  134.4 3.2 %collective-permute-start.23 = (bf16[64,1216]{1,0:T(8,128)(2,1)S(1)}, bf16[64,1216]{1,0:T(8,128)(2,1)S(1)}, u32[]{:S(2)}, u32[]{:S(2)}) collective-permute-start(bf16[64,1216]{1,0:T(8,128)(2,1)S(1)} %multiply_convert_fusion.2), channel_id=1, source_target_pairs={{0,4},{1,5},{2,6},{3,7},{4,8},{5,9},{6,10},{7,11},{8,12},{9,13},{1... | collective-permute-start | bytes 466952 | tf_op jit(solution)/shard_map/ppermute | solution.py:12
  137.9 2.9 %collective-permute-start.24 = (bf16[64,1216]{1,0:T(8,128)(2,1)S(1)}, bf16[64,1216]{1,0:T(8,128)(2,1)S(1)}, u32[]{:S(2)}, u32[]{:S(2)}) collective-permute-start(bf16[64,1216]{1,0:T(8,128)(2,1)S(1)} %multiply_convert_fusion.2), channel_id=1, source_target_pairs={{0,3},{1,4},{2,5},{3,6},{4,7},{5,8},{6,9},{7,10},{8,11},{9,12},{10... | collective-permute-start | bytes 466952 | tf_op jit(solution)/shard_map/ppermute | solution.py:12
  141.0 3.3 %collective-permute-start.25 = (bf16[64,1216]{1,0:T(8,128)(2,1)S(1)}, bf16[64,1216]{1,0:T(8,128)(2,1)S(1)}, u32[]{:S(2)}, u32[]{:S(2)}) collective-permute-start(bf16[64,1216]{1,0:T(8,128)(2,1)S(1)} %multiply_convert_fusion.2), channel_id=1, source_target_pairs={{0,2},{1,3},{2,4},{3,5},{4,6},{5,7},{6,8},{7,9},{8,10},{9,11},{10,... | collective-permute-start | bytes 466952 | tf_op jit(solution)/shard_map/ppermute | solution.py:12
  144.6 2.2 %collective-permute-start.26 = (bf16[64,1216]{1,0:T(8,128)(2,1)S(1)}, bf16[64,1216]{1,0:T(8,128)(2,1)S(1)}, u32[]{:S(2)}, u32[]{:S(2)}) collective-permute-start(bf16[64,1216]{1,0:T(8,128)(2,1)S(1)} %multiply_convert_fusion.2), channel_id=1, source_target_pairs={{0,1},{1,2},{2,3},{3,4},{4,5},{5,6},{6,7},{7,8},{8,9},{9,10},{10,1... | collective-permute-start | bytes 466952 | tf_op jit(solution)/shard_map/ppermute | solution.py:12
  148.6 1.3 collective-permute-start.28
  151.7 1.3 collective-permute-start.30
  156.6 4.5 %collective-permute-done.28 = bf16[64,1216]{1,0:T(8,128)(2,1)S(1)} collective-permute-done((bf16[64,1216]{1,0:T(8,128)(2,1)S(1)}, bf16[64,1216]{1,0:T(8,128)(2,1)S(1)}, u32[]{:S(2)}, u32[]{:S(2)}) %collective-permute-start.28) | collective-permute-done | bytes 155680 | tf_op jit(solution)/shard_map/ppermute | solution.py:12
  164.2 5.3 %collective-permute-done.30 = bf16[64,1216]{1,0:T(8,128)(2,1)S(1)} collective-permute-done((bf16[64,1216]{1,0:T(8,128)(2,1)S(1)}, bf16[64,1216]{1,0:T(8,128)(2,1)S(1)}, u32[]{:S(2)}, u32[]{:S(2)}) %collective-permute-start.30) | collective-permute-done | bytes 155680 | tf_op jit(solution)/shard_map/ppermute | solution.py:12
  169.5 1.5 collective-permute-start.35
  171.4 3.5 %collective-permute-done.32 = bf16[64,1216]{1,0:T(8,128)(2,1)S(1)} collective-permute-done((bf16[64,1216]{1,0:T(8,128)(2,1)S(1)}, bf16[64,1216]{1,0:T(8,128)(2,1)S(1)}, u32[]{:S(2)}, u32[]{:S(2)}) %collective-permute-start.32) | collective-permute-done | bytes 155680 | tf_op jit(solution)/shard_map/ppermute | solution.py:12
  175.1 1.6 collective-permute-done.33
  176.9 25.3 %collective-permute-done.34 = bf16[64,1216]{1,0:T(8,128)(2,1)S(1)} collective-permute-done((bf16[64,1216]{1,0:T(8,128)(2,1)S(1)}, bf16[64,1216]{1,0:T(8,128)(2,1)S(1)}, u32[]{:S(2)}, u32[]{:S(2)}) %collective-permute-start.34) | collective-permute-done | bytes 155680 | tf_op jit(solution)/shard_map/ppermute | solution.py:12
  (289 shorter events, 66.4 us)
Async XLA Ops:
  1.0 19.9 %collective-permute-start = (bf16[64,1216]{1,0:T(8,128)(2,1)S(1)}, bf16[64,1216]{1,0:T(8,128)(2,1)S(1)}, u32[]{:S(2)}, u32[]{:S(2)}) collective-permute-start(bf16[64,1216]{1,0:T(8,128)(2,1)S(1)} %convert_element_type.51), channel_id=1, source_target_pairs={{0,9},{1,10},{2,11},{3,12},{4,13},{5,14},{6,15},{7,16},{8,17},{9,1... | collective-permute-start | bytes 466952 | tf_op jit(solution)/shard_map/ppermute | solution.py:12
  6.4 16.9 %collective-permute-start.1 = (bf16[64,1216]{1,0:T(8,128)(2,1)S(1)}, bf16[64,1216]{1,0:T(8,128)(2,1)S(1)}, u32[]{:S(2)}, u32[]{:S(2)}) collective-permute-start(bf16[64,1216]{1,0:T(8,128)(2,1)S(1)} %convert_element_type.51), channel_id=1, source_target_pairs={{0,8},{1,9},{2,10},{3,11},{4,12},{5,13},{6,14},{7,15},{8,16},{9,17... | collective-permute-start | bytes 466952 | tf_op jit(solution)/shard_map/ppermute | solution.py:12
  9.6 17.3 %collective-permute-start.2 = (bf16[64,1216]{1,0:T(8,128)(2,1)S(1)}, bf16[64,1216]{1,0:T(8,128)(2,1)S(1)}, u32[]{:S(2)}, u32[]{:S(2)}) collective-permute-start(bf16[64,1216]{1,0:T(8,128)(2,1)S(1)} %convert_element_type.51), channel_id=1, source_target_pairs={{0,7},{1,8},{2,9},{3,10},{4,11},{5,12},{6,13},{7,14},{8,15},{9,16}... | collective-permute-start | bytes 466952 | tf_op jit(solution)/shard_map/ppermute | solution.py:12
  14.1 26.3 %collective-permute-start.3 = (bf16[64,1216]{1,0:T(8,128)(2,1)S(1)}, bf16[64,1216]{1,0:T(8,128)(2,1)S(1)}, u32[]{:S(2)}, u32[]{:S(2)}) collective-permute-start(bf16[64,1216]{1,0:T(8,128)(2,1)S(1)} %convert_element_type.51), channel_id=1, source_target_pairs={{0,6},{1,7},{2,8},{3,9},{4,10},{5,11},{6,12},{7,13},{8,14},{9,15},... | collective-permute-start | bytes 466952 | tf_op jit(solution)/shard_map/ppermute | solution.py:12
  19.4 22.4 %collective-permute-start.4 = (bf16[64,1216]{1,0:T(8,128)(2,1)S(1)}, bf16[64,1216]{1,0:T(8,128)(2,1)S(1)}, u32[]{:S(2)}, u32[]{:S(2)}) collective-permute-start(bf16[64,1216]{1,0:T(8,128)(2,1)S(1)} %convert_element_type.51), channel_id=1, source_target_pairs={{0,5},{1,6},{2,7},{3,8},{4,9},{5,10},{6,11},{7,12},{8,13},{9,14},{... | collective-permute-start | bytes 466952 | tf_op jit(solution)/shard_map/ppermute | solution.py:12
  20.9 23.1 %collective-permute-start.5 = (bf16[64,1216]{1,0:T(8,128)(2,1)S(1)}, bf16[64,1216]{1,0:T(8,128)(2,1)S(1)}, u32[]{:S(2)}, u32[]{:S(2)}) collective-permute-start(bf16[64,1216]{1,0:T(8,128)(2,1)S(1)} %convert_element_type.51), channel_id=1, source_target_pairs={{0,4},{1,5},{2,6},{3,7},{4,8},{5,9},{6,10},{7,11},{8,12},{9,13},{1... | collective-permute-start | bytes 466952 | tf_op jit(solution)/shard_map/ppermute | solution.py:12
  23.3 22.2 %collective-permute-start.6 = (bf16[64,1216]{1,0:T(8,128)(2,1)S(1)}, bf16[64,1216]{1,0:T(8,128)(2,1)S(1)}, u32[]{:S(2)}, u32[]{:S(2)}) collective-permute-start(bf16[64,1216]{1,0:T(8,128)(2,1)S(1)} %convert_element_type.51), channel_id=1, source_target_pairs={{0,3},{1,4},{2,5},{3,6},{4,7},{5,8},{6,9},{7,10},{8,11},{9,12},{10... | collective-permute-start | bytes 466952 | tf_op jit(solution)/shard_map/ppermute | solution.py:12
  26.9 20.8 %collective-permute-start.7 = (bf16[64,1216]{1,0:T(8,128)(2,1)S(1)}, bf16[64,1216]{1,0:T(8,128)(2,1)S(1)}, u32[]{:S(2)}, u32[]{:S(2)}) collective-permute-start(bf16[64,1216]{1,0:T(8,128)(2,1)S(1)} %convert_element_type.51), channel_id=1, source_target_pairs={{0,2},{1,3},{2,4},{3,5},{4,6},{5,7},{6,8},{7,9},{8,10},{9,11},{10,... | collective-permute-start | bytes 466952 | tf_op jit(solution)/shard_map/ppermute | solution.py:12
  44.0 10.3 %collective-permute-start.10 = (bf16[64,1216]{1,0:T(8,128)(2,1)S(1)}, bf16[64,1216]{1,0:T(8,128)(2,1)S(1)}, u32[]{:S(2)}, u32[]{:S(2)}) collective-permute-start(bf16[64,1216]{1,0:T(8,128)(2,1)S(1)} %convert_element_type.51), channel_id=1, source_target_pairs={{2,0},{3,1},{4,2},{5,3},{6,4},{7,5},{8,6},{9,7},{10,8},{11,9},{12,... | collective-permute-start | bytes 466952 | tf_op jit(solution)/shard_map/ppermute | solution.py:12
  45.5 10.9 %collective-permute-start.11 = (bf16[64,1216]{1,0:T(8,128)(2,1)S(1)}, bf16[64,1216]{1,0:T(8,128)(2,1)S(1)}, u32[]{:S(2)}, u32[]{:S(2)}) collective-permute-start(bf16[64,1216]{1,0:T(8,128)(2,1)S(1)} %convert_element_type.51), channel_id=1, source_target_pairs={{3,0},{4,1},{5,2},{6,3},{7,4},{8,5},{9,6},{10,7},{11,8},{12,9},{13... | collective-permute-start | bytes 466952 | tf_op jit(solution)/shard_map/ppermute | solution.py:12
  47.7 14.8 %collective-permute-start.12 = (bf16[64,1216]{1,0:T(8,128)(2,1)S(1)}, bf16[64,1216]{1,0:T(8,128)(2,1)S(1)}, u32[]{:S(2)}, u32[]{:S(2)}) collective-permute-start(bf16[64,1216]{1,0:T(8,128)(2,1)S(1)} %convert_element_type.51), channel_id=1, source_target_pairs={{4,0},{5,1},{6,2},{7,3},{8,4},{9,5},{10,6},{11,7},{12,8},{13,9},{1... | collective-permute-start | bytes 466952 | tf_op jit(solution)/shard_map/ppermute | solution.py:12
  49.8 14.2 %collective-permute-start.13 = (bf16[64,1216]{1,0:T(8,128)(2,1)S(1)}, bf16[64,1216]{1,0:T(8,128)(2,1)S(1)}, u32[]{:S(2)}, u32[]{:S(2)}) collective-permute-start(bf16[64,1216]{1,0:T(8,128)(2,1)S(1)} %convert_element_type.51), channel_id=1, source_target_pairs={{5,0},{6,1},{7,2},{8,3},{9,4},{10,5},{11,6},{12,7},{13,8},{14,9},{... | collective-permute-start | bytes 466952 | tf_op jit(solution)/shard_map/ppermute | solution.py:12
  52.2 16.7 %collective-permute-start.14 = (bf16[64,1216]{1,0:T(8,128)(2,1)S(1)}, bf16[64,1216]{1,0:T(8,128)(2,1)S(1)}, u32[]{:S(2)}, u32[]{:S(2)}) collective-permute-start(bf16[64,1216]{1,0:T(8,128)(2,1)S(1)} %convert_element_type.51), channel_id=1, source_target_pairs={{6,0},{7,1},{8,2},{9,3},{10,4},{11,5},{12,6},{13,7},{14,8},{15,9},... | collective-permute-start | bytes 466952 | tf_op jit(solution)/shard_map/ppermute | solution.py:12
  54.3 15.9 %collective-permute-start.15 = (bf16[64,1216]{1,0:T(8,128)(2,1)S(1)}, bf16[64,1216]{1,0:T(8,128)(2,1)S(1)}, u32[]{:S(2)}, u32[]{:S(2)}) collective-permute-start(bf16[64,1216]{1,0:T(8,128)(2,1)S(1)} %convert_element_type.51), channel_id=1, source_target_pairs={{7,0},{8,1},{9,2},{10,3},{11,4},{12,5},{13,6},{14,7},{15,8},{16,9}... | collective-permute-start | bytes 466952 | tf_op jit(solution)/shard_map/ppermute | solution.py:12
  56.4 38.3 %collective-permute-start.16 = (bf16[64,1216]{1,0:T(8,128)(2,1)S(1)}, bf16[64,1216]{1,0:T(8,128)(2,1)S(1)}, u32[]{:S(2)}, u32[]{:S(2)}) collective-permute-start(bf16[64,1216]{1,0:T(8,128)(2,1)S(1)} %convert_element_type.51), channel_id=1, source_target_pairs={{8,0},{9,1},{10,2},{11,3},{12,4},{13,5},{14,6},{15,7},{16,8},{17,9... | collective-permute-start | bytes 466952 | tf_op jit(solution)/shard_map/ppermute | solution.py:12
  62.5 33.7 %collective-permute-start.17 = (bf16[64,1216]{1,0:T(8,128)(2,1)S(1)}, bf16[64,1216]{1,0:T(8,128)(2,1)S(1)}, u32[]{:S(2)}, u32[]{:S(2)}) collective-permute-start(bf16[64,1216]{1,0:T(8,128)(2,1)S(1)} %convert_element_type.51), channel_id=1, source_target_pairs={{9,0},{10,1},{11,2},{12,3},{13,4},{14,5},{15,6},{16,7},{17,8},{18,... | collective-permute-start | bytes 466952 | tf_op jit(solution)/shard_map/ppermute | solution.py:12
  106.2 28.2 %collective-permute-start.18 = (bf16[64,1216]{1,0:T(8,128)(2,1)S(1)}, bf16[64,1216]{1,0:T(8,128)(2,1)S(1)}, u32[]{:S(2)}, u32[]{:S(2)}) collective-permute-start(bf16[64,1216]{1,0:T(8,128)(2,1)S(1)} %multiply_convert_fusion.2), channel_id=1, source_target_pairs={{0,9},{1,10},{2,11},{3,12},{4,13},{5,14},{6,15},{7,16},{8,17},{9,1... | collective-permute-start | bytes 466952 | tf_op jit(solution)/shard_map/ppermute | solution.py:12
  107.5 30.4 %collective-permute-start.19 = (bf16[64,1216]{1,0:T(8,128)(2,1)S(1)}, bf16[64,1216]{1,0:T(8,128)(2,1)S(1)}, u32[]{:S(2)}, u32[]{:S(2)}) collective-permute-start(bf16[64,1216]{1,0:T(8,128)(2,1)S(1)} %multiply_convert_fusion.2), channel_id=1, source_target_pairs={{0,8},{1,9},{2,10},{3,11},{4,12},{5,13},{6,14},{7,15},{8,16},{9,17... | collective-permute-start | bytes 466952 | tf_op jit(solution)/shard_map/ppermute | solution.py:12
  120.2 20.8 %collective-permute-start.20 = (bf16[64,1216]{1,0:T(8,128)(2,1)S(1)}, bf16[64,1216]{1,0:T(8,128)(2,1)S(1)}, u32[]{:S(2)}, u32[]{:S(2)}) collective-permute-start(bf16[64,1216]{1,0:T(8,128)(2,1)S(1)} %multiply_convert_fusion.2), channel_id=1, source_target_pairs={{0,7},{1,8},{2,9},{3,10},{4,11},{5,12},{6,13},{7,14},{8,15},{9,16}... | collective-permute-start | bytes 466952 | tf_op jit(solution)/shard_map/ppermute | solution.py:12
  122.6 22.0 %collective-permute-start.21 = (bf16[64,1216]{1,0:T(8,128)(2,1)S(1)}, bf16[64,1216]{1,0:T(8,128)(2,1)S(1)}, u32[]{:S(2)}, u32[]{:S(2)}) collective-permute-start(bf16[64,1216]{1,0:T(8,128)(2,1)S(1)} %multiply_convert_fusion.2), channel_id=1, source_target_pairs={{0,6},{1,7},{2,8},{3,9},{4,10},{5,11},{6,12},{7,13},{8,14},{9,15},... | collective-permute-start | bytes 466952 | tf_op jit(solution)/shard_map/ppermute | solution.py:12
  123.9 23.1 %collective-permute-start.22 = (bf16[64,1216]{1,0:T(8,128)(2,1)S(1)}, bf16[64,1216]{1,0:T(8,128)(2,1)S(1)}, u32[]{:S(2)}, u32[]{:S(2)}) collective-permute-start(bf16[64,1216]{1,0:T(8,128)(2,1)S(1)} %multiply_convert_fusion.2), channel_id=1, source_target_pairs={{0,5},{1,6},{2,7},{3,8},{4,9},{5,10},{6,11},{7,12},{8,13},{9,14},{... | collective-permute-start | bytes 466952 | tf_op jit(solution)/shard_map/ppermute | solution.py:12
  134.4 14.2 %collective-permute-start.23 = (bf16[64,1216]{1,0:T(8,128)(2,1)S(1)}, bf16[64,1216]{1,0:T(8,128)(2,1)S(1)}, u32[]{:S(2)}, u32[]{:S(2)}) collective-permute-start(bf16[64,1216]{1,0:T(8,128)(2,1)S(1)} %multiply_convert_fusion.2), channel_id=1, source_target_pairs={{0,4},{1,5},{2,6},{3,7},{4,8},{5,9},{6,10},{7,11},{8,12},{9,13},{1... | collective-permute-start | bytes 466952 | tf_op jit(solution)/shard_map/ppermute | solution.py:12
  137.9 12.2 %collective-permute-start.24 = (bf16[64,1216]{1,0:T(8,128)(2,1)S(1)}, bf16[64,1216]{1,0:T(8,128)(2,1)S(1)}, u32[]{:S(2)}, u32[]{:S(2)}) collective-permute-start(bf16[64,1216]{1,0:T(8,128)(2,1)S(1)} %multiply_convert_fusion.2), channel_id=1, source_target_pairs={{0,3},{1,4},{2,5},{3,6},{4,7},{5,8},{6,9},{7,10},{8,11},{9,12},{10... | collective-permute-start | bytes 466952 | tf_op jit(solution)/shard_map/ppermute | solution.py:12
  141.0 10.7 %collective-permute-start.25 = (bf16[64,1216]{1,0:T(8,128)(2,1)S(1)}, bf16[64,1216]{1,0:T(8,128)(2,1)S(1)}, u32[]{:S(2)}, u32[]{:S(2)}) collective-permute-start(bf16[64,1216]{1,0:T(8,128)(2,1)S(1)} %multiply_convert_fusion.2), channel_id=1, source_target_pairs={{0,2},{1,3},{2,4},{3,5},{4,6},{5,7},{6,8},{7,9},{8,10},{9,11},{10,... | collective-permute-start | bytes 466952 | tf_op jit(solution)/shard_map/ppermute | solution.py:12
  148.6 12.5 %collective-permute-start.28 = (bf16[64,1216]{1,0:T(8,128)(2,1)S(1)}, bf16[64,1216]{1,0:T(8,128)(2,1)S(1)}, u32[]{:S(2)}, u32[]{:S(2)}) collective-permute-start(bf16[64,1216]{1,0:T(8,128)(2,1)S(1)} %multiply_convert_fusion.2), channel_id=1, source_target_pairs={{2,0},{3,1},{4,2},{5,3},{6,4},{7,5},{8,6},{9,7},{10,8},{11,9},{12,... | collective-permute-start | bytes 466952 | tf_op jit(solution)/shard_map/ppermute | solution.py:12
  150.1 12.5 %collective-permute-start.29 = (bf16[64,1216]{1,0:T(8,128)(2,1)S(1)}, bf16[64,1216]{1,0:T(8,128)(2,1)S(1)}, u32[]{:S(2)}, u32[]{:S(2)}) collective-permute-start(bf16[64,1216]{1,0:T(8,128)(2,1)S(1)} %multiply_convert_fusion.2), channel_id=1, source_target_pairs={{3,0},{4,1},{5,2},{6,3},{7,4},{8,5},{9,6},{10,7},{11,8},{12,9},{13... | collective-permute-start | bytes 466952 | tf_op jit(solution)/shard_map/ppermute | solution.py:12
  151.7 17.8 %collective-permute-start.30 = (bf16[64,1216]{1,0:T(8,128)(2,1)S(1)}, bf16[64,1216]{1,0:T(8,128)(2,1)S(1)}, u32[]{:S(2)}, u32[]{:S(2)}) collective-permute-start(bf16[64,1216]{1,0:T(8,128)(2,1)S(1)} %multiply_convert_fusion.2), channel_id=1, source_target_pairs={{4,0},{5,1},{6,2},{7,3},{8,4},{9,5},{10,6},{11,7},{12,8},{13,9},{1... | collective-permute-start | bytes 466952 | tf_op jit(solution)/shard_map/ppermute | solution.py:12
  153.2 17.9 %collective-permute-start.31 = (bf16[64,1216]{1,0:T(8,128)(2,1)S(1)}, bf16[64,1216]{1,0:T(8,128)(2,1)S(1)}, u32[]{:S(2)}, u32[]{:S(2)}) collective-permute-start(bf16[64,1216]{1,0:T(8,128)(2,1)S(1)} %multiply_convert_fusion.2), channel_id=1, source_target_pairs={{5,0},{6,1},{7,2},{8,3},{9,4},{10,5},{11,6},{12,7},{13,8},{14,9},{... | collective-permute-start | bytes 466952 | tf_op jit(solution)/shard_map/ppermute | solution.py:12
  155.0 19.9 %collective-permute-start.32 = (bf16[64,1216]{1,0:T(8,128)(2,1)S(1)}, bf16[64,1216]{1,0:T(8,128)(2,1)S(1)}, u32[]{:S(2)}, u32[]{:S(2)}) collective-permute-start(bf16[64,1216]{1,0:T(8,128)(2,1)S(1)} %multiply_convert_fusion.2), channel_id=1, source_target_pairs={{6,0},{7,1},{8,2},{9,3},{10,4},{11,5},{12,6},{13,7},{14,8},{15,9},... | collective-permute-start | bytes 466952 | tf_op jit(solution)/shard_map/ppermute | solution.py:12
  161.1 15.6 %collective-permute-start.33 = (bf16[64,1216]{1,0:T(8,128)(2,1)S(1)}, bf16[64,1216]{1,0:T(8,128)(2,1)S(1)}, u32[]{:S(2)}, u32[]{:S(2)}) collective-permute-start(bf16[64,1216]{1,0:T(8,128)(2,1)S(1)} %multiply_convert_fusion.2), channel_id=1, source_target_pairs={{7,0},{8,1},{9,2},{10,3},{11,4},{12,5},{13,6},{14,7},{15,8},{16,9}... | collective-permute-start | bytes 466952 | tf_op jit(solution)/shard_map/ppermute | solution.py:12
  162.6 39.6 %collective-permute-start.34 = (bf16[64,1216]{1,0:T(8,128)(2,1)S(1)}, bf16[64,1216]{1,0:T(8,128)(2,1)S(1)}, u32[]{:S(2)}, u32[]{:S(2)}) collective-permute-start(bf16[64,1216]{1,0:T(8,128)(2,1)S(1)} %multiply_convert_fusion.2), channel_id=1, source_target_pairs={{8,0},{9,1},{10,2},{11,3},{12,4},{13,5},{14,6},{15,7},{16,8},{17,9... | collective-permute-start | bytes 466952 | tf_op jit(solution)/shard_map/ppermute | solution.py:12
  169.5 34.1 %collective-permute-start.35 = (bf16[64,1216]{1,0:T(8,128)(2,1)S(1)}, bf16[64,1216]{1,0:T(8,128)(2,1)S(1)}, u32[]{:S(2)}, u32[]{:S(2)}) collective-permute-start(bf16[64,1216]{1,0:T(8,128)(2,1)S(1)} %multiply_convert_fusion.2), channel_id=1, source_target_pairs={{9,0},{10,1},{11,2},{12,3},{13,4},{14,5},{15,6},{16,7},{17,8},{18,... | collective-permute-start | bytes 466952 | tf_op jit(solution)/shard_map/ppermute | solution.py:12
  (53 other events, 161.4 us)
where the time goes:
time: 222 us; the launch traced here: 219 us
  starting transfers between devices  94.8 us (43%)
  waiting for transfers between devices  74.6 us (34%)
  local copies, waits for them, and re-layouts  24.3 us (11%)
  matrix products  21.8 us (10%)
    ppermute x36, starting transfers between devices, from_behind(): lax.ppermute(value, axis, [(source, source + steps) for source in range(f...  94.8 us
    ppermute x36, waiting for transfers between devices, from_behind(): lax.ppermute(value, axis, [(source, source + steps) for source in range(f...  74.6 us
    unnamed x152, local copies, waits for them, and re-layouts  21.9 us
    dot_general x76, matrix products, band_product(): jnp.einsum('iax,ibx->iab', left_part, right_part, preferred_element_type=...  21.8 us
  transfers between devices with their start and end apart: 36, of which 12 were waited for; matrix products, arithmetic and copies ran while one was open for 6% of the time, Pallas kernels for 0%

commit v1 on v0

v1 whole, which is shorter than its diff:
```python
import jax
import jax.numpy as jnp
from jax import lax
from jax.experimental import pallas as pl
from jax.experimental.pallas import tpu as pltpu
from jax.sharding import PartitionSpec as P

AXES = ("row", "col")
GROUP = 32
Z_ORDER = (0, 1, 3, 2)


def after(value, *earlier):
    return lax.optimization_barrier((value,) + earlier)[0]


def join(*parts):
    return jnp.concatenate(parts, axis=0)


def send(value, count, target):
    pairs = [(source, target(source)) for source in range(count)]
    return lax.ppermute(value, AXES, [(s, t) for s, t in pairs if 0 <= t < count])


def along_z(value, count, step):
    return send(value, count, lambda d: (d & ~12) | (((d >> 2) + step) % 4 << 2))


def first_flip(parity):
    return 2 + 14 * parity


def flip_first(value, count):
    return send(value, count, lambda d: d ^ first_flip(d & 1))


def flip_second(value, count):
    return send(value, count, lambda d: d ^ (18 - first_flip(d & 1)))


def flip_core(value, count):
    return send(value, count, lambda d: d ^ 1)


def gather(row, count):
    near = along_z(row, count, 1)
    first = flip_first(row, count)
    next_near = along_z(after(row, first), count, 3)
    pair = join(row, first)
    own = [pair, flip_second(pair, count)]
    first = flip_first(near, count)
    far = along_z(after(row, near), count, 2)
    pair = join(near, first)
    ones = [pair, flip_second(pair, count)]
    others = flip_core(after(join(*own), first), count)
    first = flip_first(after(next_near, first), count)
    pair = join(next_near, first)
    threes = [pair, flip_second(pair, count)]
    others_one = flip_core(after(join(*ones), first), count)
    first = flip_first(after(far, first, ones[1]), count)
    direct = flip_second(after(far, ones[1]), count)
    others_three = flip_core(after(join(*threes), first), count)
    last = flip_second(first, count)
    twos = [join(far, first), join(direct, last)]
    others_two = flip_core(join(*twos), count)
    return own + ones + threes + twos + [others, others_one, others_three, others_two]


def nt_dot(left, right):
    return lax.dot_general(left, right, (((1,), (1,)), ((), ())), preferred_element_type=jnp.float32)


def purify_kernel(block, half, copies, *refs):
    pieces, out_ref = refs[: 12 * copies], refs[12 * copies]
    band_ref, next_ref, flag_ref, mask_ref = refs[12 * copies + 1 :]
    slots = 2 * half + 1
    width = (slots + 1) * block
    window = (2 * half + 4) * block
    place = lax.axis_index("row") * lax.axis_size("col") + lax.axis_index("col")
    local, start = place % GROUP, place // GROUP * GROUP
    parity = local % 2
    origin = place - parity - 2 * half

    band_ref[...] = jnp.zeros_like(band_ref)
    next_ref[...] = jnp.zeros_like(next_ref)
    flag_ref[...] = jnp.zeros_like(flag_ref)
    lanes = lax.broadcasted_iota(jnp.int32, (block, 128), 1)

    def put(piece, at, index, odd):
        offset = index - origin

        @pl.when((offset >= 0) & (offset < 4 * half + 2))
        def _():
            rows = pl.ds(pl.multiple_of(offset * block, block), block)
            column = pl.multiple_of((offset + 1) // 2 * 128, 128)
            low = (1 - odd) * block
            head = piece[at : at + block, :128].astype(jnp.float32)
            tail = piece[at : at + block, width - 128 :].astype(jnp.float32)
            head_kept = lanes >= low
            tail_kept = lanes < low + block
            band_ref[rows, pl.ds(column, 128)] = jnp.where(head_kept, head, 0.0).astype(jnp.bfloat16)
            band_ref[rows, pl.ds(column + 128, width - 256)] = piece[at : at + block, 128 : width - 128]
            band_ref[rows, pl.ds(column + width - 128, 128)] = jnp.where(tail_kept, tail, 0.0).astype(jnp.bfloat16)
            number = offset - half

            @pl.when((number >= 0) & (number < 20))
            def _():
                flags = jnp.where(head_kept, 0.0, head) + jnp.where(tail_kept, 0.0, tail)
                flag_ref[pl.ds(number % 4 * 8 + number // 4, 1), :] = flags[:1]

    for copy in range(copies):
        shift = start + (0, -GROUP, GROUP)[copy]
        for core in range(2):
            odd = parity if core == 0 else 1 - parity
            flip = first_flip(odd)
            for k, step in enumerate(Z_ORDER):
                base = (local & ~13) | ((((local >> 2) & 3) + 4 - step) % 4 << 2) | odd
                for number, turned in enumerate((base, base ^ flip, base ^ (18 - flip), base ^ 18)):
                    if core == 0:
                        piece, at = pieces[12 * copy + 2 * k + number // 2], number % 2 * block
                    else:
                        piece, at = pieces[12 * copy + 8 + k], number * block
                    put(piece, at, shift + turned, odd)

    spot = lax.broadcasted_iota(jnp.int32, (128, window), 0) % block
    column_block = lax.broadcasted_iota(jnp.int32, (128, window), 1) // block
    for q in range(4):
        spread = ((column_block == spot + q) & (spot < slots)).astype(jnp.bfloat16)
        mask_ref[q] = lax.dot_general(
            flag_ref[8 * q : 8 * q + 8, :].astype(jnp.bfloat16),
            spread,
            (((1,), (0,)), ((), ())),
            preferred_element_type=jnp.float32,
        )

    def group(m, carry):
        at = pl.multiple_of(m * 4 * block, 4 * block)
        columns = pl.ds(pl.multiple_of(10 * block + at, 128), window)
        kept = jnp.concatenate(
            [jnp.broadcast_to(mask_ref[q, pl.ds(m, 1), :], (block, window)) for q in range(4)], axis=0
        )
        far = band_ref[pl.ds(at, window), columns]
        square = kept * nt_dot(band_ref[pl.ds(half * block + at, 4 * block), columns], far)
        cube = nt_dot(square.astype(jnp.bfloat16), far)
        current = kept * (3.0 * square - 2.0 * cube)
        next_ref[pl.ds(block + at, 4 * block), pl.ds(at, window)] = current.astype(jnp.bfloat16)
        return carry

    lax.fori_loop(0, 5, group, 0)
    far = next_ref[:, 8 * block : 8 * block + window]
    mine = next_ref[pl.ds(pl.multiple_of((10 + parity) * block, block), block), 8 * block : 8 * block + window]
    kept = mask_ref[pl.ds(1 + parity, 1), 2:3, :].reshape(1, window)
    square = kept * nt_dot(mine, far)
    cube = nt_dot(square.astype(jnp.bfloat16), far)
    current = kept * (3.0 * square - 2.0 * cube)
    out_ref[...] = jnp.where(
        parity == 0,
        current[:, block : block + slots * block],
        current[:, 2 * block : 2 * block + slots * block],
    )


def local(density, pattern):
    block, width = density.shape
    slots = pattern.shape[1]
    half = (slots - 1) // 2
    count = lax.axis_size("row") * lax.axis_size("col")
    place = lax.axis_index("row") * lax.axis_size("col") + lax.axis_index("col")
    flags = jnp.broadcast_to(pattern.astype(jnp.bfloat16), (block, slots))
    flags = jnp.pad(flags, ((0, 0), (0, block - slots)))
    low = density.astype(jnp.bfloat16)
    row = jnp.where(
        place % 2 == 0,
        jnp.concatenate([flags, low], axis=1),
        jnp.concatenate([low, flags], axis=1),
    )
    pieces = gather(row, count)
    copies = 1
    if count > GROUP:
        pieces = (
            pieces
            + [send(piece, count, lambda d: d + GROUP) for piece in pieces]
            + [send(piece, count, lambda d: d - GROUP) for piece in pieces]
        )
        copies = 3

    def kernel(*refs):
        purify_kernel(block, half, copies, *refs)

    window = (2 * half + 4) * block
    return pl.pallas_call(
        kernel,
        out_shape=jax.ShapeDtypeStruct((block, width), jnp.float32),
        in_specs=[pl.BlockSpec(memory_space=pltpu.VMEM)] * len(pieces),
        out_specs=pl.BlockSpec(memory_space=pltpu.VMEM),
        scratch_shapes=[
            pltpu.VMEM(((4 * half + 2) * block, (6 * half + 4) * block), jnp.bfloat16),
            pltpu.VMEM((window, (4 * half + 2) * block), jnp.bfloat16),
            pltpu.VMEM((32, 128), jnp.float32),
            pltpu.VMEM((4, 8, window), jnp.float32),
        ],
        compiler_params=pltpu.CompilerParams(vmem_limit_bytes=56 * 2**20),
    )(*pieces)


def solution(mesh):
    placed = (P(AXES, None), P(AXES, None))
    return jax.shard_map(local, mesh=mesh, in_specs=placed, out_specs=P(AXES, None), check_vma=False)
```

time: 222 us -> 69.2 us (0.31)
  the two profiles are of different devices: /device:TPU:0 before, /device:TPU:13 now
where the time goes in v1:
time: 69.2 us; the launch traced here: 69 us
  waiting for transfers between devices  23.8 us (34%)
  Pallas kernels  22.1 us (32%)
  starting transfers between devices  16.8 us (24%)
  other arithmetic  3.48 us (5%)
  local copies, waits for them, and re-layouts  2.68 us (4%)
    ppermute x16, waiting for transfers between devices, send(): lax.ppermute(value, AXES, [(s, t) for s, t in pairs if 0 <= t < count])  23.8 us
    pallas_call x1, Pallas kernels, local(): pl.pallas_call(kernel, out_shape=jax.ShapeDtypeStruct((block, width), jnp...  22.1 us
    ppermute x16, starting transfers between devices, send(): lax.ppermute(value, AXES, [(s, t) for s, t in pairs if 0 <= t < count])  16.8 us
    unnamed x22, local copies, waits for them, and re-layouts  2.65 us
    concatenate x7, other arithmetic, join(): return jnp.concatenate(parts, axis=0)  1.72 us
  transfers between devices with their start and end apart: 16, of which 7 were waited for; matrix products, arithmetic and copies ran while one was open for 3% of the time, Pallas kernels for 0%

profile of v1, /device:TPU:13, one launch (start us, length us, event | category | flops | bytes accessed | tf_op | source)
XLA Modules:
  0.0 69.0 jit_solution(17159340574993524251)
XLA Ops:
  0.0 0.7 convert_bitcast_fusion
  0.7 1.0 %convert_element_type.9 = bf16[64,1216]{1,0:T(8,128)(2,1)S(1)} convert(f32[64,1216]{1,0:T(8,128)} %param.2) | non-fusion elementwise | flops 77824 | bytes 466944 | tf_op jit(solution)/shard_map/convert_element_type | solution.py:172
  1.8 1.3 %collective-permute-start.2 = (bf16[64,1280]{1,0:T(8,128)(2,1)S(1)}, bf16[64,1280]{1,0:T(8,128)(2,1)S(1)}, u32[]{:S(2)}, u32[]{:S(2)}) collective-permute-start(bf16[64,1280]{1,0:T(8,128)(2,1)S(1)} %maximum_select_fusion), channel_id=1, source_target_pairs={{0,4},{1,5},{2,6},{3,7},{4,8},{5,9},{6,10},{7,11},{8,12},{9,13},{1... | collective-permute-start | bytes 491528 | tf_op jit(solution)/shard_map/ppermute | solution.py:23
  3.2 1.2 %collective-permute-start = (bf16[64,1280]{1,0:T(8,128)(2,1)S(1)}, bf16[64,1280]{1,0:T(8,128)(2,1)S(1)}, u32[]{:S(2)}, u32[]{:S(2)}) collective-permute-start(bf16[64,1280]{1,0:T(8,128)(2,1)S(1)} %maximum_select_fusion), channel_id=1, source_target_pairs={{0,2},{1,17},{2,0},{3,19},{4,6},{5,21},{6,4},{7,23},{8,10},{9,25},... | collective-permute-start | bytes 491528 | tf_op jit(solution)/shard_map/ppermute | solution.py:23
  4.4 2.6 %collective-permute-done.2 = bf16[64,1280]{1,0:T(8,128)(2,1)S(1)} collective-permute-done((bf16[64,1280]{1,0:T(8,128)(2,1)S(1)}, bf16[64,1280]{1,0:T(8,128)(2,1)S(1)}, u32[]{:S(2)}, u32[]{:S(2)}) %collective-permute-start.2) | collective-permute-done | bytes 163872 | tf_op jit(solution)/shard_map/ppermute | solution.py:23
  6.9 2.3 %collective-permute-start.8 = (bf16[64,1280]{1,0:T(8,128)(2,1)S(1)}, bf16[64,1280]{1,0:T(8,128)(2,1)S(1)}, u32[]{:S(2)}, u32[]{:S(2)}) collective-permute-start(bf16[64,1280]{1,0:T(8,128)(2,1)S(1)} %maximum_select_fusion), channel_id=1, source_target_pairs={{0,8},{1,9},{2,10},{3,11},{4,12},{5,13},{6,14},{7,15},{8,0},{9,1},... | collective-permute-start | bytes 491528 | tf_op jit(solution)/shard_map/ppermute | solution.py:23
  9.4 0.3 collective-permute-start.1
  9.7 1.2 %collective-permute-start.3 = (bf16[64,1280]{1,0:T(8,128)(2,1)S(1)}, bf16[64,1280]{1,0:T(8,128)(2,1)S(1)}, u32[]{:S(2)}, u32[]{:S(2)}) collective-permute-start(bf16[64,1280]{1,0:T(8,128)(2,1)S(1)} %collective-permute-done.2), channel_id=1, source_target_pairs={{0,2},{1,17},{2,0},{3,19},{4,6},{5,21},{6,4},{7,23},{8,10},{9,25},... | collective-permute-start | bytes 491528 | tf_op jit(solution)/shard_map/ppermute | solution.py:23
  11.0 3.2 %collective-permute-done.3 = bf16[64,1280]{1,0:T(8,128)(2,1)S(1)} collective-permute-done((bf16[64,1280]{1,0:T(8,128)(2,1)S(1)}, bf16[64,1280]{1,0:T(8,128)(2,1)S(1)}, u32[]{:S(2)}, u32[]{:S(2)}) %collective-permute-start.3) | collective-permute-done | bytes 163872 | tf_op jit(solution)/shard_map/ppermute | solution.py:23
  14.2 6.2 %collective-permute-done.5 = bf16[64,1280]{1,0:T(8,128)(2,1)S(1)} collective-permute-done((bf16[64,1280]{1,0:T(8,128)(2,1)S(1)}, bf16[64,1280]{1,0:T(8,128)(2,1)S(1)}, u32[]{:S(2)}, u32[]{:S(2)}) %collective-permute-start.5) | collective-permute-done | bytes 163872 | tf_op jit(solution)/shard_map/ppermute | solution.py:23
  20.4 1.2 %collective-permute-start.6 = (bf16[64,1280]{1,0:T(8,128)(2,1)S(1)}, bf16[64,1280]{1,0:T(8,128)(2,1)S(1)}, u32[]{:S(2)}, u32[]{:S(2)}) collective-permute-start(bf16[64,1280]{1,0:T(8,128)(2,1)S(1)} %collective-permute-done.5), channel_id=1, source_target_pairs={{0,2},{1,17},{2,0},{3,19},{4,6},{5,21},{6,4},{7,23},{8,10},{9,25},... | collective-permute-start | bytes 491528 | tf_op jit(solution)/shard_map/ppermute | solution.py:23
  21.6 0.3 collective-permute-start.4
  21.9 2.9 %collective-permute-done.6 = bf16[64,1280]{1,0:T(8,128)(2,1)S(1)} collective-permute-done((bf16[64,1280]{1,0:T(8,128)(2,1)S(1)}, bf16[64,1280]{1,0:T(8,128)(2,1)S(1)}, u32[]{:S(2)}, u32[]{:S(2)}) %collective-permute-start.6) | collective-permute-done | bytes 163872 | tf_op jit(solution)/shard_map/ppermute | solution.py:23
  24.9 0.4 collective-permute-start.7
  25.3 0.3 copy-done.5
  25.6 0.4 copy-done
  26.0 4.9 %collective-permute-start.12 = (bf16[256,1280]{1,0:T(8,128)(2,1)S(1)}, bf16[256,1280]{1,0:T(8,128)(2,1)S(1)}, u32[]{:S(2)}, u32[]{:S(2)}) collective-permute-start(bf16[256,1280]{1,0:T(8,128)(2,1)S(1)} %pad_maximum_fusion), channel_id=1, source_target_pairs={{0,1},{1,0},{2,3},{3,2},{4,5},{5,4},{6,7},{7,6},{8,9},{9,8},{10,11... | collective-permute-start | bytes 1966088 | tf_op jit(solution)/shard_map/ppermute | solution.py:23
  30.9 0.3 collective-permute-start.9
  31.2 0.2 collective-permute-start.10
  31.5 0.8 %collective-permute-start.13 = (bf16[256,1280]{1,0:T(8,128)(2,1)S(1)}, bf16[256,1280]{1,0:T(8,128)(2,1)S(1)}, u32[]{:S(2)}, u32[]{:S(2)}) collective-permute-start(bf16[256,1280]{1,0:T(8,128)(2,1)S(1)} %pad_maximum_fusion.1), channel_id=1, source_target_pairs={{0,1},{1,0},{2,3},{3,2},{4,5},{5,4},{6,7},{7,6},{8,9},{9,8},{10,11... | collective-permute-start | bytes 1966088 | tf_op jit(solution)/shard_map/ppermute | solution.py:23
  32.3 5.0 %collective-permute-done.9 = bf16[64,1280]{1,0:T(8,128)(2,1)S(1)} collective-permute-done((bf16[64,1280]{1,0:T(8,128)(2,1)S(1)}, bf16[64,1280]{1,0:T(8,128)(2,1)S(1)}, u32[]{:S(2)}, u32[]{:S(2)}) %collective-permute-start.9) | collective-permute-done | bytes 163872 | tf_op jit(solution)/shard_map/ppermute | solution.py:23
  37.2 0.2 collective-permute-start.11
  37.5 0.4 collective-permute-start.14
  37.9 3.8 %collective-permute-done.11 = bf16[64,1280]{1,0:T(8,128)(2,1)S(1)} collective-permute-done((bf16[64,1280]{1,0:T(8,128)(2,1)S(1)}, bf16[64,1280]{1,0:T(8,128)(2,1)S(1)}, u32[]{:S(2)}, u32[]{:S(2)}) %collective-permute-start.11) | collective-permute-done | bytes 163872 | tf_op jit(solution)/shard_map/ppermute | solution.py:23
  41.8 1.5 %collective-permute-start.15 = (bf16[256,1280]{1,0:T(8,128)(2,1)S(1)}, bf16[256,1280]{1,0:T(8,128)(2,1)S(1)}, u32[]{:S(2)}, u32[]{:S(2)}) collective-permute-start(bf16[256,1280]{1,0:T(8,128)(2,1)S(1)} %pad_maximum_fusion.3), channel_id=1, source_target_pairs={{0,1},{1,0},{2,3},{3,2},{4,5},{5,4},{6,7},{7,6},{8,9},{9,8},{10,11... | collective-permute-start | bytes 1966088 | tf_op jit(solution)/shard_map/ppermute | solution.py:23
  43.2 0.8 %pad_maximum_fusion.5.refs_6_ = bf16[128,1280]{1,0:T(8,128)(2,1)} fusion(bf16[64,1280]{1,0:T(8,128)(2,1)S(1)} %collective-permute-done.9, bf16[64,1280]{1,0:T(8,128)(2,1)S(1)} %collective-permute-done.8), kind=kLoop, calls=%fused_computation.5 | loop fusion | flops 655360 | bytes 655360 | tf_op jit(solution)/shard_map/concatenate | solution.py:18
  44.0 0.8 %pad_maximum_fusion.6.refs_7_ = bf16[128,1280]{1,0:T(8,128)(2,1)} fusion(bf16[64,1280]{1,0:T(8,128)(2,1)S(1)} %collective-permute-done.11, bf16[64,1280]{1,0:T(8,128)(2,1)S(1)} %collective-permute-done.10), kind=kLoop, calls=%fused_computation.6 | loop fusion | flops 655360 | bytes 655360 | tf_op jit(solution)/shard_map/concatenate | solution.py:18
  45.0 0.7 copy-done.6
  45.6 0.2 copy-done.7
  45.8 0.2 copy-done.8
  46.1 0.8 %copy-done.9 = bf16[256,1280]{1,0:T(8,128)(2,1)} copy-done((bf16[256,1280]{1,0:T(8,128)(2,1)}, bf16[256,1280]{1,0:T(8,128)(2,1)S(1)}, u32[]{:S(2)}) %copy-start.9) | copy-done | bytes 655384
  46.9 22.1 %shard_map.28 = f32[64,1216]{1,0:T(8,128)} custom-call(bf16[128,1280]{1,0:T(8,128)(2,1)} %copy-done.3, bf16[128,1280]{1,0:T(8,128)(2,1)} %copy-done, bf16[128,1280]{1,0:T(8,128)(2,1)} %copy-done.4, bf16[128,1280]{1,0:T(8,128)(2,1)} %copy-done.1, bf16[128,1280]{1,0:T(8,128)(2,1)} %copy-done.5, bf16[128,1280]{1,0:T(8,128)(2,1)} %copy-done.2, ...), custom_call_target="tpu_custom_call" | custom-call | tf_op jit(solution)/shard_map/pallas_call | solution.py:192
  (37 shorter events, 0.7 us)
Async XLA Ops:
  1.8 5.1 %collective-permute-start.2 = (bf16[64,1280]{1,0:T(8,128)(2,1)S(1)}, bf16[64,1280]{1,0:T(8,128)(2,1)S(1)}, u32[]{:S(2)}, u32[]{:S(2)}) collective-permute-start(bf16[64,1280]{1,0:T(8,128)(2,1)S(1)} %maximum_select_fusion), channel_id=1, source_target_pairs={{0,4},{1,5},{2,6},{3,7},{4,8},{5,9},{6,10},{7,11},{8,12},{9,13},{1... | collective-permute-start | bytes 491528 | tf_op jit(solution)/shard_map/ppermute | solution.py:23
  3.2 6.1 %collective-permute-start = (bf16[64,1280]{1,0:T(8,128)(2,1)S(1)}, bf16[64,1280]{1,0:T(8,128)(2,1)S(1)}, u32[]{:S(2)}, u32[]{:S(2)}) collective-permute-start(bf16[64,1280]{1,0:T(8,128)(2,1)S(1)} %maximum_select_fusion), channel_id=1, source_target_pairs={{0,2},{1,17},{2,0},{3,19},{4,6},{5,21},{6,4},{7,23},{8,10},{9,25},... | collective-permute-start | bytes 491528 | tf_op jit(solution)/shard_map/ppermute | solution.py:23
  6.9 24.0 %collective-permute-start.8 = (bf16[64,1280]{1,0:T(8,128)(2,1)S(1)}, bf16[64,1280]{1,0:T(8,128)(2,1)S(1)}, u32[]{:S(2)}, u32[]{:S(2)}) collective-permute-start(bf16[64,1280]{1,0:T(8,128)(2,1)S(1)} %maximum_select_fusion), channel_id=1, source_target_pairs={{0,8},{1,9},{2,10},{3,11},{4,12},{5,13},{6,14},{7,15},{8,0},{9,1},... | collective-permute-start | bytes 491528 | tf_op jit(solution)/shard_map/ppermute | solution.py:23
  9.2 11.1 %collective-permute-start.5 = (bf16[64,1280]{1,0:T(8,128)(2,1)S(1)}, bf16[64,1280]{1,0:T(8,128)(2,1)S(1)}, u32[]{:S(2)}, u32[]{:S(2)}) collective-permute-start(bf16[64,1280]{1,0:T(8,128)(2,1)S(1)} %maximum_select_fusion), channel_id=1, source_target_pairs={{0,12},{1,13},{2,14},{3,15},{4,0},{5,1},{6,2},{7,3},{8,4},{9,5},{1... | collective-permute-start | bytes 491528 | tf_op jit(solution)/shard_map/ppermute | solution.py:23
  9.4 15.4 %copy-start.3 = (bf16[128,1280]{1,0:T(8,128)(2,1)}, bf16[128,1280]{1,0:T(8,128)(2,1)S(1)}, u32[]{:S(2)}) copy-start(bf16[128,1280]{1,0:T(8,128)(2,1)S(1)} %pad_maximum_fusion.4.refs_0_) | copy-start | bytes 983044
  9.4 15.8 %collective-permute-start.1 = (bf16[128,1280]{1,0:T(8,128)(2,1)S(1)}, bf16[128,1280]{1,0:T(8,128)(2,1)S(1)}, u32[]{:S(2)}, u32[]{:S(2)}) collective-permute-start(bf16[128,1280]{1,0:T(8,128)(2,1)S(1)} %pad_maximum_fusion.4.refs_0_), channel_id=1, source_target_pairs={{0,16},{1,3},{2,18},{3,1},{4,20},{5,7},{6,22},{7,5},{8,24},{9,11},... | collective-permute-start | bytes 983048 | tf_op jit(solution)/shard_map/ppermute | solution.py:23
  9.7 4.5 %collective-permute-start.3 = (bf16[64,1280]{1,0:T(8,128)(2,1)S(1)}, bf16[64,1280]{1,0:T(8,128)(2,1)S(1)}, u32[]{:S(2)}, u32[]{:S(2)}) collective-permute-start(bf16[64,1280]{1,0:T(8,128)(2,1)S(1)} %collective-permute-done.2), channel_id=1, source_target_pairs={{0,2},{1,17},{2,0},{3,19},{4,6},{5,21},{6,4},{7,23},{8,10},{9,25},... | collective-permute-start | bytes 491528 | tf_op jit(solution)/shard_map/ppermute | solution.py:23
  20.4 4.5 %collective-permute-start.6 = (bf16[64,1280]{1,0:T(8,128)(2,1)S(1)}, bf16[64,1280]{1,0:T(8,128)(2,1)S(1)}, u32[]{:S(2)}, u32[]{:S(2)}) collective-permute-start(bf16[64,1280]{1,0:T(8,128)(2,1)S(1)} %collective-permute-done.5), channel_id=1, source_target_pairs={{0,2},{1,17},{2,0},{3,19},{4,6},{5,21},{6,4},{7,23},{8,10},{9,25},... | collective-permute-start | bytes 491528 | tf_op jit(solution)/shard_map/ppermute | solution.py:23
  21.6 3.7 %copy-start.4 = (bf16[128,1280]{1,0:T(8,128)(2,1)}, bf16[128,1280]{1,0:T(8,128)(2,1)S(1)}, u32[]{:S(2)}) copy-start(bf16[128,1280]{1,0:T(8,128)(2,1)S(1)} %constant_dynamic-update-slice_fusion.refs_2_) | copy-start | bytes 983044
  21.6 9.3 %collective-permute-start.4 = (bf16[128,1280]{1,0:T(8,128)(2,1)S(1)}, bf16[128,1280]{1,0:T(8,128)(2,1)S(1)}, u32[]{:S(2)}, u32[]{:S(2)}) collective-permute-start(bf16[128,1280]{1,0:T(8,128)(2,1)S(1)} %constant_dynamic-update-slice_fusion.refs_2_), channel_id=1, source_target_pairs={{0,16},{1,3},{2,18},{3,1},{4,20},{5,7},{6,22},{7,5},{8,24},{9,11},... | collective-permute-start | bytes 983048 | tf_op jit(solution)/shard_map/ppermute | solution.py:23
  24.9 0.7 %copy-start.5 = (bf16[128,1280]{1,0:T(8,128)(2,1)}, bf16[128,1280]{1,0:T(8,128)(2,1)S(1)}, u32[]{:S(2)}) copy-start(bf16[128,1280]{1,0:T(8,128)(2,1)S(1)} %constant_dynamic-update-slice_fusion.2.refs_4_) | copy-start | bytes 983044
  24.9 12.6 %collective-permute-start.7 = (bf16[128,1280]{1,0:T(8,128)(2,1)S(1)}, bf16[128,1280]{1,0:T(8,128)(2,1)S(1)}, u32[]{:S(2)}, u32[]{:S(2)}) collective-permute-start(bf16[128,1280]{1,0:T(8,128)(2,1)S(1)} %constant_dynamic-update-slice_fusion.2.refs_4_), channel_id=1, source_target_pairs={{0,16},{1,3},{2,18},{3,1},{4,20},{5,7},{6,22},{7,5},{8,24},{9,11},... | collective-permute-start | bytes 983048 | tf_op jit(solution)/shard_map/ppermute | solution.py:23
  25.2 0.7 %copy-start = (bf16[128,1280]{1,0:T(8,128)(2,1)}, bf16[128,1280]{1,0:T(8,128)(2,1)S(1)}, u32[]{:S(2)}) copy-start(bf16[128,1280]{1,0:T(8,128)(2,1)S(1)} %collective-permute-done.1.refs_1_) | copy-start | bytes 983044
  26.0 18.8 %collective-permute-start.12 = (bf16[256,1280]{1,0:T(8,128)(2,1)S(1)}, bf16[256,1280]{1,0:T(8,128)(2,1)S(1)}, u32[]{:S(2)}, u32[]{:S(2)}) collective-permute-start(bf16[256,1280]{1,0:T(8,128)(2,1)S(1)} %pad_maximum_fusion), channel_id=1, source_target_pairs={{0,1},{1,0},{2,3},{3,2},{4,5},{5,4},{6,7},{7,6},{8,9},{9,8},{10,11... | collective-permute-start | bytes 1966088 | tf_op jit(solution)/shard_map/ppermute | solution.py:23
  30.9 6.6 %copy-start.1 = (bf16[128,1280]{1,0:T(8,128)(2,1)}, bf16[128,1280]{1,0:T(8,128)(2,1)S(1)}, u32[]{:S(2)}) copy-start(bf16[128,1280]{1,0:T(8,128)(2,1)S(1)} %collective-permute-done.4.refs_3_) | copy-start | bytes 983044
  30.9 6.3 %collective-permute-start.9 = (bf16[64,1280]{1,0:T(8,128)(2,1)S(1)}, bf16[64,1280]{1,0:T(8,128)(2,1)S(1)}, u32[]{:S(2)}, u32[]{:S(2)}) collective-permute-start(bf16[64,1280]{1,0:T(8,128)(2,1)S(1)} %collective-permute-done.8), channel_id=1, source_target_pairs={{0,2},{1,17},{2,0},{3,19},{4,6},{5,21},{6,4},{7,23},{8,10},{9,25},... | collective-permute-start | bytes 491528 | tf_op jit(solution)/shard_map/ppermute | solution.py:23
  31.2 6.8 %collective-permute-start.10 = (bf16[64,1280]{1,0:T(8,128)(2,1)S(1)}, bf16[64,1280]{1,0:T(8,128)(2,1)S(1)}, u32[]{:S(2)}, u32[]{:S(2)}) collective-permute-start(bf16[64,1280]{1,0:T(8,128)(2,1)S(1)} %collective-permute-done.8), channel_id=1, source_target_pairs={{0,16},{1,3},{2,18},{3,1},{4,20},{5,7},{6,22},{7,5},{8,24},{9,11},... | collective-permute-start | bytes 491528 | tf_op jit(solution)/shard_map/ppermute | solution.py:23
  31.5 13.3 %collective-permute-start.13 = (bf16[256,1280]{1,0:T(8,128)(2,1)S(1)}, bf16[256,1280]{1,0:T(8,128)(2,1)S(1)}, u32[]{:S(2)}, u32[]{:S(2)}) collective-permute-start(bf16[256,1280]{1,0:T(8,128)(2,1)S(1)} %pad_maximum_fusion.1), channel_id=1, source_target_pairs={{0,1},{1,0},{2,3},{3,2},{4,5},{5,4},{6,7},{7,6},{8,9},{9,8},{10,11... | collective-permute-start | bytes 1966088 | tf_op jit(solution)/shard_map/ppermute | solution.py:23
  37.2 4.5 %collective-permute-start.11 = (bf16[64,1280]{1,0:T(8,128)(2,1)S(1)}, bf16[64,1280]{1,0:T(8,128)(2,1)S(1)}, u32[]{:S(2)}, u32[]{:S(2)}) collective-permute-start(bf16[64,1280]{1,0:T(8,128)(2,1)S(1)} %collective-permute-done.9), channel_id=1, source_target_pairs={{0,16},{1,3},{2,18},{3,1},{4,20},{5,7},{6,22},{7,5},{8,24},{9,11},... | collective-permute-start | bytes 491528 | tf_op jit(solution)/shard_map/ppermute | solution.py:23
  37.5 4.3 %copy-start.2 = (bf16[128,1280]{1,0:T(8,128)(2,1)}, bf16[128,1280]{1,0:T(8,128)(2,1)S(1)}, u32[]{:S(2)}) copy-start(bf16[128,1280]{1,0:T(8,128)(2,1)S(1)} %collective-permute-done.7.refs_5_) | copy-start | bytes 983044
  37.5 7.3 %collective-permute-start.14 = (bf16[256,1280]{1,0:T(8,128)(2,1)S(1)}, bf16[256,1280]{1,0:T(8,128)(2,1)S(1)}, u32[]{:S(2)}, u32[]{:S(2)}) collective-permute-start(bf16[256,1280]{1,0:T(8,128)(2,1)S(1)} %pad_maximum_fusion.2), channel_id=1, source_target_pairs={{0,1},{1,0},{2,3},{3,2},{4,5},{5,4},{6,7},{7,6},{8,9},{9,8},{10,11... | collective-permute-start | bytes 1966088 | tf_op jit(solution)/shard_map/ppermute | solution.py:23
  41.8 3.2 %collective-permute-start.15 = (bf16[256,1280]{1,0:T(8,128)(2,1)S(1)}, bf16[256,1280]{1,0:T(8,128)(2,1)S(1)}, u32[]{:S(2)}, u32[]{:S(2)}) collective-permute-start(bf16[256,1280]{1,0:T(8,128)(2,1)S(1)} %pad_maximum_fusion.3), channel_id=1, source_target_pairs={{0,1},{1,0},{2,3},{3,2},{4,5},{5,4},{6,7},{7,6},{8,9},{9,8},{10,11... | collective-permute-start | bytes 1966088 | tf_op jit(solution)/shard_map/ppermute | solution.py:23
  44.8 0.9 %copy-start.6 = (bf16[256,1280]{1,0:T(8,128)(2,1)}, bf16[256,1280]{1,0:T(8,128)(2,1)S(1)}, u32[]{:S(2)}) copy-start(bf16[256,1280]{1,0:T(8,128)(2,1)S(1)} %collective-permute-done.12.refs_8_) | copy-start | bytes 1966084
  44.8 1.1 %copy-start.7 = (bf16[256,1280]{1,0:T(8,128)(2,1)}, bf16[256,1280]{1,0:T(8,128)(2,1)S(1)}, u32[]{:S(2)}) copy-start(bf16[256,1280]{1,0:T(8,128)(2,1)S(1)} %collective-permute-done.13.refs_9_) | copy-start | bytes 1966084
  44.8 1.3 %copy-start.8 = (bf16[256,1280]{1,0:T(8,128)(2,1)}, bf16[256,1280]{1,0:T(8,128)(2,1)S(1)}, u32[]{:S(2)}) copy-start(bf16[256,1280]{1,0:T(8,128)(2,1)S(1)} %collective-permute-done.14.refs_10_) | copy-start | bytes 1966084
  46.1 0.8 %copy-start.9 = (bf16[256,1280]{1,0:T(8,128)(2,1)}, bf16[256,1280]{1,0:T(8,128)(2,1)S(1)}, u32[]{:S(2)}) copy-start(bf16[256,1280]{1,0:T(8,128)(2,1)S(1)} %collective-permute-done.15.refs_11_) | copy-start | bytes 1966084

commit v2 on v1

v2 whole, which is shorter than its diff:
```python
import jax
import jax.numpy as jnp
from jax import lax
from jax.experimental import pallas as pl
from jax.experimental.pallas import tpu as pltpu
from jax.sharding import PartitionSpec as P

AXES = ("row", "col")
GROUP = 32
Z_ORDER = (0, 1, 3, 2)


def after(value, *earlier):
    return lax.optimization_barrier((value,) + earlier)[0]


def join(*parts):
    return jnp.concatenate(parts, axis=0)


def send(value, count, target):
    pairs = [(source, target(source)) for source in range(count)]
    return lax.ppermute(value, AXES, [(s, t) for s, t in pairs if 0 <= t < count])


def along_z(value, count, step):
    return send(value, count, lambda d: (d & ~12) | (((d >> 2) + step) % 4 << 2))


def first_flip(parity):
    return 2 + 14 * parity


def flip_first(value, count):
    return send(value, count, lambda d: d ^ first_flip(d & 1))


def flip_second(value, count):
    return send(value, count, lambda d: d ^ (18 - first_flip(d & 1)))


def flip_core(value, count):
    return send(value, count, lambda d: d ^ 1)


def gather(row, count):
    near = along_z(row, count, 1)
    first = flip_first(row, count)
    next_near = along_z(after(row, first), count, 3)
    far = along_z(after(row, near), count, 2)
    pieces = [row, first, flip_second(join(row, first), count)]
    first = flip_first(near, count)
    pieces += [near, first, flip_second(join(near, first), count)]
    first = flip_first(next_near, count)
    pieces += [next_near, first, flip_second(join(next_near, first), count)]
    first = flip_first(far, count)
    pieces += [far, first, flip_second(far, count), flip_second(first, count)]
    return pieces + [flip_core(piece, count) for piece in pieces]


def dot(left, right, on=0):
    return lax.dot_general(left, right, (((1,), (on,)), ((), ())), preferred_element_type=jnp.float32)


def purify_kernel(block, half, copies, *refs):
    count = len(refs) - 7
    pieces, out_ref = refs[:count], refs[count]
    band_ref, next_ref, flag_ref, mask_ref, square_ref, low_ref = refs[count + 1 :]
    slots = 2 * half + 1
    width = (slots + 1) * block
    reach = 4 * half + 2
    window = (2 * half + 4) * block
    panel = 4 * block
    bits = jnp.bfloat16
    place = lax.axis_index("row") * lax.axis_size("col") + lax.axis_index("col")
    local, start = place % GROUP, place // GROUP * GROUP
    parity = local % 2
    origin = place - parity - 2 * half

    left = 10 * block
    band_ref[:, left : left + reach * block] = jnp.zeros((reach * block, reach * block), bits)
    flag_ref[...] = jnp.zeros_like(flag_ref)
    next_ref[...] = jnp.zeros_like(next_ref)
    lanes = lax.broadcasted_iota(jnp.int32, (block, 128), 1)

    def put(piece, index, odd):
        offset = index - origin

        @pl.when((offset >= 0) & (offset < reach))
        def _():
            rows = pl.ds(pl.multiple_of(offset * block, block), block)
            column = pl.multiple_of((offset + 1) // 2 * 128, 128)
            low = (1 - odd) * block
            head = piece[:, :128].astype(jnp.float32)
            tail = piece[:, width - 128 :].astype(jnp.float32)
            head_kept = lanes >= low
            tail_kept = lanes < low + block
            band_ref[rows, pl.ds(column, 128)] = jnp.where(head_kept, head, 0.0).astype(bits)
            band_ref[rows, pl.ds(column + 128, width - 256)] = piece[:, 128 : width - 128]
            band_ref[rows, pl.ds(column + width - 128, 128)] = jnp.where(tail_kept, tail, 0.0).astype(bits)
            flags = jnp.where(head_kept, 0.0, head) + jnp.where(tail_kept, 0.0, tail)
            flag_ref[pl.ds(offset, 1), :] = flags[:1]

    each = count // copies
    for copy in range(copies):
        shift = start + (0, -GROUP, GROUP)[copy]
        held = [
            piece.at[pl.ds(at, block), :]
            for piece in pieces[each * copy : each * copy + each]
            for at in range(0, piece.shape[0], block)
        ]
        for core in range(2):
            odd = parity if core == 0 else 1 - parity
            flip = first_flip(odd)
            for k, step in enumerate(Z_ORDER):
                base = (local & ~13) | ((((local >> 2) & 3) + 4 - step) % 4 << 2) | odd
                for number, turned in enumerate((base, base ^ flip, base ^ (18 - flip), base ^ 18)):
                    put(held[16 * core + 4 * k + number], shift + turned, odd)

    shape = (128, mask_ref.shape[1])
    lane = lax.broadcasted_iota(jnp.int32, shape, 0)
    slot = lane % block
    spread = (lax.broadcasted_iota(jnp.int32, shape, 1) // block == slot + lane // block + 4) & (slot < slots)
    mask_ref[...] = dot(flag_ref[...].astype(bits), spread.astype(bits))

    chunks = ((0, 2 * panel, 0, 5 * panel), (2 * panel, 2 * panel, 0, window), (4 * panel, window - 4 * panel, panel, window))

    def group(m, carry):
        at = pl.multiple_of(m * panel, panel)

        def kept(n, size):
            rows = []
            for w in range(n // block, (n + size) // block):
                column = (22 + w % 2 - w) * block
                row = mask_ref[pl.ds(4 * m + w, 1), column : column + panel]
                rows.append(jnp.broadcast_to(row, (block, panel)))
            return jnp.concatenate(rows, axis=0)

        def rows(first, size, low, high):
            return band_ref[pl.ds(at + first, size), pl.ds(pl.multiple_of(left + at + low, 128), high - low)]

        for n, size, low, high in chunks:
            square = kept(n, size) * dot(rows(n, size, low, high), rows(half * block, panel, low, high), 1)
            square_ref[n : n + size, :] = square
            low_ref[n : n + size, :] = square.astype(bits)
        for n, size, low, high in chunks:
            cube = dot(rows(n, size, low, high), low_ref[low:high, :])
            current = kept(n, size) * (3.0 * square_ref[n : n + size, :] - 2.0 * cube)
            next_ref[pl.ds(at + n, size), pl.ds(pl.multiple_of(at + 2 * block, 128), panel)] = current.astype(bits)
        return carry

    lax.fori_loop(0, 5, group, 0)

    inner = slice(half * block, (half + 20) * block)
    chosen = lax.broadcasted_iota(jnp.int32, (block, panel), 1)
    chosen = chosen == lax.broadcasted_iota(jnp.int32, (block, panel), 0) + (1 + parity) * block
    mine = dot(chosen.astype(bits), next_ref[inner, 10 * block : 14 * block], 1).astype(bits)
    kept = mask_ref[pl.ds(2 * half + parity, 1), 2 * block : 2 * block + window]
    square = kept * dot(mine, next_ref[inner, :])
    cube = dot(square.astype(bits)[:, 2 * block :], next_ref[inner, :])
    current = kept * (3.0 * square - 2.0 * cube)
    out_ref[...] = jnp.where(
        parity == 0,
        current[:, 2 * block : (slots + 2) * block],
        current[:, 3 * block : (slots + 3) * block],
    )


def local(density, pattern):
    block, width = density.shape
    slots = pattern.shape[1]
    half = (slots - 1) // 2
    count = lax.axis_size("row") * lax.axis_size("col")
    place = lax.axis_index("row") * lax.axis_size("col") + lax.axis_index("col")
    flags = jnp.broadcast_to(pattern.astype(jnp.bfloat16), (block, slots))
    flags = jnp.pad(flags, ((0, 0), (0, block - slots)))
    low = density.astype(jnp.bfloat16)
    row = jnp.where(
        place % 2 == 0,
        jnp.concatenate([flags, low], axis=1),
        jnp.concatenate([low, flags], axis=1),
    )
    pieces = gather(row, count)
    copies = 1
    if count > GROUP:
        pieces = (
            pieces
            + [send(piece, count, lambda d: d + GROUP) for piece in pieces]
            + [send(piece, count, lambda d: d - GROUP) for piece in pieces]
        )
        copies = 3

    def kernel(*refs):
        purify_kernel(block, half, copies, *refs)

    window = (2 * half + 4) * block
    reach = (4 * half + 2) * block
    return pl.pallas_call(
        kernel,
        out_shape=jax.ShapeDtypeStruct((block, width), jnp.float32),
        in_specs=[pl.BlockSpec(memory_space=pltpu.VMEM)] * len(pieces),
        out_specs=pl.BlockSpec(memory_space=pltpu.VMEM),
        scratch_shapes=[
            pltpu.VMEM((reach, (6 * half + 4) * block), jnp.bfloat16),
            pltpu.VMEM((reach, window), jnp.bfloat16),
            pltpu.VMEM((40, 128), jnp.float32),
            pltpu.VMEM((40, 26 * block), jnp.float32),
            pltpu.VMEM((window, 4 * block), jnp.float32),
            pltpu.VMEM((window, 4 * block), jnp.bfloat16),
        ],
        compiler_params=pltpu.CompilerParams(vmem_limit_bytes=36 * 2**20),
    )(*pieces)


def solution(mesh):
    placed = (P(AXES, None), P(AXES, None))
    return jax.shard_map(local, mesh=mesh, in_specs=placed, out_specs=P(AXES, None), check_vma=False)
```

time: 69.2 us -> 59.3 us (0.86)
  the two profiles are of different devices: /device:TPU:13 before, /device:TPU:11 now
where the time goes in v2:
time: 59.3 us; the launch traced here: 59.2 us
  starting transfers between devices  25.9 us (44%)
  waiting for transfers between devices  15.8 us (27%)
  Pallas kernels  15.6 us (26%)
  other arithmetic  1.18 us (2%)
  local copies, waits for them, and re-layouts  0.67 us (1%)
    ppermute x25, starting transfers between devices, send(): lax.ppermute(value, AXES, [(s, t) for s, t in pairs if 0 <= t < count])  25.9 us
    ppermute x25, waiting for transfers between devices, send(): lax.ppermute(value, AXES, [(s, t) for s, t in pairs if 0 <= t < count])  15.8 us
    pallas_call x1, Pallas kernels, local(): pl.pallas_call(kernel, out_shape=jax.ShapeDtypeStruct((block, width), jnp...  15.6 us
  transfers between devices with their start and end apart: 25, of which 8 were waited for; matrix products, arithmetic and copies ran while one was open for 0% of the time, Pallas kernels for 0%

profile of v2, /device:TPU:11, one launch (start us, length us, event | category | flops | bytes accessed | tf_op | source)
XLA Modules:
  0.0 59.2 jit_solution(12384205557116268628)
XLA Ops:
  0.0 0.7 %copy-done = s32[1,19]{1,0:T(1,128)S(1)} copy-done((s32[1,19]{1,0:T(1,128)S(1)}, s32[1,19]{1,0:T(1,128)}, u32[]{:S(2)}) %copy-start) | copy-done | bytes 100
  0.7 1.0 %convert_element_type.9 = bf16[64,1216]{1,0:T(8,128)(2,1)S(1)} convert(f32[64,1216]{1,0:T(8,128)} %param.2) | non-fusion elementwise | flops 77824 | bytes 466944 | tf_op jit(solution)/shard_map/convert_element_type | solution.py:177
  1.8 1.3 %collective-permute-start.2 = (bf16[64,1280]{1,0:T(8,128)(2,1)S(1)}, bf16[64,1280]{1,0:T(8,128)(2,1)S(1)}, u32[]{:S(2)}, u32[]{:S(2)}) collective-permute-start(bf16[64,1280]{1,0:T(8,128)(2,1)S(1)} %maximum_select_fusion.refs_0_), channel_id=1, source_target_pairs={{0,4},{1,5},{2,6},{3,7},{4,8},{5,9},{6,10},{7,11},{8,12},{9,13},{1... | collective-permute-start | bytes 491528 | tf_op jit(solution)/shard_map/ppermute | solution.py:23
  3.2 0.3 collective-permute-start
  3.4 2.2 %collective-permute-start.12 = (bf16[64,1280]{1,0:T(8,128)(2,1)S(1)}, bf16[64,1280]{1,0:T(8,128)(2,1)S(1)}, u32[]{:S(2)}, u32[]{:S(2)}) collective-permute-start(bf16[64,1280]{1,0:T(8,128)(2,1)S(1)} %maximum_select_fusion.refs_0_), channel_id=1, source_target_pairs={{0,1},{1,0},{2,3},{3,2},{4,5},{5,4},{6,7},{7,6},{8,9},{9,8},{10,11... | collective-permute-start | bytes 491528 | tf_op jit(solution)/shard_map/ppermute | solution.py:23
  5.6 1.3 %collective-permute-done.2.refs_3_ = bf16[64,1280]{1,0:T(8,128)(2,1)S(1)} collective-permute-done((bf16[64,1280]{1,0:T(8,128)(2,1)S(1)}, bf16[64,1280]{1,0:T(8,128)(2,1)S(1)}, u32[]{:S(2)}, u32[]{:S(2)}) %collective-permute-start.2) | collective-permute-done | bytes 163872 | tf_op jit(solution)/shard_map/ppermute | solution.py:23
  6.9 2.3 %collective-permute-start.8 = (bf16[64,1280]{1,0:T(8,128)(2,1)S(1)}, bf16[64,1280]{1,0:T(8,128)(2,1)S(1)}, u32[]{:S(2)}, u32[]{:S(2)}) collective-permute-start(bf16[64,1280]{1,0:T(8,128)(2,1)S(1)} %maximum_select_fusion.refs_0_), channel_id=1, source_target_pairs={{0,8},{1,9},{2,10},{3,11},{4,12},{5,13},{6,14},{7,15},{8,0},{9,1},... | collective-permute-start | bytes 491528 | tf_op jit(solution)/shard_map/ppermute | solution.py:23
  9.4 2.1 %collective-permute-start.15 = (bf16[64,1280]{1,0:T(8,128)(2,1)S(1)}, bf16[64,1280]{1,0:T(8,128)(2,1)S(1)}, u32[]{:S(2)}, u32[]{:S(2)}) collective-permute-start(bf16[64,1280]{1,0:T(8,128)(2,1)S(1)} %collective-permute-done.2.refs_3_), channel_id=1, source_target_pairs={{0,1},{1,0},{2,3},{3,2},{4,5},{5,4},{6,7},{7,6},{8,9},{9,8},{10,11... | collective-permute-start | bytes 491528 | tf_op jit(solution)/shard_map/ppermute | solution.py:23
  11.5 0.3 collective-permute-start.3
  11.8 4.2 %collective-permute-done.3.refs_4_ = bf16[64,1280]{1,0:T(8,128)(2,1)S(1)} collective-permute-done((bf16[64,1280]{1,0:T(8,128)(2,1)S(1)}, bf16[64,1280]{1,0:T(8,128)(2,1)S(1)}, u32[]{:S(2)}, u32[]{:S(2)}) %collective-permute-start.3) | collective-permute-done | bytes 163872 | tf_op jit(solution)/shard_map/ppermute | solution.py:23
  16.0 0.9 %collective-permute-start.13 = (bf16[64,1280]{1,0:T(8,128)(2,1)S(1)}, bf16[64,1280]{1,0:T(8,128)(2,1)S(1)}, u32[]{:S(2)}, u32[]{:S(2)}) collective-permute-start(bf16[64,1280]{1,0:T(8,128)(2,1)S(1)} %collective-permute-done.refs_1_), channel_id=1, source_target_pairs={{0,1},{1,0},{2,3},{3,2},{4,5},{5,4},{6,7},{7,6},{8,9},{9,8},{10,11... | collective-permute-start | bytes 491528 | tf_op jit(solution)/shard_map/ppermute | solution.py:23
  16.8 3.5 %collective-permute-done.5.refs_6_ = bf16[64,1280]{1,0:T(8,128)(2,1)S(1)} collective-permute-done((bf16[64,1280]{1,0:T(8,128)(2,1)S(1)}, bf16[64,1280]{1,0:T(8,128)(2,1)S(1)}, u32[]{:S(2)}, u32[]{:S(2)}) %collective-permute-start.5) | collective-permute-done | bytes 163872 | tf_op jit(solution)/shard_map/ppermute | solution.py:23
  20.4 0.3 collective-permute-start.6
  20.7 1.2 %collective-permute-start.1 = (bf16[128,1280]{1,0:T(8,128)(2,1)S(1)}, bf16[128,1280]{1,0:T(8,128)(2,1)S(1)}, u32[]{:S(2)}, u32[]{:S(2)}) collective-permute-start(bf16[128,1280]{1,0:T(8,128)(2,1)S(1)} %pad_maximum_fusion), channel_id=1, source_target_pairs={{0,16},{1,3},{2,18},{3,1},{4,20},{5,7},{6,22},{7,5},{8,24},{9,11},... | collective-permute-start | bytes 983048 | tf_op jit(solution)/shard_map/ppermute | solution.py:23
  22.0 1.6 %collective-permute-start.21 = (bf16[64,1280]{1,0:T(8,128)(2,1)S(1)}, bf16[64,1280]{1,0:T(8,128)(2,1)S(1)}, u32[]{:S(2)}, u32[]{:S(2)}) collective-permute-start(bf16[64,1280]{1,0:T(8,128)(2,1)S(1)} %collective-permute-done.8.refs_9_), channel_id=1, source_target_pairs={{0,1},{1,0},{2,3},{3,2},{4,5},{5,4},{6,7},{7,6},{8,9},{9,8},{10,11... | collective-permute-start | bytes 491528 | tf_op jit(solution)/shard_map/ppermute | solution.py:23
  23.6 0.2 collective-permute-start.10
  23.9 1.2 %collective-permute-start.9 = (bf16[64,1280]{1,0:T(8,128)(2,1)S(1)}, bf16[64,1280]{1,0:T(8,128)(2,1)S(1)}, u32[]{:S(2)}, u32[]{:S(2)}) collective-permute-start(bf16[64,1280]{1,0:T(8,128)(2,1)S(1)} %collective-permute-done.8.refs_9_), channel_id=1, source_target_pairs={{0,2},{1,17},{2,0},{3,19},{4,6},{5,21},{6,4},{7,23},{8,10},{9,25},... | collective-permute-start | bytes 491528 | tf_op jit(solution)/shard_map/ppermute | solution.py:23
  25.1 3.5 %collective-permute-start.16 = (bf16[64,1280]{1,0:T(8,128)(2,1)S(1)}, bf16[64,1280]{1,0:T(8,128)(2,1)S(1)}, u32[]{:S(2)}, u32[]{:S(2)}) collective-permute-start(bf16[64,1280]{1,0:T(8,128)(2,1)S(1)} %collective-permute-done.3.refs_4_), channel_id=1, source_target_pairs={{0,1},{1,0},{2,3},{3,2},{4,5},{5,4},{6,7},{7,6},{8,9},{9,8},{10,11... | collective-permute-start | bytes 491528 | tf_op jit(solution)/shard_map/ppermute | solution.py:23
  28.6 1.3 %collective-permute-start.4 = (bf16[128,1280]{1,0:T(8,128)(2,1)S(1)}, bf16[128,1280]{1,0:T(8,128)(2,1)S(1)}, u32[]{:S(2)}, u32[]{:S(2)}) collective-permute-start(bf16[128,1280]{1,0:T(8,128)(2,1)S(1)} %pad_maximum_fusion.1), channel_id=1, source_target_pairs={{0,16},{1,3},{2,18},{3,1},{4,20},{5,7},{6,22},{7,5},{8,24},{9,11},... | collective-permute-start | bytes 983048 | tf_op jit(solution)/shard_map/ppermute | solution.py:23
  29.9 2.4 %collective-permute-done.10.refs_11_ = bf16[64,1280]{1,0:T(8,128)(2,1)S(1)} collective-permute-done((bf16[64,1280]{1,0:T(8,128)(2,1)S(1)}, bf16[64,1280]{1,0:T(8,128)(2,1)S(1)}, u32[]{:S(2)}, u32[]{:S(2)}) %collective-permute-start.10) | collective-permute-done | bytes 163872 | tf_op jit(solution)/shard_map/ppermute | solution.py:23
  32.3 1.2 %collective-permute-start.7 = (bf16[128,1280]{1,0:T(8,128)(2,1)S(1)}, bf16[128,1280]{1,0:T(8,128)(2,1)S(1)}, u32[]{:S(2)}, u32[]{:S(2)}) collective-permute-start(bf16[128,1280]{1,0:T(8,128)(2,1)S(1)} %pad_maximum_fusion.2), channel_id=1, source_target_pairs={{0,16},{1,3},{2,18},{3,1},{4,20},{5,7},{6,22},{7,5},{8,24},{9,11},... | collective-permute-start | bytes 983048 | tf_op jit(solution)/shard_map/ppermute | solution.py:23
  33.5 0.7 %collective-permute-start.18 = (bf16[64,1280]{1,0:T(8,128)(2,1)S(1)}, bf16[64,1280]{1,0:T(8,128)(2,1)S(1)}, u32[]{:S(2)}, u32[]{:S(2)}) collective-permute-start(bf16[64,1280]{1,0:T(8,128)(2,1)S(1)} %collective-permute-done.5.refs_6_), channel_id=1, source_target_pairs={{0,1},{1,0},{2,3},{3,2},{4,5},{5,4},{6,7},{7,6},{8,9},{9,8},{10,11... | collective-permute-start | bytes 491528 | tf_op jit(solution)/shard_map/ppermute | solution.py:23
  34.3 1.0 %collective-permute-done.18.refs_19_ = bf16[64,1280]{1,0:T(8,128)(2,1)S(1)} collective-permute-done((bf16[64,1280]{1,0:T(8,128)(2,1)S(1)}, bf16[64,1280]{1,0:T(8,128)(2,1)S(1)}, u32[]{:S(2)}, u32[]{:S(2)}) %collective-permute-start.18) | collective-permute-done | bytes 163872 | tf_op jit(solution)/shard_map/ppermute | solution.py:23
  35.2 0.4 collective-permute-start.22
  35.6 0.2 collective-permute-start.11
  35.8 1.4 %collective-permute-start.14 = (bf16[128,1280]{1,0:T(8,128)(2,1)S(1)}, bf16[128,1280]{1,0:T(8,128)(2,1)S(1)}, u32[]{:S(2)}, u32[]{:S(2)}) collective-permute-start(bf16[128,1280]{1,0:T(8,128)(2,1)S(1)} %collective-permute-done.1.refs_2_), channel_id=1, source_target_pairs={{0,1},{1,0},{2,3},{3,2},{4,5},{5,4},{6,7},{7,6},{8,9},{9,8},{10,11... | collective-permute-start | bytes 983048 | tf_op jit(solution)/shard_map/ppermute | solution.py:23
  37.3 2.0 %collective-permute-done.7.refs_8_ = bf16[128,1280]{1,0:T(8,128)(2,1)S(1)} collective-permute-done((bf16[128,1280]{1,0:T(8,128)(2,1)S(1)}, bf16[128,1280]{1,0:T(8,128)(2,1)S(1)}, u32[]{:S(2)}, u32[]{:S(2)}) %collective-permute-start.7) | collective-permute-done | bytes 327712 | tf_op jit(solution)/shard_map/ppermute | solution.py:23
  39.3 1.4 %collective-permute-start.20 = (bf16[128,1280]{1,0:T(8,128)(2,1)S(1)}, bf16[128,1280]{1,0:T(8,128)(2,1)S(1)}, u32[]{:S(2)}, u32[]{:S(2)}) collective-permute-start(bf16[128,1280]{1,0:T(8,128)(2,1)S(1)} %collective-permute-done.7.refs_8_), channel_id=1, source_target_pairs={{0,1},{1,0},{2,3},{3,2},{4,5},{5,4},{6,7},{7,6},{8,9},{9,8},{10,11... | collective-permute-start | bytes 983048 | tf_op jit(solution)/shard_map/ppermute | solution.py:23
  40.8 0.3 collective-permute-done.11.refs_12_
  41.1 1.4 %collective-permute-start.24 = (bf16[64,1280]{1,0:T(8,128)(2,1)S(1)}, bf16[64,1280]{1,0:T(8,128)(2,1)S(1)}, u32[]{:S(2)}, u32[]{:S(2)}) collective-permute-start(bf16[64,1280]{1,0:T(8,128)(2,1)S(1)} %collective-permute-done.11.refs_12_), channel_id=1, source_target_pairs={{0,1},{1,0},{2,3},{3,2},{4,5},{5,4},{6,7},{7,6},{8,9},{9,8},{10,11... | collective-permute-start | bytes 491528 | tf_op jit(solution)/shard_map/ppermute | solution.py:23
  42.5 1.0 %collective-permute-done.24.refs_25_ = bf16[64,1280]{1,0:T(8,128)(2,1)S(1)} collective-permute-done((bf16[64,1280]{1,0:T(8,128)(2,1)S(1)}, bf16[64,1280]{1,0:T(8,128)(2,1)S(1)}, u32[]{:S(2)}, u32[]{:S(2)}) %collective-permute-start.24) | collective-permute-done | bytes 163872 | tf_op jit(solution)/shard_map/ppermute | solution.py:23
  43.5 15.6 %shard_map.28 = f32[64,1216]{1,0:T(8,128)} custom-call(bf16[64,1280]{1,0:T(8,128)(2,1)S(1)} %maximum_select_fusion.refs_0_, bf16[64,1280]{1,0:T(8,128)(2,1)S(1)} %collective-permute-done.refs_1_, bf16[128,1280]{1,0:T(8,128)(2,1)S(1)} %collective-permute-done.1.refs_2_, bf16[64,1280]{1,0:T(8,128)(2,1)S(1)} %collective-permute-done.2.refs_3_, ...), custom_call_target="tpu_custom_call" | custom-call | tf_op jit(solution)/shard_map/pallas_call | solution.py:198
  (29 shorter events, 0.6 us)
Async XLA Ops:
  0.0 0.7 %copy-start = (s32[1,19]{1,0:T(1,128)S(1)}, s32[1,19]{1,0:T(1,128)}, u32[]{:S(2)}) copy-start(s32[1,19]{1,0:T(1,128)} %param.3) | copy-start | bytes 232
  1.8 5.1 %collective-permute-start.2 = (bf16[64,1280]{1,0:T(8,128)(2,1)S(1)}, bf16[64,1280]{1,0:T(8,128)(2,1)S(1)}, u32[]{:S(2)}, u32[]{:S(2)}) collective-permute-start(bf16[64,1280]{1,0:T(8,128)(2,1)S(1)} %maximum_select_fusion.refs_0_), channel_id=1, source_target_pairs={{0,4},{1,5},{2,6},{3,7},{4,8},{5,9},{6,10},{7,11},{8,12},{9,13},{1... | collective-permute-start | bytes 491528 | tf_op jit(solution)/shard_map/ppermute | solution.py:23
  3.2 6.1 %collective-permute-start = (bf16[64,1280]{1,0:T(8,128)(2,1)S(1)}, bf16[64,1280]{1,0:T(8,128)(2,1)S(1)}, u32[]{:S(2)}, u32[]{:S(2)}) collective-permute-start(bf16[64,1280]{1,0:T(8,128)(2,1)S(1)} %maximum_select_fusion.refs_0_), channel_id=1, source_target_pairs={{0,2},{1,17},{2,0},{3,19},{4,6},{5,21},{6,4},{7,23},{8,10},{9,25},... | collective-permute-start | bytes 491528 | tf_op jit(solution)/shard_map/ppermute | solution.py:23
  3.4 17.3 %collective-permute-start.12 = (bf16[64,1280]{1,0:T(8,128)(2,1)S(1)}, bf16[64,1280]{1,0:T(8,128)(2,1)S(1)}, u32[]{:S(2)}, u32[]{:S(2)}) collective-permute-start(bf16[64,1280]{1,0:T(8,128)(2,1)S(1)} %maximum_select_fusion.refs_0_), channel_id=1, source_target_pairs={{0,1},{1,0},{2,3},{3,2},{4,5},{5,4},{6,7},{7,6},{8,9},{9,8},{10,11... | collective-permute-start | bytes 491528 | tf_op jit(solution)/shard_map/ppermute | solution.py:23
  6.9 15.0 %collective-permute-start.8 = (bf16[64,1280]{1,0:T(8,128)(2,1)S(1)}, bf16[64,1280]{1,0:T(8,128)(2,1)S(1)}, u32[]{:S(2)}, u32[]{:S(2)}) collective-permute-start(bf16[64,1280]{1,0:T(8,128)(2,1)S(1)} %maximum_select_fusion.refs_0_), channel_id=1, source_target_pairs={{0,8},{1,9},{2,10},{3,11},{4,12},{5,13},{6,14},{7,15},{8,0},{9,1},... | collective-permute-start | bytes 491528 | tf_op jit(solution)/shard_map/ppermute | solution.py:23
  9.2 11.1 %collective-permute-start.5 = (bf16[64,1280]{1,0:T(8,128)(2,1)S(1)}, bf16[64,1280]{1,0:T(8,128)(2,1)S(1)}, u32[]{:S(2)}, u32[]{:S(2)}) collective-permute-start(bf16[64,1280]{1,0:T(8,128)(2,1)S(1)} %maximum_select_fusion.refs_0_), channel_id=1, source_target_pairs={{0,12},{1,13},{2,14},{3,15},{4,0},{5,1},{6,2},{7,3},{8,4},{9,5},{1... | collective-permute-start | bytes 491528 | tf_op jit(solution)/shard_map/ppermute | solution.py:23
  9.4 14.2 %collective-permute-start.15 = (bf16[64,1280]{1,0:T(8,128)(2,1)S(1)}, bf16[64,1280]{1,0:T(8,128)(2,1)S(1)}, u32[]{:S(2)}, u32[]{:S(2)}) collective-permute-start(bf16[64,1280]{1,0:T(8,128)(2,1)S(1)} %collective-permute-done.2.refs_3_), channel_id=1, source_target_pairs={{0,1},{1,0},{2,3},{3,2},{4,5},{5,4},{6,7},{7,6},{8,9},{9,8},{10,11... | collective-permute-start | bytes 491528 | tf_op jit(solution)/shard_map/ppermute | solution.py:23
  11.5 4.5 %collective-permute-start.3 = (bf16[64,1280]{1,0:T(8,128)(2,1)S(1)}, bf16[64,1280]{1,0:T(8,128)(2,1)S(1)}, u32[]{:S(2)}, u32[]{:S(2)}) collective-permute-start(bf16[64,1280]{1,0:T(8,128)(2,1)S(1)} %collective-permute-done.2.refs_3_), channel_id=1, source_target_pairs={{0,2},{1,17},{2,0},{3,19},{4,6},{5,21},{6,4},{7,23},{8,10},{9,25},... | collective-permute-start | bytes 491528 | tf_op jit(solution)/shard_map/ppermute | solution.py:23
  16.0 7.9 %collective-permute-start.13 = (bf16[64,1280]{1,0:T(8,128)(2,1)S(1)}, bf16[64,1280]{1,0:T(8,128)(2,1)S(1)}, u32[]{:S(2)}, u32[]{:S(2)}) collective-permute-start(bf16[64,1280]{1,0:T(8,128)(2,1)S(1)} %collective-permute-done.refs_1_), channel_id=1, source_target_pairs={{0,1},{1,0},{2,3},{3,2},{4,5},{5,4},{6,7},{7,6},{8,9},{9,8},{10,11... | collective-permute-start | bytes 491528 | tf_op jit(solution)/shard_map/ppermute | solution.py:23
  20.4 4.7 %collective-permute-start.6 = (bf16[64,1280]{1,0:T(8,128)(2,1)S(1)}, bf16[64,1280]{1,0:T(8,128)(2,1)S(1)}, u32[]{:S(2)}, u32[]{:S(2)}) collective-permute-start(bf16[64,1280]{1,0:T(8,128)(2,1)S(1)} %collective-permute-done.5.refs_6_), channel_id=1, source_target_pairs={{0,2},{1,17},{2,0},{3,19},{4,6},{5,21},{6,4},{7,23},{8,10},{9,25},... | collective-permute-start | bytes 491528 | tf_op jit(solution)/shard_map/ppermute | solution.py:23
  20.7 14.9 %collective-permute-start.1 = (bf16[128,1280]{1,0:T(8,128)(2,1)S(1)}, bf16[128,1280]{1,0:T(8,128)(2,1)S(1)}, u32[]{:S(2)}, u32[]{:S(2)}) collective-permute-start(bf16[128,1280]{1,0:T(8,128)(2,1)S(1)} %pad_maximum_fusion), channel_id=1, source_target_pairs={{0,16},{1,3},{2,18},{3,1},{4,20},{5,7},{6,22},{7,5},{8,24},{9,11},... | collective-permute-start | bytes 983048 | tf_op jit(solution)/shard_map/ppermute | solution.py:23
  22.0 6.6 %collective-permute-start.21 = (bf16[64,1280]{1,0:T(8,128)(2,1)S(1)}, bf16[64,1280]{1,0:T(8,128)(2,1)S(1)}, u32[]{:S(2)}, u32[]{:S(2)}) collective-permute-start(bf16[64,1280]{1,0:T(8,128)(2,1)S(1)} %collective-permute-done.8.refs_9_), channel_id=1, source_target_pairs={{0,1},{1,0},{2,3},{3,2},{4,5},{5,4},{6,7},{7,6},{8,9},{9,8},{10,11... | collective-permute-start | bytes 491528 | tf_op jit(solution)/shard_map/ppermute | solution.py:23
  23.6 8.7 %collective-permute-start.10 = (bf16[64,1280]{1,0:T(8,128)(2,1)S(1)}, bf16[64,1280]{1,0:T(8,128)(2,1)S(1)}, u32[]{:S(2)}, u32[]{:S(2)}) collective-permute-start(bf16[64,1280]{1,0:T(8,128)(2,1)S(1)} %collective-permute-done.8.refs_9_), channel_id=1, source_target_pairs={{0,16},{1,3},{2,18},{3,1},{4,20},{5,7},{6,22},{7,5},{8,24},{9,11},... | collective-permute-start | bytes 491528 | tf_op jit(solution)/shard_map/ppermute | solution.py:23
  23.9 9.6 %collective-permute-start.9 = (bf16[64,1280]{1,0:T(8,128)(2,1)S(1)}, bf16[64,1280]{1,0:T(8,128)(2,1)S(1)}, u32[]{:S(2)}, u32[]{:S(2)}) collective-permute-start(bf16[64,1280]{1,0:T(8,128)(2,1)S(1)} %collective-permute-done.8.refs_9_), channel_id=1, source_target_pairs={{0,2},{1,17},{2,0},{3,19},{4,6},{5,21},{6,4},{7,23},{8,10},{9,25},... | collective-permute-start | bytes 491528 | tf_op jit(solution)/shard_map/ppermute | solution.py:23
  25.1 9.1 %collective-permute-start.16 = (bf16[64,1280]{1,0:T(8,128)(2,1)S(1)}, bf16[64,1280]{1,0:T(8,128)(2,1)S(1)}, u32[]{:S(2)}, u32[]{:S(2)}) collective-permute-start(bf16[64,1280]{1,0:T(8,128)(2,1)S(1)} %collective-permute-done.3.refs_4_), channel_id=1, source_target_pairs={{0,1},{1,0},{2,3},{3,2},{4,5},{5,4},{6,7},{7,6},{8,9},{9,8},{10,11... | collective-permute-start | bytes 491528 | tf_op jit(solution)/shard_map/ppermute | solution.py:23
  28.6 8.7 %collective-permute-start.4 = (bf16[128,1280]{1,0:T(8,128)(2,1)S(1)}, bf16[128,1280]{1,0:T(8,128)(2,1)S(1)}, u32[]{:S(2)}, u32[]{:S(2)}) collective-permute-start(bf16[128,1280]{1,0:T(8,128)(2,1)S(1)} %pad_maximum_fusion.1), channel_id=1, source_target_pairs={{0,16},{1,3},{2,18},{3,1},{4,20},{5,7},{6,22},{7,5},{8,24},{9,11},... | collective-permute-start | bytes 983048 | tf_op jit(solution)/shard_map/ppermute | solution.py:23
  32.3 7.0 %collective-permute-start.7 = (bf16[128,1280]{1,0:T(8,128)(2,1)S(1)}, bf16[128,1280]{1,0:T(8,128)(2,1)S(1)}, u32[]{:S(2)}, u32[]{:S(2)}) collective-permute-start(bf16[128,1280]{1,0:T(8,128)(2,1)S(1)} %pad_maximum_fusion.2), channel_id=1, source_target_pairs={{0,16},{1,3},{2,18},{3,1},{4,20},{5,7},{6,22},{7,5},{8,24},{9,11},... | collective-permute-start | bytes 983048 | tf_op jit(solution)/shard_map/ppermute | solution.py:23
  33.5 1.8 %collective-permute-start.18 = (bf16[64,1280]{1,0:T(8,128)(2,1)S(1)}, bf16[64,1280]{1,0:T(8,128)(2,1)S(1)}, u32[]{:S(2)}, u32[]{:S(2)}) collective-permute-start(bf16[64,1280]{1,0:T(8,128)(2,1)S(1)} %collective-permute-done.5.refs_6_), channel_id=1, source_target_pairs={{0,1},{1,0},{2,3},{3,2},{4,5},{5,4},{6,7},{7,6},{8,9},{9,8},{10,11... | collective-permute-start | bytes 491528 | tf_op jit(solution)/shard_map/ppermute | solution.py:23
  34.2 1.6 %collective-permute-start.23 = (bf16[64,1280]{1,0:T(8,128)(2,1)S(1)}, bf16[64,1280]{1,0:T(8,128)(2,1)S(1)}, u32[]{:S(2)}, u32[]{:S(2)}) collective-permute-start(bf16[64,1280]{1,0:T(8,128)(2,1)S(1)} %collective-permute-done.10.refs_11_), channel_id=1, source_target_pairs={{0,1},{1,0},{2,3},{3,2},{4,5},{5,4},{6,7},{7,6},{8,9},{9,8},{10,11... | collective-permute-start | bytes 491528 | tf_op jit(solution)/shard_map/ppermute | solution.py:23
  35.2 5.5 %collective-permute-start.22 = (bf16[64,1280]{1,0:T(8,128)(2,1)S(1)}, bf16[64,1280]{1,0:T(8,128)(2,1)S(1)}, u32[]{:S(2)}, u32[]{:S(2)}) collective-permute-start(bf16[64,1280]{1,0:T(8,128)(2,1)S(1)} %collective-permute-done.9.refs_10_), channel_id=1, source_target_pairs={{0,1},{1,0},{2,3},{3,2},{4,5},{5,4},{6,7},{7,6},{8,9},{9,8},{10,11... | collective-permute-start | bytes 491528 | tf_op jit(solution)/shard_map/ppermute | solution.py:23
  35.6 5.5 %collective-permute-start.11 = (bf16[64,1280]{1,0:T(8,128)(2,1)S(1)}, bf16[64,1280]{1,0:T(8,128)(2,1)S(1)}, u32[]{:S(2)}, u32[]{:S(2)}) collective-permute-start(bf16[64,1280]{1,0:T(8,128)(2,1)S(1)} %collective-permute-done.9.refs_10_), channel_id=1, source_target_pairs={{0,16},{1,3},{2,18},{3,1},{4,20},{5,7},{6,22},{7,5},{8,24},{9,11},... | collective-permute-start | bytes 491528 | tf_op jit(solution)/shard_map/ppermute | solution.py:23
  35.8 7.7 %collective-permute-start.14 = (bf16[128,1280]{1,0:T(8,128)(2,1)S(1)}, bf16[128,1280]{1,0:T(8,128)(2,1)S(1)}, u32[]{:S(2)}, u32[]{:S(2)}) collective-permute-start(bf16[128,1280]{1,0:T(8,128)(2,1)S(1)} %collective-permute-done.1.refs_2_), channel_id=1, source_target_pairs={{0,1},{1,0},{2,3},{3,2},{4,5},{5,4},{6,7},{7,6},{8,9},{9,8},{10,11... | collective-permute-start | bytes 983048 | tf_op jit(solution)/shard_map/ppermute | solution.py:23
  37.3 6.3 %collective-permute-start.17 = (bf16[128,1280]{1,0:T(8,128)(2,1)S(1)}, bf16[128,1280]{1,0:T(8,128)(2,1)S(1)}, u32[]{:S(2)}, u32[]{:S(2)}) collective-permute-start(bf16[128,1280]{1,0:T(8,128)(2,1)S(1)} %collective-permute-done.4.refs_5_), channel_id=1, source_target_pairs={{0,1},{1,0},{2,3},{3,2},{4,5},{5,4},{6,7},{7,6},{8,9},{9,8},{10,11... | collective-permute-start | bytes 983048 | tf_op jit(solution)/shard_map/ppermute | solution.py:23
  39.3 4.2 %collective-permute-start.20 = (bf16[128,1280]{1,0:T(8,128)(2,1)S(1)}, bf16[128,1280]{1,0:T(8,128)(2,1)S(1)}, u32[]{:S(2)}, u32[]{:S(2)}) collective-permute-start(bf16[128,1280]{1,0:T(8,128)(2,1)S(1)} %collective-permute-done.7.refs_8_), channel_id=1, source_target_pairs={{0,1},{1,0},{2,3},{3,2},{4,5},{5,4},{6,7},{7,6},{8,9},{9,8},{10,11... | collective-permute-start | bytes 983048 | tf_op jit(solution)/shard_map/ppermute | solution.py:23
  40.7 1.8 %collective-permute-start.19 = (bf16[64,1280]{1,0:T(8,128)(2,1)S(1)}, bf16[64,1280]{1,0:T(8,128)(2,1)S(1)}, u32[]{:S(2)}, u32[]{:S(2)}) collective-permute-start(bf16[64,1280]{1,0:T(8,128)(2,1)S(1)} %collective-permute-done.6.refs_7_), channel_id=1, source_target_pairs={{0,1},{1,0},{2,3},{3,2},{4,5},{5,4},{6,7},{7,6},{8,9},{9,8},{10,11... | collective-permute-start | bytes 491528 | tf_op jit(solution)/shard_map/ppermute | solution.py:23
  41.1 2.5 %collective-permute-start.24 = (bf16[64,1280]{1,0:T(8,128)(2,1)S(1)}, bf16[64,1280]{1,0:T(8,128)(2,1)S(1)}, u32[]{:S(2)}, u32[]{:S(2)}) collective-permute-start(bf16[64,1280]{1,0:T(8,128)(2,1)S(1)} %collective-permute-done.11.refs_12_), channel_id=1, source_target_pairs={{0,1},{1,0},{2,3},{3,2},{4,5},{5,4},{6,7},{7,6},{8,9},{9,8},{10,11... | collective-permute-start | bytes 491528 | tf_op jit(solution)/shard_map/ppermute | solution.py:23

commit v3 on v2

--- a/solution.py
+++ b/solution.py
@@ -7,7 +7,8 @@
 
 AXES = ("row", "col")
 GROUP = 32
-Z_ORDER = (0, 1, 3, 2)
+HELD = ((0, 1, 0), (0, 0, 1), (0, 1, 1), (2, 0, 0), (1, 0, 0), (3, 0, 0), (1, 1, 0), (3, 1, 0))
+HELD += ((1, 0, 1), (3, 0, 1), (1, 1, 1), (3, 1, 1), (2, 1, 0), (2, 0, 1), (2, 1, 1), (0, 0, 0))
 
 
 def after(value, *earlier):
@@ -44,17 +45,19 @@
 
 
 def gather(row, count):
+    first = flip_first(row, count)
     near = along_z(row, count, 1)
-    first = flip_first(row, count)
-    next_near = along_z(after(row, first), count, 3)
-    far = along_z(after(row, near), count, 2)
-    pieces = [row, first, flip_second(join(row, first), count)]
-    first = flip_first(near, count)
-    pieces += [near, first, flip_second(join(near, first), count)]
-    first = flip_first(next_near, count)
-    pieces += [next_near, first, flip_second(join(next_near, first), count)]
-    first = flip_first(far, count)
-    pieces += [far, first, flip_second(far, count), flip_second(first, count)]
+    next_near = along_z(row, count, 3)
+    second = flip_second(join(row, first), count)
+    far = along_z(after(row, first), count, 2)
+    pair = join(near, next_near)
+    pair_first = flip_first(after(pair, second), count)
+    pair_second = flip_second(after(pair, second), count)
+    pair_last = flip_second(pair_first, count)
+    far_first = flip_first(far, count)
+    far_second = flip_second(far, count)
+    far_last = flip_second(far_first, count)
+    pieces = [first, second, far, pair, pair_first, pair_second, pair_last, far_first, far_second, far_last, row]
     return pieces + [flip_core(piece, count) for piece in pieces]
 
 
@@ -112,10 +115,9 @@
         for core in range(2):
             odd = parity if core == 0 else 1 - parity
             flip = first_flip(odd)
-            for k, step in enumerate(Z_ORDER):
+            for number, (step, one, two) in enumerate(HELD):
                 base = (local & ~13) | ((((local >> 2) & 3) + 4 - step) % 4 << 2) | odd
-                for number, turned in enumerate((base, base ^ flip, base ^ (18 - flip), base ^ 18)):
-                    put(held[16 * core + 4 * k + number], shift + turned, odd)
+                put(held[16 * core + number], shift + (base ^ (one * flip + two * (18 - flip))), odd)
 
     shape = (128, mask_ref.shape[1])
     lane = lax.broadcasted_iota(jnp.int32, shape, 0)
@@ -123,33 +125,36 @@
     spread = (lax.broadcasted_iota(jnp.int32, shape, 1) // block == slot + lane // block + 4) & (slot < slots)
     mask_ref[...] = dot(flag_ref[...].astype(bits), spread.astype(bits))
 
-    chunks = ((0, 2 * panel, 0, 5 * panel), (2 * panel, 2 * panel, 0, window), (4 * panel, window - 4 * panel, panel, window))
-
-    def group(m, carry):
-        at = pl.multiple_of(m * panel, panel)
+    def spans():
+        for n in range(0, window, panel):
+            size = min(panel, window - n)
+            low = max(0, n - half * block) // 128 * 128
+            high = min(window, -(-(n + size + half * block) // 128) * 128)
+            yield n, size, low, high
+
+    for m in range(5):
+        at = m * panel
 
         def kept(n, size):
             rows = []
             for w in range(n // block, (n + size) // block):
                 column = (22 + w % 2 - w) * block
-                row = mask_ref[pl.ds(4 * m + w, 1), column : column + panel]
+                row = mask_ref[4 * m + w : 4 * m + w + 1, column : column + panel]
                 rows.append(jnp.broadcast_to(row, (block, panel)))
             return jnp.concatenate(rows, axis=0)
 
         def rows(first, size, low, high):
-            return band_ref[pl.ds(at + first, size), pl.ds(pl.multiple_of(left + at + low, 128), high - low)]
-
-        for n, size, low, high in chunks:
+            return band_ref[at + first : at + first + size, left + at + low : left + at + high]
+
+        for n, size, low, high in spans():
             square = kept(n, size) * dot(rows(n, size, low, high), rows(half * block, panel, low, high), 1)
             square_ref[n : n + size, :] = square
             low_ref[n : n + size, :] = square.astype(bits)
-        for n, size, low, high in chunks:
-            cube = dot(rows(n, size, low, high), low_ref[low:high, :])
-            current = kept(n, size) * (3.0 * square_ref[n : n + size, :] - 2.0 * cube)
-            next_ref[pl.ds(at + n, size), pl.ds(pl.multiple_of(at + 2 * block, 128), panel)] = current.astype(bits)
-        return carry
-
-    lax.fori_loop(0, 5, group, 0)
+        for n, size, low, high in spans():
+            if half * block < at + n + size and at + n < (half + 20) * block:
+                cube = dot(rows(n, size, low, high), low_ref[low:high, :])
+                current = kept(n, size) * (3.0 * square_ref[n : n + size, :] - 2.0 * cube)
+                next_ref[at + n : at + n + size, at + 2 * block : at + 2 * block + panel] = current.astype(bits)
 
     inner = slice(half * block, (half + 20) * block)
     chosen = lax.broadcasted_iota(jnp.int32, (block, panel), 1)

time: 59.3 us -> 52.3 us (0.88)
  the two profiles are of different devices: /device:TPU:11 before, /device:TPU:0 now
where the time goes in v3:
time: 52.3 us; the launch traced here: 52.1 us
  starting transfers between devices  20.3 us (39%)
  waiting for transfers between devices  17.6 us (34%)
  Pallas kernels  12.3 us (24%)
  other arithmetic  1.13 us (2%)
  local copies, waits for them, and re-layouts  0.69 us (1%)
    ppermute x22, starting transfers between devices, send(): lax.ppermute(value, AXES, [(s, t) for s, t in pairs if 0 <= t < count])  20.3 us
    ppermute x22, waiting for transfers between devices, send(): lax.ppermute(value, AXES, [(s, t) for s, t in pairs if 0 <= t < count])  17.6 us
    pallas_call x1, Pallas kernels, local(): pl.pallas_call(kernel, out_shape=jax.ShapeDtypeStruct((block, width), jnp...  12.3 us
  transfers between devices with their start and end apart: 22, of which 9 were waited for; matrix products, arithmetic and copies ran while one was open for 0% of the time, Pallas kernels for 0%

profile of v3, /device:TPU:0, one launch (start us, length us, event | category | flops | bytes accessed | tf_op | source)
XLA Modules:
  0.0 52.1 jit_solution(1146486646998376086)
XLA Ops:
  0.0 0.7 %copy-done = s32[1,19]{1,0:T(1,128)S(1)} copy-done((s32[1,19]{1,0:T(1,128)S(1)}, s32[1,19]{1,0:T(1,128)}, u32[]{:S(2)}) %copy-start) | copy-done | bytes 100
  0.7 1.0 %convert_element_type.9 = bf16[64,1216]{1,0:T(8,128)(2,1)S(1)} convert(f32[64,1216]{1,0:T(8,128)} %param.2) | non-fusion elementwise | flops 77824 | bytes 466944 | tf_op jit(solution)/shard_map/convert_element_type | solution.py:182
  1.7 0.1 maximum_select_fusion.refs_10_
  1.8 3.0 %collective-permute-start = (bf16[64,1280]{1,0:T(8,128)(2,1)S(1)}, bf16[64,1280]{1,0:T(8,128)(2,1)S(1)}, u32[]{:S(2)}, u32[]{:S(2)}) collective-permute-start(bf16[64,1280]{1,0:T(8,128)(2,1)S(1)} %maximum_select_fusion.refs_10_), channel_id=1, source_target_pairs={{0,2},{1,17},{2,0},{3,19},{4,6},{5,21},{6,4},{7,23},{8,10},{9,25},... | collective-permute-start | bytes 491528 | tf_op jit(solution)/shard_map/ppermute | solution.py:24
  4.8 3.6 %collective-permute-start.4 = (bf16[64,1280]{1,0:T(8,128)(2,1)S(1)}, bf16[64,1280]{1,0:T(8,128)(2,1)S(1)}, u32[]{:S(2)}, u32[]{:S(2)}) collective-permute-start(bf16[64,1280]{1,0:T(8,128)(2,1)S(1)} %maximum_select_fusion.refs_10_), channel_id=1, source_target_pairs={{0,12},{1,13},{2,14},{3,15},{4,0},{5,1},{6,2},{7,3},{8,4},{9,5},{1... | collective-permute-start | bytes 491528 | tf_op jit(solution)/shard_map/ppermute | solution.py:24
  8.4 2.8 %collective-permute-start.2 = (bf16[64,1280]{1,0:T(8,128)(2,1)S(1)}, bf16[64,1280]{1,0:T(8,128)(2,1)S(1)}, u32[]{:S(2)}, u32[]{:S(2)}) collective-permute-start(bf16[64,1280]{1,0:T(8,128)(2,1)S(1)} %maximum_select_fusion.refs_10_), channel_id=1, source_target_pairs={{0,8},{1,9},{2,10},{3,11},{4,12},{5,13},{6,14},{7,15},{8,0},{9,1},... | collective-permute-start | bytes 491528 | tf_op jit(solution)/shard_map/ppermute | solution.py:24
  11.3 1.6 %collective-permute-start.1 = (bf16[128,1280]{1,0:T(8,128)(2,1)S(1)}, bf16[128,1280]{1,0:T(8,128)(2,1)S(1)}, u32[]{:S(2)}, u32[]{:S(2)}) collective-permute-start(bf16[128,1280]{1,0:T(8,128)(2,1)S(1)} %pad_maximum_fusion), channel_id=1, source_target_pairs={{0,16},{1,3},{2,18},{3,1},{4,20},{5,7},{6,22},{7,5},{8,24},{9,11},... | collective-permute-start | bytes 983048 | tf_op jit(solution)/shard_map/ppermute | solution.py:24
  12.8 4.7 %collective-permute-done.3 = bf16[64,1280]{1,0:T(8,128)(2,1)S(1)} collective-permute-done((bf16[64,1280]{1,0:T(8,128)(2,1)S(1)}, bf16[64,1280]{1,0:T(8,128)(2,1)S(1)}, u32[]{:S(2)}, u32[]{:S(2)}) %collective-permute-start.3) | collective-permute-done | bytes 163872 | tf_op jit(solution)/shard_map/ppermute | solution.py:24
  17.5 0.9 %collective-permute-done.1.refs_1_ = bf16[128,1280]{1,0:T(8,128)(2,1)S(1)} collective-permute-done((bf16[128,1280]{1,0:T(8,128)(2,1)S(1)}, bf16[128,1280]{1,0:T(8,128)(2,1)S(1)}, u32[]{:S(2)}, u32[]{:S(2)}) %collective-permute-start.1) | collective-permute-done | bytes 327712 | tf_op jit(solution)/shard_map/ppermute | solution.py:24
  18.4 1.5 %collective-permute-start.5 = (bf16[128,1280]{1,0:T(8,128)(2,1)S(1)}, bf16[128,1280]{1,0:T(8,128)(2,1)S(1)}, u32[]{:S(2)}, u32[]{:S(2)}) collective-permute-start(bf16[128,1280]{1,0:T(8,128)(2,1)S(1)} %constant_dynamic-update-slice_fusion.refs_3_), channel_id=1, source_target_pairs={{0,2},{1,17},{2,0},{3,19},{4,6},{5,21},{6,4},{7,23},{8,10},{9,25},... | collective-permute-start | bytes 983048 | tf_op jit(solution)/shard_map/ppermute | solution.py:24
  19.9 0.0 collective-permute-start.21
  19.9 0.5 collective-permute-start.11
  20.4 1.6 %collective-permute-done.2.refs_2_ = bf16[64,1280]{1,0:T(8,128)(2,1)S(1)} collective-permute-done((bf16[64,1280]{1,0:T(8,128)(2,1)S(1)}, bf16[64,1280]{1,0:T(8,128)(2,1)S(1)}, u32[]{:S(2)}, u32[]{:S(2)}) %collective-permute-start.2) | collective-permute-done | bytes 163872 | tf_op jit(solution)/shard_map/ppermute | solution.py:24
  22.0 0.5 collective-permute-start.14
  22.5 0.0 collective-permute-done.21.refs_21_
  22.5 1.2 %collective-permute-start.9 = (bf16[64,1280]{1,0:T(8,128)(2,1)S(1)}, bf16[64,1280]{1,0:T(8,128)(2,1)S(1)}, u32[]{:S(2)}, u32[]{:S(2)}) collective-permute-start(bf16[64,1280]{1,0:T(8,128)(2,1)S(1)} %collective-permute-done.2.refs_2_), channel_id=1, source_target_pairs={{0,16},{1,3},{2,18},{3,1},{4,20},{5,7},{6,22},{7,5},{8,24},{9,11},... | collective-permute-start | bytes 491528 | tf_op jit(solution)/shard_map/ppermute | solution.py:24
  23.7 0.0 collective-permute-done.11.refs_11_
  23.7 1.5 %collective-permute-start.8 = (bf16[64,1280]{1,0:T(8,128)(2,1)S(1)}, bf16[64,1280]{1,0:T(8,128)(2,1)S(1)}, u32[]{:S(2)}, u32[]{:S(2)}) collective-permute-start(bf16[64,1280]{1,0:T(8,128)(2,1)S(1)} %collective-permute-done.2.refs_2_), channel_id=1, source_target_pairs={{0,2},{1,17},{2,0},{3,19},{4,6},{5,21},{6,4},{7,23},{8,10},{9,25},... | collective-permute-start | bytes 491528 | tf_op jit(solution)/shard_map/ppermute | solution.py:24
  25.2 0.9 %collective-permute-start.6 = (bf16[128,1280]{1,0:T(8,128)(2,1)S(1)}, bf16[128,1280]{1,0:T(8,128)(2,1)S(1)}, u32[]{:S(2)}, u32[]{:S(2)}) collective-permute-start(bf16[128,1280]{1,0:T(8,128)(2,1)S(1)} %constant_dynamic-update-slice_fusion.refs_3_), channel_id=1, source_target_pairs={{0,16},{1,3},{2,18},{3,1},{4,20},{5,7},{6,22},{7,5},{8,24},{9,11},... | collective-permute-start | bytes 983048 | tf_op jit(solution)/shard_map/ppermute | solution.py:24
  26.1 0.0 collective-permute-done.5.refs_4_
  26.1 1.5 %collective-permute-start.7 = (bf16[128,1280]{1,0:T(8,128)(2,1)S(1)}, bf16[128,1280]{1,0:T(8,128)(2,1)S(1)}, u32[]{:S(2)}, u32[]{:S(2)}) collective-permute-start(bf16[128,1280]{1,0:T(8,128)(2,1)S(1)} %collective-permute-done.5.refs_4_), channel_id=1, source_target_pairs={{0,16},{1,3},{2,18},{3,1},{4,20},{5,7},{6,22},{7,5},{8,24},{9,11},... | collective-permute-start | bytes 983048 | tf_op jit(solution)/shard_map/ppermute | solution.py:24
  27.5 1.8 %collective-permute-done.9.refs_8_ = bf16[64,1280]{1,0:T(8,128)(2,1)S(1)} collective-permute-done((bf16[64,1280]{1,0:T(8,128)(2,1)S(1)}, bf16[64,1280]{1,0:T(8,128)(2,1)S(1)}, u32[]{:S(2)}, u32[]{:S(2)}) %collective-permute-start.9) | collective-permute-done | bytes 163872 | tf_op jit(solution)/shard_map/ppermute | solution.py:24
  29.3 1.5 %collective-permute-done.8.refs_7_ = bf16[64,1280]{1,0:T(8,128)(2,1)S(1)} collective-permute-done((bf16[64,1280]{1,0:T(8,128)(2,1)S(1)}, bf16[64,1280]{1,0:T(8,128)(2,1)S(1)}, u32[]{:S(2)}, u32[]{:S(2)}) %collective-permute-start.8) | collective-permute-done | bytes 163872 | tf_op jit(solution)/shard_map/ppermute | solution.py:24
  30.8 0.0 collective-permute-start.18
  30.9 0.9 %collective-permute-start.10 = (bf16[64,1280]{1,0:T(8,128)(2,1)S(1)}, bf16[64,1280]{1,0:T(8,128)(2,1)S(1)}, u32[]{:S(2)}, u32[]{:S(2)}) collective-permute-start(bf16[64,1280]{1,0:T(8,128)(2,1)S(1)} %collective-permute-done.8.refs_7_), channel_id=1, source_target_pairs={{0,16},{1,3},{2,18},{3,1},{4,20},{5,7},{6,22},{7,5},{8,24},{9,11},... | collective-permute-start | bytes 491528 | tf_op jit(solution)/shard_map/ppermute | solution.py:24
  31.7 0.8 %collective-permute-start.12 = (bf16[128,1280]{1,0:T(8,128)(2,1)S(1)}, bf16[128,1280]{1,0:T(8,128)(2,1)S(1)}, u32[]{:S(2)}, u32[]{:S(2)}) collective-permute-start(bf16[128,1280]{1,0:T(8,128)(2,1)S(1)} %collective-permute-done.1.refs_1_), channel_id=1, source_target_pairs={{0,1},{1,0},{2,3},{3,2},{4,5},{5,4},{6,7},{7,6},{8,9},{9,8},{10,11... | collective-permute-start | bytes 983048 | tf_op jit(solution)/shard_map/ppermute | solution.py:24
  32.5 0.1 collective-permute-start.15
  32.6 0.5 collective-permute-done.6.refs_5_
  33.1 3.5 %collective-permute-done.7.refs_6_ = bf16[128,1280]{1,0:T(8,128)(2,1)S(1)} collective-permute-done((bf16[128,1280]{1,0:T(8,128)(2,1)S(1)}, bf16[128,1280]{1,0:T(8,128)(2,1)S(1)}, u32[]{:S(2)}, u32[]{:S(2)}) %collective-permute-start.7) | collective-permute-done | bytes 327712 | tf_op jit(solution)/shard_map/ppermute | solution.py:24
  36.6 1.8 %collective-permute-done.10.refs_9_ = bf16[64,1280]{1,0:T(8,128)(2,1)S(1)} collective-permute-done((bf16[64,1280]{1,0:T(8,128)(2,1)S(1)}, bf16[64,1280]{1,0:T(8,128)(2,1)S(1)}, u32[]{:S(2)}, u32[]{:S(2)}) %collective-permute-start.10) | collective-permute-done | bytes 163872 | tf_op jit(solution)/shard_map/ppermute | solution.py:24
  38.4 1.4 %collective-permute-done.20.refs_20_ = bf16[64,1280]{1,0:T(8,128)(2,1)S(1)} collective-permute-done((bf16[64,1280]{1,0:T(8,128)(2,1)S(1)}, bf16[64,1280]{1,0:T(8,128)(2,1)S(1)}, u32[]{:S(2)}, u32[]{:S(2)}) %collective-permute-start.20) | collective-permute-done | bytes 163872 | tf_op jit(solution)/shard_map/ppermute | solution.py:24
  39.8 12.3 %shard_map.28 = f32[64,1216]{1,0:T(8,128)} custom-call(bf16[64,1280]{1,0:T(8,128)(2,1)S(1)} %collective-permute-done.refs_0_, bf16[128,1280]{1,0:T(8,128)(2,1)S(1)} %collective-permute-done.1.refs_1_, bf16[64,1280]{1,0:T(8,128)(2,1)S(1)} %collective-permute-done.2.refs_2_, bf16[128,1280]{1,0:T(8,128)(2,1)S(1)} %constant_dynamic-update-slice_fusion.refs_3_, ...), custom_call_target="tpu_custom_call" | custom-call | tf_op jit(solution)/shard_map/pallas_call | solution.py:203
  (23 shorter events, 0.1 us)
Async XLA Ops:
  0.0 0.7 %copy-start = (s32[1,19]{1,0:T(1,128)S(1)}, s32[1,19]{1,0:T(1,128)}, u32[]{:S(2)}) copy-start(s32[1,19]{1,0:T(1,128)} %param.3) | copy-start | bytes 232
  1.8 6.6 %collective-permute-start = (bf16[64,1280]{1,0:T(8,128)(2,1)S(1)}, bf16[64,1280]{1,0:T(8,128)(2,1)S(1)}, u32[]{:S(2)}, u32[]{:S(2)}) collective-permute-start(bf16[64,1280]{1,0:T(8,128)(2,1)S(1)} %maximum_select_fusion.refs_10_), channel_id=1, source_target_pairs={{0,2},{1,17},{2,0},{3,19},{4,6},{5,21},{6,4},{7,23},{8,10},{9,25},... | collective-permute-start | bytes 491528 | tf_op jit(solution)/shard_map/ppermute | solution.py:24
  4.8 12.7 %collective-permute-start.4 = (bf16[64,1280]{1,0:T(8,128)(2,1)S(1)}, bf16[64,1280]{1,0:T(8,128)(2,1)S(1)}, u32[]{:S(2)}, u32[]{:S(2)}) collective-permute-start(bf16[64,1280]{1,0:T(8,128)(2,1)S(1)} %maximum_select_fusion.refs_10_), channel_id=1, source_target_pairs={{0,12},{1,13},{2,14},{3,15},{4,0},{5,1},{6,2},{7,3},{8,4},{9,5},{1... | collective-permute-start | bytes 491528 | tf_op jit(solution)/shard_map/ppermute | solution.py:24
  8.4 9.0 %collective-permute-start.3 = (bf16[64,1280]{1,0:T(8,128)(2,1)S(1)}, bf16[64,1280]{1,0:T(8,128)(2,1)S(1)}, u32[]{:S(2)}, u32[]{:S(2)}) collective-permute-start(bf16[64,1280]{1,0:T(8,128)(2,1)S(1)} %maximum_select_fusion.refs_10_), channel_id=1, source_target_pairs={{0,4},{1,5},{2,6},{3,7},{4,8},{5,9},{6,10},{7,11},{8,12},{9,13},{1... | collective-permute-start | bytes 491528 | tf_op jit(solution)/shard_map/ppermute | solution.py:24
  8.4 13.6 %collective-permute-start.2 = (bf16[64,1280]{1,0:T(8,128)(2,1)S(1)}, bf16[64,1280]{1,0:T(8,128)(2,1)S(1)}, u32[]{:S(2)}, u32[]{:S(2)}) collective-permute-start(bf16[64,1280]{1,0:T(8,128)(2,1)S(1)} %maximum_select_fusion.refs_10_), channel_id=1, source_target_pairs={{0,8},{1,9},{2,10},{3,11},{4,12},{5,13},{6,14},{7,15},{8,0},{9,1},... | collective-permute-start | bytes 491528 | tf_op jit(solution)/shard_map/ppermute | solution.py:24
  11.3 7.1 %collective-permute-start.1 = (bf16[128,1280]{1,0:T(8,128)(2,1)S(1)}, bf16[128,1280]{1,0:T(8,128)(2,1)S(1)}, u32[]{:S(2)}, u32[]{:S(2)}) collective-permute-start(bf16[128,1280]{1,0:T(8,128)(2,1)S(1)} %pad_maximum_fusion), channel_id=1, source_target_pairs={{0,16},{1,3},{2,18},{3,1},{4,20},{5,7},{6,22},{7,5},{8,24},{9,11},... | collective-permute-start | bytes 983048 | tf_op jit(solution)/shard_map/ppermute | solution.py:24
  18.4 7.7 %collective-permute-start.5 = (bf16[128,1280]{1,0:T(8,128)(2,1)S(1)}, bf16[128,1280]{1,0:T(8,128)(2,1)S(1)}, u32[]{:S(2)}, u32[]{:S(2)}) collective-permute-start(bf16[128,1280]{1,0:T(8,128)(2,1)S(1)} %constant_dynamic-update-slice_fusion.refs_3_), channel_id=1, source_target_pairs={{0,2},{1,17},{2,0},{3,19},{4,6},{5,21},{6,4},{7,23},{8,10},{9,25},... | collective-permute-start | bytes 983048 | tf_op jit(solution)/shard_map/ppermute | solution.py:24
  19.9 2.6 %collective-permute-start.21 = (bf16[64,1280]{1,0:T(8,128)(2,1)S(1)}, bf16[64,1280]{1,0:T(8,128)(2,1)S(1)}, u32[]{:S(2)}, u32[]{:S(2)}) collective-permute-start(bf16[64,1280]{1,0:T(8,128)(2,1)S(1)} %maximum_select_fusion.refs_10_), channel_id=1, source_target_pairs={{0,1},{1,0},{2,3},{3,2},{4,5},{5,4},{6,7},{7,6},{8,9},{9,8},{10,11... | collective-permute-start | bytes 491528 | tf_op jit(solution)/shard_map/ppermute | solution.py:24
  19.9 3.8 %collective-permute-start.11 = (bf16[64,1280]{1,0:T(8,128)(2,1)S(1)}, bf16[64,1280]{1,0:T(8,128)(2,1)S(1)}, u32[]{:S(2)}, u32[]{:S(2)}) collective-permute-start(bf16[64,1280]{1,0:T(8,128)(2,1)S(1)} %collective-permute-done.refs_0_), channel_id=1, source_target_pairs={{0,1},{1,0},{2,3},{3,2},{4,5},{5,4},{6,7},{7,6},{8,9},{9,8},{10,11... | collective-permute-start | bytes 491528 | tf_op jit(solution)/shard_map/ppermute | solution.py:24
  22.0 3.2 %collective-permute-start.13 = (bf16[64,1280]{1,0:T(8,128)(2,1)S(1)}, bf16[64,1280]{1,0:T(8,128)(2,1)S(1)}, u32[]{:S(2)}, u32[]{:S(2)}) collective-permute-start(bf16[64,1280]{1,0:T(8,128)(2,1)S(1)} %collective-permute-done.2.refs_2_), channel_id=1, source_target_pairs={{0,1},{1,0},{2,3},{3,2},{4,5},{5,4},{6,7},{7,6},{8,9},{9,8},{10,11... | collective-permute-start | bytes 491528 | tf_op jit(solution)/shard_map/ppermute | solution.py:24
  22.0 8.8 %collective-permute-start.14 = (bf16[128,1280]{1,0:T(8,128)(2,1)S(1)}, bf16[128,1280]{1,0:T(8,128)(2,1)S(1)}, u32[]{:S(2)}, u32[]{:S(2)}) collective-permute-start(bf16[128,1280]{1,0:T(8,128)(2,1)S(1)} %constant_dynamic-update-slice_fusion.refs_3_), channel_id=1, source_target_pairs={{0,1},{1,0},{2,3},{3,2},{4,5},{5,4},{6,7},{7,6},{8,9},{9,8},{10,11... | collective-permute-start | bytes 983048 | tf_op jit(solution)/shard_map/ppermute | solution.py:24
  22.5 6.8 %collective-permute-start.9 = (bf16[64,1280]{1,0:T(8,128)(2,1)S(1)}, bf16[64,1280]{1,0:T(8,128)(2,1)S(1)}, u32[]{:S(2)}, u32[]{:S(2)}) collective-permute-start(bf16[64,1280]{1,0:T(8,128)(2,1)S(1)} %collective-permute-done.2.refs_2_), channel_id=1, source_target_pairs={{0,16},{1,3},{2,18},{3,1},{4,20},{5,7},{6,22},{7,5},{8,24},{9,11},... | collective-permute-start | bytes 491528 | tf_op jit(solution)/shard_map/ppermute | solution.py:24
  23.7 7.1 %collective-permute-start.8 = (bf16[64,1280]{1,0:T(8,128)(2,1)S(1)}, bf16[64,1280]{1,0:T(8,128)(2,1)S(1)}, u32[]{:S(2)}, u32[]{:S(2)}) collective-permute-start(bf16[64,1280]{1,0:T(8,128)(2,1)S(1)} %collective-permute-done.2.refs_2_), channel_id=1, source_target_pairs={{0,2},{1,17},{2,0},{3,19},{4,6},{5,21},{6,4},{7,23},{8,10},{9,25},... | collective-permute-start | bytes 491528 | tf_op jit(solution)/shard_map/ppermute | solution.py:24
  25.2 7.9 %collective-permute-start.6 = (bf16[128,1280]{1,0:T(8,128)(2,1)S(1)}, bf16[128,1280]{1,0:T(8,128)(2,1)S(1)}, u32[]{:S(2)}, u32[]{:S(2)}) collective-permute-start(bf16[128,1280]{1,0:T(8,128)(2,1)S(1)} %constant_dynamic-update-slice_fusion.refs_3_), channel_id=1, source_target_pairs={{0,16},{1,3},{2,18},{3,1},{4,20},{5,7},{6,22},{7,5},{8,24},{9,11},... | collective-permute-start | bytes 983048 | tf_op jit(solution)/shard_map/ppermute | solution.py:24
  26.1 10.5 %collective-permute-start.7 = (bf16[128,1280]{1,0:T(8,128)(2,1)S(1)}, bf16[128,1280]{1,0:T(8,128)(2,1)S(1)}, u32[]{:S(2)}, u32[]{:S(2)}) collective-permute-start(bf16[128,1280]{1,0:T(8,128)(2,1)S(1)} %collective-permute-done.5.refs_4_), channel_id=1, source_target_pairs={{0,16},{1,3},{2,18},{3,1},{4,20},{5,7},{6,22},{7,5},{8,24},{9,11},... | collective-permute-start | bytes 983048 | tf_op jit(solution)/shard_map/ppermute | solution.py:24
  29.3 2.4 %collective-permute-start.19 = (bf16[64,1280]{1,0:T(8,128)(2,1)S(1)}, bf16[64,1280]{1,0:T(8,128)(2,1)S(1)}, u32[]{:S(2)}, u32[]{:S(2)}) collective-permute-start(bf16[64,1280]{1,0:T(8,128)(2,1)S(1)} %collective-permute-done.9.refs_8_), channel_id=1, source_target_pairs={{0,1},{1,0},{2,3},{3,2},{4,5},{5,4},{6,7},{7,6},{8,9},{9,8},{10,11... | collective-permute-start | bytes 491528 | tf_op jit(solution)/shard_map/ppermute | solution.py:24
  30.8 1.7 %collective-permute-start.18 = (bf16[64,1280]{1,0:T(8,128)(2,1)S(1)}, bf16[64,1280]{1,0:T(8,128)(2,1)S(1)}, u32[]{:S(2)}, u32[]{:S(2)}) collective-permute-start(bf16[64,1280]{1,0:T(8,128)(2,1)S(1)} %collective-permute-done.8.refs_7_), channel_id=1, source_target_pairs={{0,1},{1,0},{2,3},{3,2},{4,5},{5,4},{6,7},{7,6},{8,9},{9,8},{10,11... | collective-permute-start | bytes 491528 | tf_op jit(solution)/shard_map/ppermute | solution.py:24
  30.9 7.5 %collective-permute-start.10 = (bf16[64,1280]{1,0:T(8,128)(2,1)S(1)}, bf16[64,1280]{1,0:T(8,128)(2,1)S(1)}, u32[]{:S(2)}, u32[]{:S(2)}) collective-permute-start(bf16[64,1280]{1,0:T(8,128)(2,1)S(1)} %collective-permute-done.8.refs_7_), channel_id=1, source_target_pairs={{0,16},{1,3},{2,18},{3,1},{4,20},{5,7},{6,22},{7,5},{8,24},{9,11},... | collective-permute-start | bytes 491528 | tf_op jit(solution)/shard_map/ppermute | solution.py:24
  31.7 8.1 %collective-permute-start.12 = (bf16[128,1280]{1,0:T(8,128)(2,1)S(1)}, bf16[128,1280]{1,0:T(8,128)(2,1)S(1)}, u32[]{:S(2)}, u32[]{:S(2)}) collective-permute-start(bf16[128,1280]{1,0:T(8,128)(2,1)S(1)} %collective-permute-done.1.refs_1_), channel_id=1, source_target_pairs={{0,1},{1,0},{2,3},{3,2},{4,5},{5,4},{6,7},{7,6},{8,9},{9,8},{10,11... | collective-permute-start | bytes 983048 | tf_op jit(solution)/shard_map/ppermute | solution.py:24
  32.5 7.2 %collective-permute-start.15 = (bf16[128,1280]{1,0:T(8,128)(2,1)S(1)}, bf16[128,1280]{1,0:T(8,128)(2,1)S(1)}, u32[]{:S(2)}, u32[]{:S(2)}) collective-permute-start(bf16[128,1280]{1,0:T(8,128)(2,1)S(1)} %collective-permute-done.5.refs_4_), channel_id=1, source_target_pairs={{0,1},{1,0},{2,3},{3,2},{4,5},{5,4},{6,7},{7,6},{8,9},{9,8},{10,11... | collective-permute-start | bytes 983048 | tf_op jit(solution)/shard_map/ppermute | solution.py:24
  33.1 6.7 %collective-permute-start.16 = (bf16[128,1280]{1,0:T(8,128)(2,1)S(1)}, bf16[128,1280]{1,0:T(8,128)(2,1)S(1)}, u32[]{:S(2)}, u32[]{:S(2)}) collective-permute-start(bf16[128,1280]{1,0:T(8,128)(2,1)S(1)} %collective-permute-done.6.refs_5_), channel_id=1, source_target_pairs={{0,1},{1,0},{2,3},{3,2},{4,5},{5,4},{6,7},{7,6},{8,9},{9,8},{10,11... | collective-permute-start | bytes 983048 | tf_op jit(solution)/shard_map/ppermute | solution.py:24
  36.6 3.2 %collective-permute-start.17 = (bf16[128,1280]{1,0:T(8,128)(2,1)S(1)}, bf16[128,1280]{1,0:T(8,128)(2,1)S(1)}, u32[]{:S(2)}, u32[]{:S(2)}) collective-permute-start(bf16[128,1280]{1,0:T(8,128)(2,1)S(1)} %collective-permute-done.7.refs_6_), channel_id=1, source_target_pairs={{0,1},{1,0},{2,3},{3,2},{4,5},{5,4},{6,7},{7,6},{8,9},{9,8},{10,11... | collective-permute-start | bytes 983048 | tf_op jit(solution)/shard_map/ppermute | solution.py:24
  38.4 1.4 %collective-permute-start.20 = (bf16[64,1280]{1,0:T(8,128)(2,1)S(1)}, bf16[64,1280]{1,0:T(8,128)(2,1)S(1)}, u32[]{:S(2)}, u32[]{:S(2)}) collective-permute-start(bf16[64,1280]{1,0:T(8,128)(2,1)S(1)} %collective-permute-done.10.refs_9_), channel_id=1, source_target_pairs={{0,1},{1,0},{2,3},{3,2},{4,5},{5,4},{6,7},{7,6},{8,9},{9,8},{10,11... | collective-permute-start | bytes 491528 | tf_op jit(solution)/shard_map/ppermute | solution.py:24

commit v4 on v3

--- a/solution.py
+++ b/solution.py
@@ -61,6 +61,27 @@
     return pieces + [flip_core(piece, count) for piece in pieces]
 
 
+def prepare_kernel(density_ref, pattern_ref, row_ref):
+    block, width = density_ref.shape
+    slots = pattern_ref.shape[1]
+    flags = jnp.concatenate(
+        [pattern_ref[...].astype(jnp.float32), jnp.zeros((1, block - slots), jnp.float32)], axis=1
+    )
+    flags = jnp.broadcast_to(flags, (block, block)).astype(jnp.bfloat16)
+    parity = (lax.axis_index("row") * lax.axis_size("col") + lax.axis_index("col")) % 2
+    low = density_ref[...].astype(jnp.bfloat16)
+
+    @pl.when(parity == 0)
+    def _():
+        row_ref[:, :block] = flags
+        row_ref[:, block:] = low
+
+    @pl.when(parity == 1)
+    def _():
+        row_ref[:, :width] = low
+        row_ref[:, width:] = flags
+
+
 def dot(left, right, on=0):
     return lax.dot_general(left, right, (((1,), (on,)), ((), ())), preferred_element_type=jnp.float32)
 
@@ -81,9 +102,27 @@
     origin = place - parity - 2 * half
 
     left = 10 * block
-    band_ref[:, left : left + reach * block] = jnp.zeros((reach * block, reach * block), bits)
     flag_ref[...] = jnp.zeros_like(flag_ref)
-    next_ref[...] = jnp.zeros_like(next_ref)
+
+    def clear(ref, row, first, last, column):
+        if first < last:
+            shape = (block, (last - first) * block)
+            ref[row * block : (row + 1) * block, column + first * block : column + last * block] = jnp.zeros(shape, bits)
+
+    for row in range(reach):
+        first, tile = (row + 1) // 2 * 2 - half - 1, (row - half) // 4 * 4
+        clear(band_ref, row, max(0, tile), max(0, first), left)
+        clear(band_ref, row, min(reach, first + slots + 1), min(reach, tile + 2 * half + 4), left)
+
+        @pl.when((origin + row < 0) | (origin + row >= lax.axis_size("row") * lax.axis_size("col")))
+        def _():
+            clear(band_ref, row, first, first + slots + 1, left)
+
+    for row in range(half, half + 20):
+        clear(next_ref, row, 0, 2, 0)
+        for m in range(5):
+            if not 4 * m <= row < 4 * m + 2 * half + 4:
+                clear(next_ref, row, 4 * m + 2, 4 * m + 6, 0)
     lanes = lax.broadcasted_iota(jnp.int32, (block, 128), 1)
 
     def put(piece, index, odd):
@@ -125,44 +164,58 @@
     spread = (lax.broadcasted_iota(jnp.int32, shape, 1) // block == slot + lane // block + 4) & (slot < slots)
     mask_ref[...] = dot(flag_ref[...].astype(bits), spread.astype(bits))
 
-    def spans():
-        for n in range(0, window, panel):
-            size = min(panel, window - n)
-            low = max(0, n - half * block) // 128 * 128
-            high = min(window, -(-(n + size + half * block) // 128) * 128)
-            yield n, size, low, high
+    spans = [(0, 1, 0, 10), (1, 4, 0, 14), (5, 4, 0, 18), (9, 4, 0, 22), (13, 4, 4, 22), (17, 4, 8, 22), (21, 1, 12, 22)]
 
     for m in range(5):
-        at = m * panel
-
-        def kept(n, size):
+
+        def kept(first, size):
             rows = []
-            for w in range(n // block, (n + size) // block):
+            for w in range(first, first + size):
                 column = (22 + w % 2 - w) * block
                 row = mask_ref[4 * m + w : 4 * m + w + 1, column : column + panel]
                 rows.append(jnp.broadcast_to(row, (block, panel)))
             return jnp.concatenate(rows, axis=0)
 
         def rows(first, size, low, high):
-            return band_ref[at + first : at + first + size, left + at + low : left + at + high]
-
-        for n, size, low, high in spans():
-            square = kept(n, size) * dot(rows(n, size, low, high), rows(half * block, panel, low, high), 1)
-            square_ref[n : n + size, :] = square
-            low_ref[n : n + size, :] = square.astype(bits)
-        for n, size, low, high in spans():
-            if half * block < at + n + size and at + n < (half + 20) * block:
-                cube = dot(rows(n, size, low, high), low_ref[low:high, :])
-                current = kept(n, size) * (3.0 * square_ref[n : n + size, :] - 2.0 * cube)
-                next_ref[at + n : at + n + size, at + 2 * block : at + 2 * block + panel] = current.astype(bits)
+            at = 4 * m * block
+            columns = slice(left + at + low * block, left + at + high * block)
+            return band_ref[at + first * block : at + (first + size) * block, columns]
+
+        for step, (first, size, low, high) in enumerate(spans):
+            span = slice(first * block, (first + size) * block)
+            other = m + step - 3
+            if size == 4 and 0 <= other < m:
+                mirrored = (9 + 4 * (m - other)) * block
+                square = square_ref[other, mirrored : mirrored + panel, :].T
+            else:
+                square = kept(first, size) * dot(rows(first, size, low, high), rows(half, 4, low, high), 1)
+            square_ref[m, span, :] = square
+            low_ref[m, span, :] = square.astype(bits)
+        for first, size, low, high in spans:
+            if half <= 4 * m + first < half + 20:
+                span = slice(first * block, (first + size) * block)
+                cube = dot(rows(first, size, low, high), low_ref[m, low * block : high * block, :])
+                current = kept(first, size) * (3.0 * square_ref[m, span, :] - 2.0 * cube)
+                at = 4 * m * block
+                next_ref[at + span.start : at + span.stop, at + 2 * block : at + 6 * block] = current.astype(bits)
 
     inner = slice(half * block, (half + 20) * block)
     chosen = lax.broadcasted_iota(jnp.int32, (block, panel), 1)
     chosen = chosen == lax.broadcasted_iota(jnp.int32, (block, panel), 0) + (1 + parity) * block
     mine = dot(chosen.astype(bits), next_ref[inner, 10 * block : 14 * block], 1).astype(bits)
     kept = mask_ref[pl.ds(2 * half + parity, 1), 2 * block : 2 * block + window]
-    square = kept * dot(mine, next_ref[inner, :])
-    cube = dot(square.astype(bits)[:, 2 * block :], next_ref[inner, :])
+
+    def times_next(value):
+        parts = []
+        for n in range(0, window, panel):
+            low = max(0, n // block - half - 2) // 2 * 2 * block
+            high = min(20, -(-(n // block + half + 2) // 2) * 2) * block
+            rows = slice(half * block + low, half * block + high)
+            parts.append(dot(value[:, low:high], next_ref[rows, n : min(n + panel, window)]))
+        return jnp.concatenate(parts, axis=1)
+
+    square = kept * times_next(mine)
+    cube = times_next(square.astype(bits)[:, 2 * block :])
     current = kept * (3.0 * square - 2.0 * cube)
     out_ref[...] = jnp.where(
         parity == 0,
@@ -176,15 +229,12 @@
     slots = pattern.shape[1]
     half = (slots - 1) // 2
     count = lax.axis_size("row") * lax.axis_size("col")
-    place = lax.axis_index("row") * lax.axis_size("col") + lax.axis_index("col")
-    flags = jnp.broadcast_to(pattern.astype(jnp.bfloat16), (block, slots))
-    flags = jnp.pad(flags, ((0, 0), (0, block - slots)))
-    low = density.astype(jnp.bfloat16)
-    row = jnp.where(
-        place % 2 == 0,
-        jnp.concatenate([flags, low], axis=1),
-        jnp.concatenate([low, flags], axis=1),
-    )
+    row = pl.pallas_call(
+        prepare_kernel,
+        out_shape=pltpu.VMEM((block, width + block), jnp.bfloat16),
+        in_specs=[pl.BlockSpec(memory_space=pltpu.VMEM)] * 2,
+        out_specs=pl.BlockSpec(memory_space=pltpu.VMEM),
+    )(density, pattern)
     pieces = gather(row, count)
     copies = 1
     if count > GROUP:
@@ -210,10 +260,10 @@
             pltpu.VMEM((reach, window), jnp.bfloat16),
             pltpu.VMEM((40, 128), jnp.float32),
             pltpu.VMEM((40, 26 * block), jnp.float32),
-            pltpu.VMEM((window, 4 * block), jnp.float32),
-            pltpu.VMEM((window, 4 * block), jnp.bfloat16),
+            pltpu.VMEM((5, window, 4 * block), jnp.float32),
+            pltpu.VMEM((5, window, 4 * block), jnp.bfloat16),
         ],
-        compiler_params=pltpu.CompilerParams(vmem_limit_bytes=36 * 2**20),
+        compiler_params=pltpu.CompilerParams(vmem_limit_bytes=44 * 2**20),
     )(*pieces)
 
 

time: 52.3 us -> 49.7 us (0.950)
  other arithmetic: 1.13 us -> 0.02 us
  Pallas kernels: 12.3 us -> 11.6 us
  local copies, waits for them, and re-layouts: 0.69 us -> 0.02 us
    pallas_call x1, Pallas kernels: 12.3 us -> 10.5 us  [local(): pl.pallas_call(kernel, out_shape=jax.ShapeDtypeStruct((block, width), jnp...]
    pallas_call x0 -> x1, Pallas kernels: none -> 1.1 us  [local(): pl.pallas_call(prepare_kernel, out_shape=pltpu.VMEM((block, width + block...]
    convert_element_type x1 -> x0, other arithmetic: 0.99 us -> none  [local(): low = density.astype(jnp.bfloat16)]
    unnamed x3 -> x1, local copies, waits for them, and re-layouts: 0.67 us -> 0.01 us
where the time goes in v4:
time: 49.7 us; the launch traced here: 49.6 us
  starting transfers between devices  20.3 us (41%)
  waiting for transfers between devices  17.5 us (35%)
  Pallas kernels  11.6 us (23%)
    ppermute x22, starting transfers between devices, send(): lax.ppermute(value, AXES, [(s, t) for s, t in pairs if 0 <= t < count])  20.3 us
    ppermute x22, waiting for transfers between devices, send(): lax.ppermute(value, AXES, [(s, t) for s, t in pairs if 0 <= t < count])  17.5 us
    pallas_call x1, Pallas kernels, local(): pl.pallas_call(kernel, out_shape=jax.ShapeDtypeStruct((block, width), jnp...  10.5 us
    pallas_call x1, Pallas kernels, local(): pl.pallas_call(prepare_kernel, out_shape=pltpu.VMEM((block, width + block...  1.1 us
  transfers between devices with their start and end apart: 22, of which 9 were waited for; matrix products, arithmetic and copies ran while one was open for 0% of the time, Pallas kernels for 0%

profile of v4, /device:TPU:0, one launch (start us, length us, event | category | flops | bytes accessed | tf_op | source)
XLA Modules:
  0.0 49.6 jit_solution(2602590318601578337)
XLA Ops:
  0.0 1.1 %shard_map.28.refs_10_ = bf16[64,1280]{1,0:T(8,128)(2,1)S(1)} custom-call(f32[64,1216]{1,0:T(8,128)} %density_ref.1, s32[1,19]{1,0:T(1,128)} %pattern_ref.1), custom_call_target="tpu_custom_call" | custom-call | tf_op jit(solution)/shard_map/pallas_call | solution.py:232
  1.1 3.0 %collective-permute-start = (bf16[64,1280]{1,0:T(8,128)(2,1)S(1)}, bf16[64,1280]{1,0:T(8,128)(2,1)S(1)}, u32[]{:S(2)}, u32[]{:S(2)}) collective-permute-start(bf16[64,1280]{1,0:T(8,128)(2,1)S(1)} %shard_map.28.refs_10_), channel_id=1, source_target_pairs={{0,2},{1,17},{2,0},{3,19},{4,6},{5,21},{6,4},{7,23},{8,10},{9,25},... | collective-permute-start | bytes 491528 | tf_op jit(solution)/shard_map/ppermute | solution.py:24
  4.1 3.6 %collective-permute-start.4 = (bf16[64,1280]{1,0:T(8,128)(2,1)S(1)}, bf16[64,1280]{1,0:T(8,128)(2,1)S(1)}, u32[]{:S(2)}, u32[]{:S(2)}) collective-permute-start(bf16[64,1280]{1,0:T(8,128)(2,1)S(1)} %shard_map.28.refs_10_), channel_id=1, source_target_pairs={{0,12},{1,13},{2,14},{3,15},{4,0},{5,1},{6,2},{7,3},{8,4},{9,5},{1... | collective-permute-start | bytes 491528 | tf_op jit(solution)/shard_map/ppermute | solution.py:24
  7.7 0.0 collective-permute-start.3
  7.7 2.8 %collective-permute-start.2 = (bf16[64,1280]{1,0:T(8,128)(2,1)S(1)}, bf16[64,1280]{1,0:T(8,128)(2,1)S(1)}, u32[]{:S(2)}, u32[]{:S(2)}) collective-permute-start(bf16[64,1280]{1,0:T(8,128)(2,1)S(1)} %shard_map.28.refs_10_), channel_id=1, source_target_pairs={{0,8},{1,9},{2,10},{3,11},{4,12},{5,13},{6,14},{7,15},{8,0},{9,1},... | collective-permute-start | bytes 491528 | tf_op jit(solution)/shard_map/ppermute | solution.py:24
  10.6 1.6 %collective-permute-start.1 = (bf16[128,1280]{1,0:T(8,128)(2,1)S(1)}, bf16[128,1280]{1,0:T(8,128)(2,1)S(1)}, u32[]{:S(2)}, u32[]{:S(2)}) collective-permute-start(bf16[128,1280]{1,0:T(8,128)(2,1)S(1)} %pad_maximum_fusion), channel_id=1, source_target_pairs={{0,16},{1,3},{2,18},{3,1},{4,20},{5,7},{6,22},{7,5},{8,24},{9,11},... | collective-permute-start | bytes 983048 | tf_op jit(solution)/shard_map/ppermute | solution.py:24
  12.1 4.6 %collective-permute-done.3 = bf16[64,1280]{1,0:T(8,128)(2,1)S(1)} collective-permute-done((bf16[64,1280]{1,0:T(8,128)(2,1)S(1)}, bf16[64,1280]{1,0:T(8,128)(2,1)S(1)}, u32[]{:S(2)}, u32[]{:S(2)}) %collective-permute-start.3) | collective-permute-done | bytes 163872 | tf_op jit(solution)/shard_map/ppermute | solution.py:24
  16.8 0.0 collective-permute-done.4
  16.8 0.9 %collective-permute-done.1.refs_1_ = bf16[128,1280]{1,0:T(8,128)(2,1)S(1)} collective-permute-done((bf16[128,1280]{1,0:T(8,128)(2,1)S(1)}, bf16[128,1280]{1,0:T(8,128)(2,1)S(1)}, u32[]{:S(2)}, u32[]{:S(2)}) %collective-permute-start.1) | collective-permute-done | bytes 327712 | tf_op jit(solution)/shard_map/ppermute | solution.py:24
  17.7 1.5 %collective-permute-start.5 = (bf16[128,1280]{1,0:T(8,128)(2,1)S(1)}, bf16[128,1280]{1,0:T(8,128)(2,1)S(1)}, u32[]{:S(2)}, u32[]{:S(2)}) collective-permute-start(bf16[128,1280]{1,0:T(8,128)(2,1)S(1)} %constant_dynamic-update-slice_fusion.refs_3_), channel_id=1, source_target_pairs={{0,2},{1,17},{2,0},{3,19},{4,6},{5,21},{6,4},{7,23},{8,10},{9,25},... | collective-permute-start | bytes 983048 | tf_op jit(solution)/shard_map/ppermute | solution.py:24
  19.2 0.5 %collective-permute-start.11 = (bf16[64,1280]{1,0:T(8,128)(2,1)S(1)}, bf16[64,1280]{1,0:T(8,128)(2,1)S(1)}, u32[]{:S(2)}, u32[]{:S(2)}) collective-permute-start(bf16[64,1280]{1,0:T(8,128)(2,1)S(1)} %collective-permute-done.refs_0_), channel_id=1, source_target_pairs={{0,1},{1,0},{2,3},{3,2},{4,5},{5,4},{6,7},{7,6},{8,9},{9,8},{10,11... | collective-permute-start | bytes 491528 | tf_op jit(solution)/shard_map/ppermute | solution.py:24
  19.7 1.5 %collective-permute-done.2.refs_2_ = bf16[64,1280]{1,0:T(8,128)(2,1)S(1)} collective-permute-done((bf16[64,1280]{1,0:T(8,128)(2,1)S(1)}, bf16[64,1280]{1,0:T(8,128)(2,1)S(1)}, u32[]{:S(2)}, u32[]{:S(2)}) %collective-permute-start.2) | collective-permute-done | bytes 163872 | tf_op jit(solution)/shard_map/ppermute | solution.py:24
  21.2 0.5 %collective-permute-start.14 = (bf16[128,1280]{1,0:T(8,128)(2,1)S(1)}, bf16[128,1280]{1,0:T(8,128)(2,1)S(1)}, u32[]{:S(2)}, u32[]{:S(2)}) collective-permute-start(bf16[128,1280]{1,0:T(8,128)(2,1)S(1)} %constant_dynamic-update-slice_fusion.refs_3_), channel_id=1, source_target_pairs={{0,1},{1,0},{2,3},{3,2},{4,5},{5,4},{6,7},{7,6},{8,9},{9,8},{10,11... | collective-permute-start | bytes 983048 | tf_op jit(solution)/shard_map/ppermute | solution.py:24
  21.7 0.0 collective-permute-done.21.refs_21_
  21.7 1.3 %collective-permute-start.9 = (bf16[64,1280]{1,0:T(8,128)(2,1)S(1)}, bf16[64,1280]{1,0:T(8,128)(2,1)S(1)}, u32[]{:S(2)}, u32[]{:S(2)}) collective-permute-start(bf16[64,1280]{1,0:T(8,128)(2,1)S(1)} %collective-permute-done.2.refs_2_), channel_id=1, source_target_pairs={{0,16},{1,3},{2,18},{3,1},{4,20},{5,7},{6,22},{7,5},{8,24},{9,11},... | collective-permute-start | bytes 491528 | tf_op jit(solution)/shard_map/ppermute | solution.py:24
  23.0 1.4 %collective-permute-start.8 = (bf16[64,1280]{1,0:T(8,128)(2,1)S(1)}, bf16[64,1280]{1,0:T(8,128)(2,1)S(1)}, u32[]{:S(2)}, u32[]{:S(2)}) collective-permute-start(bf16[64,1280]{1,0:T(8,128)(2,1)S(1)} %collective-permute-done.2.refs_2_), channel_id=1, source_target_pairs={{0,2},{1,17},{2,0},{3,19},{4,6},{5,21},{6,4},{7,23},{8,10},{9,25},... | collective-permute-start | bytes 491528 | tf_op jit(solution)/shard_map/ppermute | solution.py:24
  24.4 0.0 collective-permute-done.13.refs_13_
  24.4 0.9 %collective-permute-start.6 = (bf16[128,1280]{1,0:T(8,128)(2,1)S(1)}, bf16[128,1280]{1,0:T(8,128)(2,1)S(1)}, u32[]{:S(2)}, u32[]{:S(2)}) collective-permute-start(bf16[128,1280]{1,0:T(8,128)(2,1)S(1)} %constant_dynamic-update-slice_fusion.refs_3_), channel_id=1, source_target_pairs={{0,16},{1,3},{2,18},{3,1},{4,20},{5,7},{6,22},{7,5},{8,24},{9,11},... | collective-permute-start | bytes 983048 | tf_op jit(solution)/shard_map/ppermute | solution.py:24
  25.3 0.0 collective-permute-done.5.refs_4_
  25.3 1.5 %collective-permute-start.7 = (bf16[128,1280]{1,0:T(8,128)(2,1)S(1)}, bf16[128,1280]{1,0:T(8,128)(2,1)S(1)}, u32[]{:S(2)}, u32[]{:S(2)}) collective-permute-start(bf16[128,1280]{1,0:T(8,128)(2,1)S(1)} %collective-permute-done.5.refs_4_), channel_id=1, source_target_pairs={{0,16},{1,3},{2,18},{3,1},{4,20},{5,7},{6,22},{7,5},{8,24},{9,11},... | collective-permute-start | bytes 983048 | tf_op jit(solution)/shard_map/ppermute | solution.py:24
  26.8 1.7 %collective-permute-done.9.refs_8_ = bf16[64,1280]{1,0:T(8,128)(2,1)S(1)} collective-permute-done((bf16[64,1280]{1,0:T(8,128)(2,1)S(1)}, bf16[64,1280]{1,0:T(8,128)(2,1)S(1)}, u32[]{:S(2)}, u32[]{:S(2)}) %collective-permute-start.9) | collective-permute-done | bytes 163872 | tf_op jit(solution)/shard_map/ppermute | solution.py:24
  28.5 1.6 %collective-permute-done.8.refs_7_ = bf16[64,1280]{1,0:T(8,128)(2,1)S(1)} collective-permute-done((bf16[64,1280]{1,0:T(8,128)(2,1)S(1)}, bf16[64,1280]{1,0:T(8,128)(2,1)S(1)}, u32[]{:S(2)}, u32[]{:S(2)}) %collective-permute-start.8) | collective-permute-done | bytes 163872 | tf_op jit(solution)/shard_map/ppermute | solution.py:24
  30.2 0.8 %collective-permute-start.10 = (bf16[64,1280]{1,0:T(8,128)(2,1)S(1)}, bf16[64,1280]{1,0:T(8,128)(2,1)S(1)}, u32[]{:S(2)}, u32[]{:S(2)}) collective-permute-start(bf16[64,1280]{1,0:T(8,128)(2,1)S(1)} %collective-permute-done.8.refs_7_), channel_id=1, source_target_pairs={{0,16},{1,3},{2,18},{3,1},{4,20},{5,7},{6,22},{7,5},{8,24},{9,11},... | collective-permute-start | bytes 491528 | tf_op jit(solution)/shard_map/ppermute | solution.py:24
  30.9 0.0 collective-permute-done.19.refs_19_
  30.9 0.9 %collective-permute-start.12 = (bf16[128,1280]{1,0:T(8,128)(2,1)S(1)}, bf16[128,1280]{1,0:T(8,128)(2,1)S(1)}, u32[]{:S(2)}, u32[]{:S(2)}) collective-permute-start(bf16[128,1280]{1,0:T(8,128)(2,1)S(1)} %collective-permute-done.1.refs_1_), channel_id=1, source_target_pairs={{0,1},{1,0},{2,3},{3,2},{4,5},{5,4},{6,7},{7,6},{8,9},{9,8},{10,11... | collective-permute-start | bytes 983048 | tf_op jit(solution)/shard_map/ppermute | solution.py:24
  31.8 0.1 collective-permute-start.15
  31.9 0.5 collective-permute-done.6.refs_5_
  32.3 0.0 collective-permute-start.16
  32.3 3.5 %collective-permute-done.7.refs_6_ = bf16[128,1280]{1,0:T(8,128)(2,1)S(1)} collective-permute-done((bf16[128,1280]{1,0:T(8,128)(2,1)S(1)}, bf16[128,1280]{1,0:T(8,128)(2,1)S(1)}, u32[]{:S(2)}, u32[]{:S(2)}) %collective-permute-start.7) | collective-permute-done | bytes 327712 | tf_op jit(solution)/shard_map/ppermute | solution.py:24
  35.8 1.8 %collective-permute-done.10.refs_9_ = bf16[64,1280]{1,0:T(8,128)(2,1)S(1)} collective-permute-done((bf16[64,1280]{1,0:T(8,128)(2,1)S(1)}, bf16[64,1280]{1,0:T(8,128)(2,1)S(1)}, u32[]{:S(2)}, u32[]{:S(2)}) %collective-permute-start.10) | collective-permute-done | bytes 163872 | tf_op jit(solution)/shard_map/ppermute | solution.py:24
  37.6 1.4 %collective-permute-done.20.refs_20_ = bf16[64,1280]{1,0:T(8,128)(2,1)S(1)} collective-permute-done((bf16[64,1280]{1,0:T(8,128)(2,1)S(1)}, bf16[64,1280]{1,0:T(8,128)(2,1)S(1)}, u32[]{:S(2)}, u32[]{:S(2)}) %collective-permute-start.20) | collective-permute-done | bytes 163872 | tf_op jit(solution)/shard_map/ppermute | solution.py:24
  39.0 10.5 %shard_map.29 = f32[64,1216]{1,0:T(8,128)} custom-call(bf16[64,1280]{1,0:T(8,128)(2,1)S(1)} %collective-permute-done.refs_0_, bf16[128,1280]{1,0:T(8,128)(2,1)S(1)} %collective-permute-done.1.refs_1_, bf16[64,1280]{1,0:T(8,128)(2,1)S(1)} %collective-permute-done.2.refs_2_, bf16[128,1280]{1,0:T(8,128)(2,1)S(1)} %constant_dynamic-update-slice_fusion.refs_3_, ...), custom_call_target="tpu_custom_call" | custom-call | tf_op jit(solution)/shard_map/pallas_call | solution.py:253
  (17 shorter events, 0.1 us)
Async XLA Ops:
  1.1 6.6 %collective-permute-start = (bf16[64,1280]{1,0:T(8,128)(2,1)S(1)}, bf16[64,1280]{1,0:T(8,128)(2,1)S(1)}, u32[]{:S(2)}, u32[]{:S(2)}) collective-permute-start(bf16[64,1280]{1,0:T(8,128)(2,1)S(1)} %shard_map.28.refs_10_), channel_id=1, source_target_pairs={{0,2},{1,17},{2,0},{3,19},{4,6},{5,21},{6,4},{7,23},{8,10},{9,25},... | collective-permute-start | bytes 491528 | tf_op jit(solution)/shard_map/ppermute | solution.py:24
  4.1 12.6 %collective-permute-start.4 = (bf16[64,1280]{1,0:T(8,128)(2,1)S(1)}, bf16[64,1280]{1,0:T(8,128)(2,1)S(1)}, u32[]{:S(2)}, u32[]{:S(2)}) collective-permute-start(bf16[64,1280]{1,0:T(8,128)(2,1)S(1)} %shard_map.28.refs_10_), channel_id=1, source_target_pairs={{0,12},{1,13},{2,14},{3,15},{4,0},{5,1},{6,2},{7,3},{8,4},{9,5},{1... | collective-permute-start | bytes 491528 | tf_op jit(solution)/shard_map/ppermute | solution.py:24
  7.7 9.0 %collective-permute-start.3 = (bf16[64,1280]{1,0:T(8,128)(2,1)S(1)}, bf16[64,1280]{1,0:T(8,128)(2,1)S(1)}, u32[]{:S(2)}, u32[]{:S(2)}) collective-permute-start(bf16[64,1280]{1,0:T(8,128)(2,1)S(1)} %shard_map.28.refs_10_), channel_id=1, source_target_pairs={{0,4},{1,5},{2,6},{3,7},{4,8},{5,9},{6,10},{7,11},{8,12},{9,13},{1... | collective-permute-start | bytes 491528 | tf_op jit(solution)/shard_map/ppermute | solution.py:24
  7.7 13.5 %collective-permute-start.2 = (bf16[64,1280]{1,0:T(8,128)(2,1)S(1)}, bf16[64,1280]{1,0:T(8,128)(2,1)S(1)}, u32[]{:S(2)}, u32[]{:S(2)}) collective-permute-start(bf16[64,1280]{1,0:T(8,128)(2,1)S(1)} %shard_map.28.refs_10_), channel_id=1, source_target_pairs={{0,8},{1,9},{2,10},{3,11},{4,12},{5,13},{6,14},{7,15},{8,0},{9,1},... | collective-permute-start | bytes 491528 | tf_op jit(solution)/shard_map/ppermute | solution.py:24
  10.6 7.1 %collective-permute-start.1 = (bf16[128,1280]{1,0:T(8,128)(2,1)S(1)}, bf16[128,1280]{1,0:T(8,128)(2,1)S(1)}, u32[]{:S(2)}, u32[]{:S(2)}) collective-permute-start(bf16[128,1280]{1,0:T(8,128)(2,1)S(1)} %pad_maximum_fusion), channel_id=1, source_target_pairs={{0,16},{1,3},{2,18},{3,1},{4,20},{5,7},{6,22},{7,5},{8,24},{9,11},... | collective-permute-start | bytes 983048 | tf_op jit(solution)/shard_map/ppermute | solution.py:24
  17.7 7.6 %collective-permute-start.5 = (bf16[128,1280]{1,0:T(8,128)(2,1)S(1)}, bf16[128,1280]{1,0:T(8,128)(2,1)S(1)}, u32[]{:S(2)}, u32[]{:S(2)}) collective-permute-start(bf16[128,1280]{1,0:T(8,128)(2,1)S(1)} %constant_dynamic-update-slice_fusion.refs_3_), channel_id=1, source_target_pairs={{0,2},{1,17},{2,0},{3,19},{4,6},{5,21},{6,4},{7,23},{8,10},{9,25},... | collective-permute-start | bytes 983048 | tf_op jit(solution)/shard_map/ppermute | solution.py:24
  19.2 2.5 %collective-permute-start.21 = (bf16[64,1280]{1,0:T(8,128)(2,1)S(1)}, bf16[64,1280]{1,0:T(8,128)(2,1)S(1)}, u32[]{:S(2)}, u32[]{:S(2)}) collective-permute-start(bf16[64,1280]{1,0:T(8,128)(2,1)S(1)} %shard_map.28.refs_10_), channel_id=1, source_target_pairs={{0,1},{1,0},{2,3},{3,2},{4,5},{5,4},{6,7},{7,6},{8,9},{9,8},{10,11... | collective-permute-start | bytes 491528 | tf_op jit(solution)/shard_map/ppermute | solution.py:24
  19.2 3.8 %collective-permute-start.11 = (bf16[64,1280]{1,0:T(8,128)(2,1)S(1)}, bf16[64,1280]{1,0:T(8,128)(2,1)S(1)}, u32[]{:S(2)}, u32[]{:S(2)}) collective-permute-start(bf16[64,1280]{1,0:T(8,128)(2,1)S(1)} %collective-permute-done.refs_0_), channel_id=1, source_target_pairs={{0,1},{1,0},{2,3},{3,2},{4,5},{5,4},{6,7},{7,6},{8,9},{9,8},{10,11... | collective-permute-start | bytes 491528 | tf_op jit(solution)/shard_map/ppermute | solution.py:24
  21.2 3.2 %collective-permute-start.13 = (bf16[64,1280]{1,0:T(8,128)(2,1)S(1)}, bf16[64,1280]{1,0:T(8,128)(2,1)S(1)}, u32[]{:S(2)}, u32[]{:S(2)}) collective-permute-start(bf16[64,1280]{1,0:T(8,128)(2,1)S(1)} %collective-permute-done.2.refs_2_), channel_id=1, source_target_pairs={{0,1},{1,0},{2,3},{3,2},{4,5},{5,4},{6,7},{7,6},{8,9},{9,8},{10,11... | collective-permute-start | bytes 491528 | tf_op jit(solution)/shard_map/ppermute | solution.py:24
  21.2 8.9 %collective-permute-start.14 = (bf16[128,1280]{1,0:T(8,128)(2,1)S(1)}, bf16[128,1280]{1,0:T(8,128)(2,1)S(1)}, u32[]{:S(2)}, u32[]{:S(2)}) collective-permute-start(bf16[128,1280]{1,0:T(8,128)(2,1)S(1)} %constant_dynamic-update-slice_fusion.refs_3_), channel_id=1, source_target_pairs={{0,1},{1,0},{2,3},{3,2},{4,5},{5,4},{6,7},{7,6},{8,9},{9,8},{10,11... | collective-permute-start | bytes 983048 | tf_op jit(solution)/shard_map/ppermute | solution.py:24
  21.7 6.8 %collective-permute-start.9 = (bf16[64,1280]{1,0:T(8,128)(2,1)S(1)}, bf16[64,1280]{1,0:T(8,128)(2,1)S(1)}, u32[]{:S(2)}, u32[]{:S(2)}) collective-permute-start(bf16[64,1280]{1,0:T(8,128)(2,1)S(1)} %collective-permute-done.2.refs_2_), channel_id=1, source_target_pairs={{0,16},{1,3},{2,18},{3,1},{4,20},{5,7},{6,22},{7,5},{8,24},{9,11},... | collective-permute-start | bytes 491528 | tf_op jit(solution)/shard_map/ppermute | solution.py:24
  23.0 7.1 %collective-permute-start.8 = (bf16[64,1280]{1,0:T(8,128)(2,1)S(1)}, bf16[64,1280]{1,0:T(8,128)(2,1)S(1)}, u32[]{:S(2)}, u32[]{:S(2)}) collective-permute-start(bf16[64,1280]{1,0:T(8,128)(2,1)S(1)} %collective-permute-done.2.refs_2_), channel_id=1, source_target_pairs={{0,2},{1,17},{2,0},{3,19},{4,6},{5,21},{6,4},{7,23},{8,10},{9,25},... | collective-permute-start | bytes 491528 | tf_op jit(solution)/shard_map/ppermute | solution.py:24
  24.4 7.9 %collective-permute-start.6 = (bf16[128,1280]{1,0:T(8,128)(2,1)S(1)}, bf16[128,1280]{1,0:T(8,128)(2,1)S(1)}, u32[]{:S(2)}, u32[]{:S(2)}) collective-permute-start(bf16[128,1280]{1,0:T(8,128)(2,1)S(1)} %constant_dynamic-update-slice_fusion.refs_3_), channel_id=1, source_target_pairs={{0,16},{1,3},{2,18},{3,1},{4,20},{5,7},{6,22},{7,5},{8,24},{9,11},... | collective-permute-start | bytes 983048 | tf_op jit(solution)/shard_map/ppermute | solution.py:24
  25.3 10.5 %collective-permute-start.7 = (bf16[128,1280]{1,0:T(8,128)(2,1)S(1)}, bf16[128,1280]{1,0:T(8,128)(2,1)S(1)}, u32[]{:S(2)}, u32[]{:S(2)}) collective-permute-start(bf16[128,1280]{1,0:T(8,128)(2,1)S(1)} %collective-permute-done.5.refs_4_), channel_id=1, source_target_pairs={{0,16},{1,3},{2,18},{3,1},{4,20},{5,7},{6,22},{7,5},{8,24},{9,11},... | collective-permute-start | bytes 983048 | tf_op jit(solution)/shard_map/ppermute | solution.py:24
  28.5 2.4 %collective-permute-start.19 = (bf16[64,1280]{1,0:T(8,128)(2,1)S(1)}, bf16[64,1280]{1,0:T(8,128)(2,1)S(1)}, u32[]{:S(2)}, u32[]{:S(2)}) collective-permute-start(bf16[64,1280]{1,0:T(8,128)(2,1)S(1)} %collective-permute-done.9.refs_8_), channel_id=1, source_target_pairs={{0,1},{1,0},{2,3},{3,2},{4,5},{5,4},{6,7},{7,6},{8,9},{9,8},{10,11... | collective-permute-start | bytes 491528 | tf_op jit(solution)/shard_map/ppermute | solution.py:24
  30.2 1.6 %collective-permute-start.18 = (bf16[64,1280]{1,0:T(8,128)(2,1)S(1)}, bf16[64,1280]{1,0:T(8,128)(2,1)S(1)}, u32[]{:S(2)}, u32[]{:S(2)}) collective-permute-start(bf16[64,1280]{1,0:T(8,128)(2,1)S(1)} %collective-permute-done.8.refs_7_), channel_id=1, source_target_pairs={{0,1},{1,0},{2,3},{3,2},{4,5},{5,4},{6,7},{7,6},{8,9},{9,8},{10,11... | collective-permute-start | bytes 491528 | tf_op jit(solution)/shard_map/ppermute | solution.py:24
  30.2 7.4 %collective-permute-start.10 = (bf16[64,1280]{1,0:T(8,128)(2,1)S(1)}, bf16[64,1280]{1,0:T(8,128)(2,1)S(1)}, u32[]{:S(2)}, u32[]{:S(2)}) collective-permute-start(bf16[64,1280]{1,0:T(8,128)(2,1)S(1)} %collective-permute-done.8.refs_7_), channel_id=1, source_target_pairs={{0,16},{1,3},{2,18},{3,1},{4,20},{5,7},{6,22},{7,5},{8,24},{9,11},... | collective-permute-start | bytes 491528 | tf_op jit(solution)/shard_map/ppermute | solution.py:24
  30.9 8.1 %collective-permute-start.12 = (bf16[128,1280]{1,0:T(8,128)(2,1)S(1)}, bf16[128,1280]{1,0:T(8,128)(2,1)S(1)}, u32[]{:S(2)}, u32[]{:S(2)}) collective-permute-start(bf16[128,1280]{1,0:T(8,128)(2,1)S(1)} %collective-permute-done.1.refs_1_), channel_id=1, source_target_pairs={{0,1},{1,0},{2,3},{3,2},{4,5},{5,4},{6,7},{7,6},{8,9},{9,8},{10,11... | collective-permute-start | bytes 983048 | tf_op jit(solution)/shard_map/ppermute | solution.py:24
  31.8 7.2 %collective-permute-start.15 = (bf16[128,1280]{1,0:T(8,128)(2,1)S(1)}, bf16[128,1280]{1,0:T(8,128)(2,1)S(1)}, u32[]{:S(2)}, u32[]{:S(2)}) collective-permute-start(bf16[128,1280]{1,0:T(8,128)(2,1)S(1)} %collective-permute-done.5.refs_4_), channel_id=1, source_target_pairs={{0,1},{1,0},{2,3},{3,2},{4,5},{5,4},{6,7},{7,6},{8,9},{9,8},{10,11... | collective-permute-start | bytes 983048 | tf_op jit(solution)/shard_map/ppermute | solution.py:24
  32.3 6.7 %collective-permute-start.16 = (bf16[128,1280]{1,0:T(8,128)(2,1)S(1)}, bf16[128,1280]{1,0:T(8,128)(2,1)S(1)}, u32[]{:S(2)}, u32[]{:S(2)}) collective-permute-start(bf16[128,1280]{1,0:T(8,128)(2,1)S(1)} %collective-permute-done.6.refs_5_), channel_id=1, source_target_pairs={{0,1},{1,0},{2,3},{3,2},{4,5},{5,4},{6,7},{7,6},{8,9},{9,8},{10,11... | collective-permute-start | bytes 983048 | tf_op jit(solution)/shard_map/ppermute | solution.py:24
  35.8 3.2 %collective-permute-start.17 = (bf16[128,1280]{1,0:T(8,128)(2,1)S(1)}, bf16[128,1280]{1,0:T(8,128)(2,1)S(1)}, u32[]{:S(2)}, u32[]{:S(2)}) collective-permute-start(bf16[128,1280]{1,0:T(8,128)(2,1)S(1)} %collective-permute-done.7.refs_6_), channel_id=1, source_target_pairs={{0,1},{1,0},{2,3},{3,2},{4,5},{5,4},{6,7},{7,6},{8,9},{9,8},{10,11... | collective-permute-start | bytes 983048 | tf_op jit(solution)/shard_map/ppermute | solution.py:24
  37.6 1.4 %collective-permute-start.20 = (bf16[64,1280]{1,0:T(8,128)(2,1)S(1)}, bf16[64,1280]{1,0:T(8,128)(2,1)S(1)}, u32[]{:S(2)}, u32[]{:S(2)}) collective-permute-start(bf16[64,1280]{1,0:T(8,128)(2,1)S(1)} %collective-permute-done.10.refs_9_), channel_id=1, source_target_pairs={{0,1},{1,0},{2,3},{3,2},{4,5},{5,4},{6,7},{7,6},{8,9},{9,8},{10,11... | collective-permute-start | bytes 491528 | tf_op jit(solution)/shard_map/ppermute | solution.py:24

commit v5 on v4

--- a/solution.py
+++ b/solution.py
@@ -50,15 +50,15 @@
     next_near = along_z(row, count, 3)
     second = flip_second(join(row, first), count)
     far = along_z(after(row, first), count, 2)
+    far_last = along_z(second[second.shape[0] // 2 :], count, 2)
     pair = join(near, next_near)
-    pair_first = flip_first(after(pair, second), count)
+    pair_first = flip_first(pair, count)
     pair_second = flip_second(after(pair, second), count)
     pair_last = flip_second(pair_first, count)
     far_first = flip_first(far, count)
     far_second = flip_second(far, count)
-    far_last = flip_second(far_first, count)
     pieces = [first, second, far, pair, pair_first, pair_second, pair_last, far_first, far_second, far_last, row]
-    return pieces + [flip_core(piece, count) for piece in pieces]
+    return pieces + [flip_core(after(piece, far_last) if piece is pair_first else piece, count) for piece in pieces]
 
 
 def prepare_kernel(density_ref, pattern_ref, row_ref):

time: 49.7 us -> 48.6 us (0.978)
  starting transfers between devices: 20.3 us -> 19.2 us
    ppermute x22, starting transfers between devices: 20.3 us -> 19.2 us  [send(): lax.ppermute(value, AXES, [(s, t) for s, t in pairs if 0 <= t < count])]
  transfers between devices with their start and end apart: 22 -> 22, of which waited for: 9 -> 6; matrix products, arithmetic and copies ran while one was open for 0% -> 0% of each run, Pallas kernels for 0% -> 0%
where the time goes in v5:
time: 48.6 us; the launch traced here: 48.4 us
  starting transfers between devices  19.2 us (40%)
  waiting for transfers between devices  17.5 us (36%)
  Pallas kernels  11.7 us (24%)
    ppermute x22, starting transfers between devices, send(): lax.ppermute(value, AXES, [(s, t) for s, t in pairs if 0 <= t < count])  19.2 us
    ppermute x22, waiting for transfers between devices, send(): lax.ppermute(value, AXES, [(s, t) for s, t in pairs if 0 <= t < count])  17.5 us
    pallas_call x1, Pallas kernels, local(): pl.pallas_call(kernel, out_shape=jax.ShapeDtypeStruct((block, width), jnp...  10.6 us
    pallas_call x1, Pallas kernels, local(): pl.pallas_call(prepare_kernel, out_shape=pltpu.VMEM((block, width + block...  1.1 us
  transfers between devices with their start and end apart: 22, of which 6 were waited for; matrix products, arithmetic and copies ran while one was open for 0% of the time, Pallas kernels for 0%

profile of v5, /device:TPU:0, one launch (start us, length us, event | category | flops | bytes accessed | tf_op | source)
XLA Modules:
  0.0 48.4 jit_solution(6682290449478653138)
XLA Ops:
  0.0 1.1 %shard_map.28.refs_10_ = bf16[64,1280]{1,0:T(8,128)(2,1)S(1)} custom-call(f32[64,1216]{1,0:T(8,128)} %density_ref.1, s32[1,19]{1,0:T(1,128)} %pattern_ref.1), custom_call_target="tpu_custom_call" | custom-call | tf_op jit(solution)/shard_map/pallas_call | solution.py:232
  1.1 3.0 %collective-permute-start = (bf16[64,1280]{1,0:T(8,128)(2,1)S(1)}, bf16[64,1280]{1,0:T(8,128)(2,1)S(1)}, u32[]{:S(2)}, u32[]{:S(2)}) collective-permute-start(bf16[64,1280]{1,0:T(8,128)(2,1)S(1)} %shard_map.28.refs_10_), channel_id=1, source_target_pairs={{0,2},{1,17},{2,0},{3,19},{4,6},{5,21},{6,4},{7,23},{8,10},{9,25},... | collective-permute-start | bytes 491528 | tf_op jit(solution)/shard_map/ppermute | solution.py:24
  4.1 3.6 %collective-permute-start.4 = (bf16[64,1280]{1,0:T(8,128)(2,1)S(1)}, bf16[64,1280]{1,0:T(8,128)(2,1)S(1)}, u32[]{:S(2)}, u32[]{:S(2)}) collective-permute-start(bf16[64,1280]{1,0:T(8,128)(2,1)S(1)} %shard_map.28.refs_10_), channel_id=1, source_target_pairs={{0,12},{1,13},{2,14},{3,15},{4,0},{5,1},{6,2},{7,3},{8,4},{9,5},{1... | collective-permute-start | bytes 491528 | tf_op jit(solution)/shard_map/ppermute | solution.py:24
  7.7 0.0 collective-permute-start.3
  7.7 0.0 collective-permute-done.refs_0_
  7.7 2.8 %collective-permute-start.2 = (bf16[64,1280]{1,0:T(8,128)(2,1)S(1)}, bf16[64,1280]{1,0:T(8,128)(2,1)S(1)}, u32[]{:S(2)}, u32[]{:S(2)}) collective-permute-start(bf16[64,1280]{1,0:T(8,128)(2,1)S(1)} %shard_map.28.refs_10_), channel_id=1, source_target_pairs={{0,8},{1,9},{2,10},{3,11},{4,12},{5,13},{6,14},{7,15},{8,0},{9,1},... | collective-permute-start | bytes 491528 | tf_op jit(solution)/shard_map/ppermute | solution.py:24
  10.6 1.6 %collective-permute-start.1 = (bf16[128,1280]{1,0:T(8,128)(2,1)S(1)}, bf16[128,1280]{1,0:T(8,128)(2,1)S(1)}, u32[]{:S(2)}, u32[]{:S(2)}) collective-permute-start(bf16[128,1280]{1,0:T(8,128)(2,1)S(1)} %pad_maximum_fusion), channel_id=1, source_target_pairs={{0,16},{1,3},{2,18},{3,1},{4,20},{5,7},{6,22},{7,5},{8,24},{9,11},... | collective-permute-start | bytes 983048 | tf_op jit(solution)/shard_map/ppermute | solution.py:24
  12.1 4.6 %collective-permute-done.3 = bf16[64,1280]{1,0:T(8,128)(2,1)S(1)} collective-permute-done((bf16[64,1280]{1,0:T(8,128)(2,1)S(1)}, bf16[64,1280]{1,0:T(8,128)(2,1)S(1)}, u32[]{:S(2)}, u32[]{:S(2)}) %collective-permute-start.3) | collective-permute-done | bytes 163872 | tf_op jit(solution)/shard_map/ppermute | solution.py:24
  16.8 0.5 %collective-permute-start.5 = (bf16[128,1280]{1,0:T(8,128)(2,1)S(1)}, bf16[128,1280]{1,0:T(8,128)(2,1)S(1)}, u32[]{:S(2)}, u32[]{:S(2)}) collective-permute-start(bf16[128,1280]{1,0:T(8,128)(2,1)S(1)} %constant_dynamic-update-slice_fusion.refs_3_), channel_id=1, source_target_pairs={{0,2},{1,17},{2,0},{3,19},{4,6},{5,21},{6,4},{7,23},{8,10},{9,25},... | collective-permute-start | bytes 983048 | tf_op jit(solution)/shard_map/ppermute | solution.py:24
  17.3 0.0 collective-permute-start.21
  17.3 0.5 %collective-permute-start.11 = (bf16[64,1280]{1,0:T(8,128)(2,1)S(1)}, bf16[64,1280]{1,0:T(8,128)(2,1)S(1)}, u32[]{:S(2)}, u32[]{:S(2)}) collective-permute-start(bf16[64,1280]{1,0:T(8,128)(2,1)S(1)} %collective-permute-done.refs_0_), channel_id=1, source_target_pairs={{0,1},{1,0},{2,3},{3,2},{4,5},{5,4},{6,7},{7,6},{8,9},{9,8},{10,11... | collective-permute-start | bytes 491528 | tf_op jit(solution)/shard_map/ppermute | solution.py:24
  17.8 3.4 %collective-permute-done.2.refs_2_ = bf16[64,1280]{1,0:T(8,128)(2,1)S(1)} collective-permute-done((bf16[64,1280]{1,0:T(8,128)(2,1)S(1)}, bf16[64,1280]{1,0:T(8,128)(2,1)S(1)}, u32[]{:S(2)}, u32[]{:S(2)}) %collective-permute-start.2) | collective-permute-done | bytes 163872 | tf_op jit(solution)/shard_map/ppermute | solution.py:24
  21.2 0.0 collective-permute-start.13
  21.2 1.3 %collective-permute-start.9 = (bf16[64,1280]{1,0:T(8,128)(2,1)S(1)}, bf16[64,1280]{1,0:T(8,128)(2,1)S(1)}, u32[]{:S(2)}, u32[]{:S(2)}) collective-permute-start(bf16[64,1280]{1,0:T(8,128)(2,1)S(1)} %collective-permute-done.2.refs_2_), channel_id=1, source_target_pairs={{0,16},{1,3},{2,18},{3,1},{4,20},{5,7},{6,22},{7,5},{8,24},{9,11},... | collective-permute-start | bytes 491528 | tf_op jit(solution)/shard_map/ppermute | solution.py:24
  22.5 0.5 %collective-permute-start.14 = (bf16[128,1280]{1,0:T(8,128)(2,1)S(1)}, bf16[128,1280]{1,0:T(8,128)(2,1)S(1)}, u32[]{:S(2)}, u32[]{:S(2)}) collective-permute-start(bf16[128,1280]{1,0:T(8,128)(2,1)S(1)} %constant_dynamic-update-slice_fusion.refs_3_), channel_id=1, source_target_pairs={{0,1},{1,0},{2,3},{3,2},{4,5},{5,4},{6,7},{7,6},{8,9},{9,8},{10,11... | collective-permute-start | bytes 983048 | tf_op jit(solution)/shard_map/ppermute | solution.py:24
  23.1 0.1 collective-permute-start.10
  23.2 1.1 %collective-permute-start.6 = (bf16[128,1280]{1,0:T(8,128)(2,1)S(1)}, bf16[128,1280]{1,0:T(8,128)(2,1)S(1)}, u32[]{:S(2)}, u32[]{:S(2)}) collective-permute-start(bf16[128,1280]{1,0:T(8,128)(2,1)S(1)} %constant_dynamic-update-slice_fusion.refs_3_), channel_id=1, source_target_pairs={{0,16},{1,3},{2,18},{3,1},{4,20},{5,7},{6,22},{7,5},{8,24},{9,11},... | collective-permute-start | bytes 983048 | tf_op jit(solution)/shard_map/ppermute | solution.py:24
  24.3 1.1 %collective-permute-start.7 = (bf16[128,1280]{1,0:T(8,128)(2,1)S(1)}, bf16[128,1280]{1,0:T(8,128)(2,1)S(1)}, u32[]{:S(2)}, u32[]{:S(2)}) collective-permute-start(bf16[128,1280]{1,0:T(8,128)(2,1)S(1)} %collective-permute-done.5.refs_4_), channel_id=1, source_target_pairs={{0,16},{1,3},{2,18},{3,1},{4,20},{5,7},{6,22},{7,5},{8,24},{9,11},... | collective-permute-start | bytes 983048 | tf_op jit(solution)/shard_map/ppermute | solution.py:24
  25.4 1.2 %collective-permute-done.9.refs_8_ = bf16[64,1280]{1,0:T(8,128)(2,1)S(1)} collective-permute-done((bf16[64,1280]{1,0:T(8,128)(2,1)S(1)}, bf16[64,1280]{1,0:T(8,128)(2,1)S(1)}, u32[]{:S(2)}, u32[]{:S(2)}) %collective-permute-start.9) | collective-permute-done | bytes 163872 | tf_op jit(solution)/shard_map/ppermute | solution.py:24
  26.6 1.5 %collective-permute-start.8 = (bf16[64,1280]{1,0:T(8,128)(2,1)S(1)}, bf16[64,1280]{1,0:T(8,128)(2,1)S(1)}, u32[]{:S(2)}, u32[]{:S(2)}) collective-permute-start(bf16[64,1280]{1,0:T(8,128)(2,1)S(1)} %collective-permute-done.2.refs_2_), channel_id=1, source_target_pairs={{0,2},{1,17},{2,0},{3,19},{4,6},{5,21},{6,4},{7,23},{8,10},{9,25},... | collective-permute-start | bytes 491528 | tf_op jit(solution)/shard_map/ppermute | solution.py:24
  28.1 5.6 %collective-permute-done.10.refs_9_ = bf16[64,1280]{1,0:T(8,128)(2,1)S(1)} collective-permute-done((bf16[64,1280]{1,0:T(8,128)(2,1)S(1)}, bf16[64,1280]{1,0:T(8,128)(2,1)S(1)}, u32[]{:S(2)}, u32[]{:S(2)}) %collective-permute-start.10) | collective-permute-done | bytes 163872 | tf_op jit(solution)/shard_map/ppermute | solution.py:24
  33.7 0.0 collective-permute-done.8.refs_7_
  33.7 0.5 %collective-permute-start.12 = (bf16[128,1280]{1,0:T(8,128)(2,1)S(1)}, bf16[128,1280]{1,0:T(8,128)(2,1)S(1)}, u32[]{:S(2)}, u32[]{:S(2)}) collective-permute-start(bf16[128,1280]{1,0:T(8,128)(2,1)S(1)} %collective-permute-done.1.refs_1_), channel_id=1, source_target_pairs={{0,1},{1,0},{2,3},{3,2},{4,5},{5,4},{6,7},{7,6},{8,9},{9,8},{10,11... | collective-permute-start | bytes 983048 | tf_op jit(solution)/shard_map/ppermute | solution.py:24
  34.2 0.1 collective-permute-start.18
  34.3 0.8 %collective-permute-done.19.refs_19_ = bf16[64,1280]{1,0:T(8,128)(2,1)S(1)} collective-permute-done((bf16[64,1280]{1,0:T(8,128)(2,1)S(1)}, bf16[64,1280]{1,0:T(8,128)(2,1)S(1)}, u32[]{:S(2)}, u32[]{:S(2)}) %collective-permute-start.19) | collective-permute-done | bytes 163872 | tf_op jit(solution)/shard_map/ppermute | solution.py:24
  35.1 0.1 collective-permute-start.15
  35.2 0.4 collective-permute-start.16
  35.6 0.1 collective-permute-start.17
  35.7 0.0 collective-permute-done.18.refs_18_
  35.8 0.3 collective-permute-start.20
  36.1 1.8 %collective-permute-done.20.refs_20_ = bf16[64,1280]{1,0:T(8,128)(2,1)S(1)} collective-permute-done((bf16[64,1280]{1,0:T(8,128)(2,1)S(1)}, bf16[64,1280]{1,0:T(8,128)(2,1)S(1)}, u32[]{:S(2)}, u32[]{:S(2)}) %collective-permute-start.20) | collective-permute-done | bytes 163872 | tf_op jit(solution)/shard_map/ppermute | solution.py:24
  37.9 10.6 %shard_map.29 = f32[64,1216]{1,0:T(8,128)} custom-call(bf16[64,1280]{1,0:T(8,128)(2,1)S(1)} %collective-permute-done.refs_0_, bf16[128,1280]{1,0:T(8,128)(2,1)S(1)} %collective-permute-done.1.refs_1_, bf16[64,1280]{1,0:T(8,128)(2,1)S(1)} %collective-permute-done.2.refs_2_, bf16[128,1280]{1,0:T(8,128)(2,1)S(1)} %constant_dynamic-update-slice_fusion.refs_3_, ...), custom_call_target="tpu_custom_call" | custom-call | tf_op jit(solution)/shard_map/pallas_call | solution.py:253
  (18 shorter events, 0.1 us)
Async XLA Ops:
  1.1 6.6 %collective-permute-start = (bf16[64,1280]{1,0:T(8,128)(2,1)S(1)}, bf16[64,1280]{1,0:T(8,128)(2,1)S(1)}, u32[]{:S(2)}, u32[]{:S(2)}) collective-permute-start(bf16[64,1280]{1,0:T(8,128)(2,1)S(1)} %shard_map.28.refs_10_), channel_id=1, source_target_pairs={{0,2},{1,17},{2,0},{3,19},{4,6},{5,21},{6,4},{7,23},{8,10},{9,25},... | collective-permute-start | bytes 491528 | tf_op jit(solution)/shard_map/ppermute | solution.py:24
  4.1 12.6 %collective-permute-start.4 = (bf16[64,1280]{1,0:T(8,128)(2,1)S(1)}, bf16[64,1280]{1,0:T(8,128)(2,1)S(1)}, u32[]{:S(2)}, u32[]{:S(2)}) collective-permute-start(bf16[64,1280]{1,0:T(8,128)(2,1)S(1)} %shard_map.28.refs_10_), channel_id=1, source_target_pairs={{0,12},{1,13},{2,14},{3,15},{4,0},{5,1},{6,2},{7,3},{8,4},{9,5},{1... | collective-permute-start | bytes 491528 | tf_op jit(solution)/shard_map/ppermute | solution.py:24
  7.7 9.0 %collective-permute-start.3 = (bf16[64,1280]{1,0:T(8,128)(2,1)S(1)}, bf16[64,1280]{1,0:T(8,128)(2,1)S(1)}, u32[]{:S(2)}, u32[]{:S(2)}) collective-permute-start(bf16[64,1280]{1,0:T(8,128)(2,1)S(1)} %shard_map.28.refs_10_), channel_id=1, source_target_pairs={{0,4},{1,5},{2,6},{3,7},{4,8},{5,9},{6,10},{7,11},{8,12},{9,13},{1... | collective-permute-start | bytes 491528 | tf_op jit(solution)/shard_map/ppermute | solution.py:24
  7.7 13.5 %collective-permute-start.2 = (bf16[64,1280]{1,0:T(8,128)(2,1)S(1)}, bf16[64,1280]{1,0:T(8,128)(2,1)S(1)}, u32[]{:S(2)}, u32[]{:S(2)}) collective-permute-start(bf16[64,1280]{1,0:T(8,128)(2,1)S(1)} %shard_map.28.refs_10_), channel_id=1, source_target_pairs={{0,8},{1,9},{2,10},{3,11},{4,12},{5,13},{6,14},{7,15},{8,0},{9,1},... | collective-permute-start | bytes 491528 | tf_op jit(solution)/shard_map/ppermute | solution.py:24
  10.6 10.7 %collective-permute-start.1 = (bf16[128,1280]{1,0:T(8,128)(2,1)S(1)}, bf16[128,1280]{1,0:T(8,128)(2,1)S(1)}, u32[]{:S(2)}, u32[]{:S(2)}) collective-permute-start(bf16[128,1280]{1,0:T(8,128)(2,1)S(1)} %pad_maximum_fusion), channel_id=1, source_target_pairs={{0,16},{1,3},{2,18},{3,1},{4,20},{5,7},{6,22},{7,5},{8,24},{9,11},... | collective-permute-start | bytes 983048 | tf_op jit(solution)/shard_map/ppermute | solution.py:24
  16.8 7.5 %collective-permute-start.5 = (bf16[128,1280]{1,0:T(8,128)(2,1)S(1)}, bf16[128,1280]{1,0:T(8,128)(2,1)S(1)}, u32[]{:S(2)}, u32[]{:S(2)}) collective-permute-start(bf16[128,1280]{1,0:T(8,128)(2,1)S(1)} %constant_dynamic-update-slice_fusion.refs_3_), channel_id=1, source_target_pairs={{0,2},{1,17},{2,0},{3,19},{4,6},{5,21},{6,4},{7,23},{8,10},{9,25},... | collective-permute-start | bytes 983048 | tf_op jit(solution)/shard_map/ppermute | solution.py:24
  17.3 5.2 %collective-permute-start.21 = (bf16[64,1280]{1,0:T(8,128)(2,1)S(1)}, bf16[64,1280]{1,0:T(8,128)(2,1)S(1)}, u32[]{:S(2)}, u32[]{:S(2)}) collective-permute-start(bf16[64,1280]{1,0:T(8,128)(2,1)S(1)} %shard_map.28.refs_10_), channel_id=1, source_target_pairs={{0,1},{1,0},{2,3},{3,2},{4,5},{5,4},{6,7},{7,6},{8,9},{9,8},{10,11... | collective-permute-start | bytes 491528 | tf_op jit(solution)/shard_map/ppermute | solution.py:24
  17.3 5.8 %collective-permute-start.11 = (bf16[64,1280]{1,0:T(8,128)(2,1)S(1)}, bf16[64,1280]{1,0:T(8,128)(2,1)S(1)}, u32[]{:S(2)}, u32[]{:S(2)}) collective-permute-start(bf16[64,1280]{1,0:T(8,128)(2,1)S(1)} %collective-permute-done.refs_0_), channel_id=1, source_target_pairs={{0,1},{1,0},{2,3},{3,2},{4,5},{5,4},{6,7},{7,6},{8,9},{9,8},{10,11... | collective-permute-start | bytes 491528 | tf_op jit(solution)/shard_map/ppermute | solution.py:24
  21.2 2.0 %collective-permute-start.13 = (bf16[64,1280]{1,0:T(8,128)(2,1)S(1)}, bf16[64,1280]{1,0:T(8,128)(2,1)S(1)}, u32[]{:S(2)}, u32[]{:S(2)}) collective-permute-start(bf16[64,1280]{1,0:T(8,128)(2,1)S(1)} %collective-permute-done.2.refs_2_), channel_id=1, source_target_pairs={{0,1},{1,0},{2,3},{3,2},{4,5},{5,4},{6,7},{7,6},{8,9},{9,8},{10,11... | collective-permute-start | bytes 491528 | tf_op jit(solution)/shard_map/ppermute | solution.py:24
  21.2 5.3 %collective-permute-start.9 = (bf16[64,1280]{1,0:T(8,128)(2,1)S(1)}, bf16[64,1280]{1,0:T(8,128)(2,1)S(1)}, u32[]{:S(2)}, u32[]{:S(2)}) collective-permute-start(bf16[64,1280]{1,0:T(8,128)(2,1)S(1)} %collective-permute-done.2.refs_2_), channel_id=1, source_target_pairs={{0,16},{1,3},{2,18},{3,1},{4,20},{5,7},{6,22},{7,5},{8,24},{9,11},... | collective-permute-start | bytes 491528 | tf_op jit(solution)/shard_map/ppermute | solution.py:24
  22.5 11.7 %collective-permute-start.14 = (bf16[128,1280]{1,0:T(8,128)(2,1)S(1)}, bf16[128,1280]{1,0:T(8,128)(2,1)S(1)}, u32[]{:S(2)}, u32[]{:S(2)}) collective-permute-start(bf16[128,1280]{1,0:T(8,128)(2,1)S(1)} %constant_dynamic-update-slice_fusion.refs_3_), channel_id=1, source_target_pairs={{0,1},{1,0},{2,3},{3,2},{4,5},{5,4},{6,7},{7,6},{8,9},{9,8},{10,11... | collective-permute-start | bytes 983048 | tf_op jit(solution)/shard_map/ppermute | solution.py:24
  23.1 10.6 %collective-permute-start.10 = (bf16[64,1280]{1,0:T(8,128)(2,1)S(1)}, bf16[64,1280]{1,0:T(8,128)(2,1)S(1)}, u32[]{:S(2)}, u32[]{:S(2)}) collective-permute-start(bf16[64,1280]{1,0:T(8,128)(2,1)S(1)} %slice.4), channel_id=1, source_target_pairs={{0,8},{1,9},{2,10},{3,11},{4,12},{5,13},{6,14},{7,15},{8,0},{9,1},... | collective-permute-start | bytes 491528 | tf_op jit(solution)/shard_map/ppermute | solution.py:24
  23.2 12.0 %collective-permute-start.6 = (bf16[128,1280]{1,0:T(8,128)(2,1)S(1)}, bf16[128,1280]{1,0:T(8,128)(2,1)S(1)}, u32[]{:S(2)}, u32[]{:S(2)}) collective-permute-start(bf16[128,1280]{1,0:T(8,128)(2,1)S(1)} %constant_dynamic-update-slice_fusion.refs_3_), channel_id=1, source_target_pairs={{0,16},{1,3},{2,18},{3,1},{4,20},{5,7},{6,22},{7,5},{8,24},{9,11},... | collective-permute-start | bytes 983048 | tf_op jit(solution)/shard_map/ppermute | solution.py:24
  24.3 11.3 %collective-permute-start.7 = (bf16[128,1280]{1,0:T(8,128)(2,1)S(1)}, bf16[128,1280]{1,0:T(8,128)(2,1)S(1)}, u32[]{:S(2)}, u32[]{:S(2)}) collective-permute-start(bf16[128,1280]{1,0:T(8,128)(2,1)S(1)} %collective-permute-done.5.refs_4_), channel_id=1, source_target_pairs={{0,16},{1,3},{2,18},{3,1},{4,20},{5,7},{6,22},{7,5},{8,24},{9,11},... | collective-permute-start | bytes 983048 | tf_op jit(solution)/shard_map/ppermute | solution.py:24
  26.6 7.1 %collective-permute-start.8 = (bf16[64,1280]{1,0:T(8,128)(2,1)S(1)}, bf16[64,1280]{1,0:T(8,128)(2,1)S(1)}, u32[]{:S(2)}, u32[]{:S(2)}) collective-permute-start(bf16[64,1280]{1,0:T(8,128)(2,1)S(1)} %collective-permute-done.2.refs_2_), channel_id=1, source_target_pairs={{0,2},{1,17},{2,0},{3,19},{4,6},{5,21},{6,4},{7,23},{8,10},{9,25},... | collective-permute-start | bytes 491528 | tf_op jit(solution)/shard_map/ppermute | solution.py:24
  33.7 1.4 %collective-permute-start.19 = (bf16[64,1280]{1,0:T(8,128)(2,1)S(1)}, bf16[64,1280]{1,0:T(8,128)(2,1)S(1)}, u32[]{:S(2)}, u32[]{:S(2)}) collective-permute-start(bf16[64,1280]{1,0:T(8,128)(2,1)S(1)} %collective-permute-done.9.refs_8_), channel_id=1, source_target_pairs={{0,1},{1,0},{2,3},{3,2},{4,5},{5,4},{6,7},{7,6},{8,9},{9,8},{10,11... | collective-permute-start | bytes 491528 | tf_op jit(solution)/shard_map/ppermute | solution.py:24
  33.7 4.2 %collective-permute-start.12 = (bf16[128,1280]{1,0:T(8,128)(2,1)S(1)}, bf16[128,1280]{1,0:T(8,128)(2,1)S(1)}, u32[]{:S(2)}, u32[]{:S(2)}) collective-permute-start(bf16[128,1280]{1,0:T(8,128)(2,1)S(1)} %collective-permute-done.1.refs_1_), channel_id=1, source_target_pairs={{0,1},{1,0},{2,3},{3,2},{4,5},{5,4},{6,7},{7,6},{8,9},{9,8},{10,11... | collective-permute-start | bytes 983048 | tf_op jit(solution)/shard_map/ppermute | solution.py:24
  34.2 1.6 %collective-permute-start.18 = (bf16[64,1280]{1,0:T(8,128)(2,1)S(1)}, bf16[64,1280]{1,0:T(8,128)(2,1)S(1)}, u32[]{:S(2)}, u32[]{:S(2)}) collective-permute-start(bf16[64,1280]{1,0:T(8,128)(2,1)S(1)} %collective-permute-done.8.refs_7_), channel_id=1, source_target_pairs={{0,1},{1,0},{2,3},{3,2},{4,5},{5,4},{6,7},{7,6},{8,9},{9,8},{10,11... | collective-permute-start | bytes 491528 | tf_op jit(solution)/shard_map/ppermute | solution.py:24
  35.1 2.8 %collective-permute-start.15 = (bf16[128,1280]{1,0:T(8,128)(2,1)S(1)}, bf16[128,1280]{1,0:T(8,128)(2,1)S(1)}, u32[]{:S(2)}, u32[]{:S(2)}) collective-permute-start(bf16[128,1280]{1,0:T(8,128)(2,1)S(1)} %collective-permute-done.5.refs_4_), channel_id=1, source_target_pairs={{0,1},{1,0},{2,3},{3,2},{4,5},{5,4},{6,7},{7,6},{8,9},{9,8},{10,11... | collective-permute-start | bytes 983048 | tf_op jit(solution)/shard_map/ppermute | solution.py:24
  35.2 2.7 %collective-permute-start.16 = (bf16[128,1280]{1,0:T(8,128)(2,1)S(1)}, bf16[128,1280]{1,0:T(8,128)(2,1)S(1)}, u32[]{:S(2)}, u32[]{:S(2)}) collective-permute-start(bf16[128,1280]{1,0:T(8,128)(2,1)S(1)} %collective-permute-done.6.refs_5_), channel_id=1, source_target_pairs={{0,1},{1,0},{2,3},{3,2},{4,5},{5,4},{6,7},{7,6},{8,9},{9,8},{10,11... | collective-permute-start | bytes 983048 | tf_op jit(solution)/shard_map/ppermute | solution.py:24
  35.6 2.3 %collective-permute-start.17 = (bf16[128,1280]{1,0:T(8,128)(2,1)S(1)}, bf16[128,1280]{1,0:T(8,128)(2,1)S(1)}, u32[]{:S(2)}, u32[]{:S(2)}) collective-permute-start(bf16[128,1280]{1,0:T(8,128)(2,1)S(1)} %collective-permute-done.7.refs_6_), channel_id=1, source_target_pairs={{0,1},{1,0},{2,3},{3,2},{4,5},{5,4},{6,7},{7,6},{8,9},{9,8},{10,11... | collective-permute-start | bytes 983048 | tf_op jit(solution)/shard_map/ppermute | solution.py:24
  35.8 2.1 %collective-permute-start.20 = (bf16[64,1280]{1,0:T(8,128)(2,1)S(1)}, bf16[64,1280]{1,0:T(8,128)(2,1)S(1)}, u32[]{:S(2)}, u32[]{:S(2)}) collective-permute-start(bf16[64,1280]{1,0:T(8,128)(2,1)S(1)} %collective-permute-done.10.refs_9_), channel_id=1, source_target_pairs={{0,1},{1,0},{2,3},{3,2},{4,5},{5,4},{6,7},{7,6},{8,9},{9,8},{10,11... | collective-permute-start | bytes 491528 | tf_op jit(solution)/shard_map/ppermute | solution.py:24

commit v6 on v5

--- a/solution.py
+++ b/solution.py
@@ -166,8 +166,7 @@
 
     spans = [(0, 1, 0, 10), (1, 4, 0, 14), (5, 4, 0, 18), (9, 4, 0, 22), (13, 4, 4, 22), (17, 4, 8, 22), (21, 1, 12, 22)]
 
-    for m in range(5):
-
+    def step_one(m, cubes):
         def kept(first, size):
             rows = []
             for w in range(first, first + size):
@@ -181,7 +180,7 @@
             columns = slice(left + at + low * block, left + at + high * block)
             return band_ref[at + first * block : at + (first + size) * block, columns]
 
-        for step, (first, size, low, high) in enumerate(spans):
+        for step, (first, size, low, high) in enumerate([] if cubes else spans):
             span = slice(first * block, (first + size) * block)
             other = m + step - 3
             if size == 4 and 0 <= other < m:
@@ -191,13 +190,19 @@
                 square = kept(first, size) * dot(rows(first, size, low, high), rows(half, 4, low, high), 1)
             square_ref[m, span, :] = square
             low_ref[m, span, :] = square.astype(bits)
-        for first, size, low, high in spans:
+        for first, size, low, high in spans if cubes else []:
             if half <= 4 * m + first < half + 20:
                 span = slice(first * block, (first + size) * block)
                 cube = dot(rows(first, size, low, high), low_ref[m, low * block : high * block, :])
                 current = kept(first, size) * (3.0 * square_ref[m, span, :] - 2.0 * cube)
                 at = 4 * m * block
                 next_ref[at + span.start : at + span.stop, at + 2 * block : at + 6 * block] = current.astype(bits)
+
+    for m in range(6):
+        if m < 5:
+            step_one(m, False)
+        if m > 0:
+            step_one(m - 1, True)
 
     inner = slice(half * block, (half + 20) * block)
     chosen = lax.broadcasted_iota(jnp.int32, (block, panel), 1)

time: 48.6 us -> 48.6 us (level)
  no operation moved by 1% of the time
where the time goes in v6:
time: 48.6 us; the launch traced here: 48.4 us
  starting transfers between devices  19.2 us (40%)
  waiting for transfers between devices  17.5 us (36%)
  Pallas kernels  11.6 us (24%)
    ppermute x22, starting transfers between devices, send(): lax.ppermute(value, AXES, [(s, t) for s, t in pairs if 0 <= t < count])  19.2 us
    ppermute x22, waiting for transfers between devices, send(): lax.ppermute(value, AXES, [(s, t) for s, t in pairs if 0 <= t < count])  17.5 us
    pallas_call x1, Pallas kernels, local(): pl.pallas_call(kernel, out_shape=jax.ShapeDtypeStruct((block, width), jnp...  10.5 us
    pallas_call x1, Pallas kernels, local(): pl.pallas_call(prepare_kernel, out_shape=pltpu.VMEM((block, width + block...  1.1 us
  transfers between devices with their start and end apart: 22, of which 6 were waited for; matrix products, arithmetic and copies ran while one was open for 0% of the time, Pallas kernels for 0%

profile of v6, /device:TPU:0, one launch (start us, length us, event | category | flops | bytes accessed | tf_op | source)
XLA Modules:
  0.0 48.4 jit_solution(17400480160332427531)
XLA Ops:
  0.0 1.1 %shard_map.28.refs_10_ = bf16[64,1280]{1,0:T(8,128)(2,1)S(1)} custom-call(f32[64,1216]{1,0:T(8,128)} %density_ref.1, s32[1,19]{1,0:T(1,128)} %pattern_ref.1), custom_call_target="tpu_custom_call" | custom-call | tf_op jit(solution)/shard_map/pallas_call | solution.py:237
  1.1 3.0 %collective-permute-start = (bf16[64,1280]{1,0:T(8,128)(2,1)S(1)}, bf16[64,1280]{1,0:T(8,128)(2,1)S(1)}, u32[]{:S(2)}, u32[]{:S(2)}) collective-permute-start(bf16[64,1280]{1,0:T(8,128)(2,1)S(1)} %shard_map.28.refs_10_), channel_id=1, source_target_pairs={{0,2},{1,17},{2,0},{3,19},{4,6},{5,21},{6,4},{7,23},{8,10},{9,25},... | collective-permute-start | bytes 491528 | tf_op jit(solution)/shard_map/ppermute | solution.py:24
  4.1 3.6 %collective-permute-start.4 = (bf16[64,1280]{1,0:T(8,128)(2,1)S(1)}, bf16[64,1280]{1,0:T(8,128)(2,1)S(1)}, u32[]{:S(2)}, u32[]{:S(2)}) collective-permute-start(bf16[64,1280]{1,0:T(8,128)(2,1)S(1)} %shard_map.28.refs_10_), channel_id=1, source_target_pairs={{0,12},{1,13},{2,14},{3,15},{4,0},{5,1},{6,2},{7,3},{8,4},{9,5},{1... | collective-permute-start | bytes 491528 | tf_op jit(solution)/shard_map/ppermute | solution.py:24
  7.7 0.0 collective-permute-start.3
  7.7 0.0 collective-permute-done.refs_0_
  7.7 2.8 %collective-permute-start.2 = (bf16[64,1280]{1,0:T(8,128)(2,1)S(1)}, bf16[64,1280]{1,0:T(8,128)(2,1)S(1)}, u32[]{:S(2)}, u32[]{:S(2)}) collective-permute-start(bf16[64,1280]{1,0:T(8,128)(2,1)S(1)} %shard_map.28.refs_10_), channel_id=1, source_target_pairs={{0,8},{1,9},{2,10},{3,11},{4,12},{5,13},{6,14},{7,15},{8,0},{9,1},... | collective-permute-start | bytes 491528 | tf_op jit(solution)/shard_map/ppermute | solution.py:24
  10.6 1.6 %collective-permute-start.1 = (bf16[128,1280]{1,0:T(8,128)(2,1)S(1)}, bf16[128,1280]{1,0:T(8,128)(2,1)S(1)}, u32[]{:S(2)}, u32[]{:S(2)}) collective-permute-start(bf16[128,1280]{1,0:T(8,128)(2,1)S(1)} %pad_maximum_fusion), channel_id=1, source_target_pairs={{0,16},{1,3},{2,18},{3,1},{4,20},{5,7},{6,22},{7,5},{8,24},{9,11},... | collective-permute-start | bytes 983048 | tf_op jit(solution)/shard_map/ppermute | solution.py:24
  12.1 4.6 %collective-permute-done.3 = bf16[64,1280]{1,0:T(8,128)(2,1)S(1)} collective-permute-done((bf16[64,1280]{1,0:T(8,128)(2,1)S(1)}, bf16[64,1280]{1,0:T(8,128)(2,1)S(1)}, u32[]{:S(2)}, u32[]{:S(2)}) %collective-permute-start.3) | collective-permute-done | bytes 163872 | tf_op jit(solution)/shard_map/ppermute | solution.py:24
  16.8 0.5 %collective-permute-start.5 = (bf16[128,1280]{1,0:T(8,128)(2,1)S(1)}, bf16[128,1280]{1,0:T(8,128)(2,1)S(1)}, u32[]{:S(2)}, u32[]{:S(2)}) collective-permute-start(bf16[128,1280]{1,0:T(8,128)(2,1)S(1)} %constant_dynamic-update-slice_fusion.refs_3_), channel_id=1, source_target_pairs={{0,2},{1,17},{2,0},{3,19},{4,6},{5,21},{6,4},{7,23},{8,10},{9,25},... | collective-permute-start | bytes 983048 | tf_op jit(solution)/shard_map/ppermute | solution.py:24
  17.3 0.0 collective-permute-start.21
  17.3 0.5 %collective-permute-start.11 = (bf16[64,1280]{1,0:T(8,128)(2,1)S(1)}, bf16[64,1280]{1,0:T(8,128)(2,1)S(1)}, u32[]{:S(2)}, u32[]{:S(2)}) collective-permute-start(bf16[64,1280]{1,0:T(8,128)(2,1)S(1)} %collective-permute-done.refs_0_), channel_id=1, source_target_pairs={{0,1},{1,0},{2,3},{3,2},{4,5},{5,4},{6,7},{7,6},{8,9},{9,8},{10,11... | collective-permute-start | bytes 491528 | tf_op jit(solution)/shard_map/ppermute | solution.py:24
  17.8 3.4 %collective-permute-done.2.refs_2_ = bf16[64,1280]{1,0:T(8,128)(2,1)S(1)} collective-permute-done((bf16[64,1280]{1,0:T(8,128)(2,1)S(1)}, bf16[64,1280]{1,0:T(8,128)(2,1)S(1)}, u32[]{:S(2)}, u32[]{:S(2)}) %collective-permute-start.2) | collective-permute-done | bytes 163872 | tf_op jit(solution)/shard_map/ppermute | solution.py:24
  21.2 0.0 collective-permute-start.13
  21.2 1.3 %collective-permute-start.9 = (bf16[64,1280]{1,0:T(8,128)(2,1)S(1)}, bf16[64,1280]{1,0:T(8,128)(2,1)S(1)}, u32[]{:S(2)}, u32[]{:S(2)}) collective-permute-start(bf16[64,1280]{1,0:T(8,128)(2,1)S(1)} %collective-permute-done.2.refs_2_), channel_id=1, source_target_pairs={{0,16},{1,3},{2,18},{3,1},{4,20},{5,7},{6,22},{7,5},{8,24},{9,11},... | collective-permute-start | bytes 491528 | tf_op jit(solution)/shard_map/ppermute | solution.py:24
  22.5 0.5 %collective-permute-start.14 = (bf16[128,1280]{1,0:T(8,128)(2,1)S(1)}, bf16[128,1280]{1,0:T(8,128)(2,1)S(1)}, u32[]{:S(2)}, u32[]{:S(2)}) collective-permute-start(bf16[128,1280]{1,0:T(8,128)(2,1)S(1)} %constant_dynamic-update-slice_fusion.refs_3_), channel_id=1, source_target_pairs={{0,1},{1,0},{2,3},{3,2},{4,5},{5,4},{6,7},{7,6},{8,9},{9,8},{10,11... | collective-permute-start | bytes 983048 | tf_op jit(solution)/shard_map/ppermute | solution.py:24
  23.1 0.1 collective-permute-start.10
  23.2 1.1 %collective-permute-start.6 = (bf16[128,1280]{1,0:T(8,128)(2,1)S(1)}, bf16[128,1280]{1,0:T(8,128)(2,1)S(1)}, u32[]{:S(2)}, u32[]{:S(2)}) collective-permute-start(bf16[128,1280]{1,0:T(8,128)(2,1)S(1)} %constant_dynamic-update-slice_fusion.refs_3_), channel_id=1, source_target_pairs={{0,16},{1,3},{2,18},{3,1},{4,20},{5,7},{6,22},{7,5},{8,24},{9,11},... | collective-permute-start | bytes 983048 | tf_op jit(solution)/shard_map/ppermute | solution.py:24
  24.3 1.1 %collective-permute-start.7 = (bf16[128,1280]{1,0:T(8,128)(2,1)S(1)}, bf16[128,1280]{1,0:T(8,128)(2,1)S(1)}, u32[]{:S(2)}, u32[]{:S(2)}) collective-permute-start(bf16[128,1280]{1,0:T(8,128)(2,1)S(1)} %collective-permute-done.5.refs_4_), channel_id=1, source_target_pairs={{0,16},{1,3},{2,18},{3,1},{4,20},{5,7},{6,22},{7,5},{8,24},{9,11},... | collective-permute-start | bytes 983048 | tf_op jit(solution)/shard_map/ppermute | solution.py:24
  25.4 1.2 %collective-permute-done.9.refs_8_ = bf16[64,1280]{1,0:T(8,128)(2,1)S(1)} collective-permute-done((bf16[64,1280]{1,0:T(8,128)(2,1)S(1)}, bf16[64,1280]{1,0:T(8,128)(2,1)S(1)}, u32[]{:S(2)}, u32[]{:S(2)}) %collective-permute-start.9) | collective-permute-done | bytes 163872 | tf_op jit(solution)/shard_map/ppermute | solution.py:24
  26.6 1.5 %collective-permute-start.8 = (bf16[64,1280]{1,0:T(8,128)(2,1)S(1)}, bf16[64,1280]{1,0:T(8,128)(2,1)S(1)}, u32[]{:S(2)}, u32[]{:S(2)}) collective-permute-start(bf16[64,1280]{1,0:T(8,128)(2,1)S(1)} %collective-permute-done.2.refs_2_), channel_id=1, source_target_pairs={{0,2},{1,17},{2,0},{3,19},{4,6},{5,21},{6,4},{7,23},{8,10},{9,25},... | collective-permute-start | bytes 491528 | tf_op jit(solution)/shard_map/ppermute | solution.py:24
  28.1 5.6 %collective-permute-done.10.refs_9_ = bf16[64,1280]{1,0:T(8,128)(2,1)S(1)} collective-permute-done((bf16[64,1280]{1,0:T(8,128)(2,1)S(1)}, bf16[64,1280]{1,0:T(8,128)(2,1)S(1)}, u32[]{:S(2)}, u32[]{:S(2)}) %collective-permute-start.10) | collective-permute-done | bytes 163872 | tf_op jit(solution)/shard_map/ppermute | solution.py:24
  33.7 0.0 collective-permute-done.8.refs_7_
  33.7 0.5 %collective-permute-start.12 = (bf16[128,1280]{1,0:T(8,128)(2,1)S(1)}, bf16[128,1280]{1,0:T(8,128)(2,1)S(1)}, u32[]{:S(2)}, u32[]{:S(2)}) collective-permute-start(bf16[128,1280]{1,0:T(8,128)(2,1)S(1)} %collective-permute-done.1.refs_1_), channel_id=1, source_target_pairs={{0,1},{1,0},{2,3},{3,2},{4,5},{5,4},{6,7},{7,6},{8,9},{9,8},{10,11... | collective-permute-start | bytes 983048 | tf_op jit(solution)/shard_map/ppermute | solution.py:24
  34.2 0.1 collective-permute-start.18
  34.3 0.8 %collective-permute-done.19.refs_19_ = bf16[64,1280]{1,0:T(8,128)(2,1)S(1)} collective-permute-done((bf16[64,1280]{1,0:T(8,128)(2,1)S(1)}, bf16[64,1280]{1,0:T(8,128)(2,1)S(1)}, u32[]{:S(2)}, u32[]{:S(2)}) %collective-permute-start.19) | collective-permute-done | bytes 163872 | tf_op jit(solution)/shard_map/ppermute | solution.py:24
  35.1 0.1 collective-permute-start.15
  35.2 0.4 collective-permute-start.16
  35.6 0.1 collective-permute-start.17
  35.7 0.0 collective-permute-done.18.refs_18_
  35.8 0.3 collective-permute-start.20
  36.1 1.8 %collective-permute-done.20.refs_20_ = bf16[64,1280]{1,0:T(8,128)(2,1)S(1)} collective-permute-done((bf16[64,1280]{1,0:T(8,128)(2,1)S(1)}, bf16[64,1280]{1,0:T(8,128)(2,1)S(1)}, u32[]{:S(2)}, u32[]{:S(2)}) %collective-permute-start.20) | collective-permute-done | bytes 163872 | tf_op jit(solution)/shard_map/ppermute | solution.py:24
  37.9 10.5 %shard_map.29 = f32[64,1216]{1,0:T(8,128)} custom-call(bf16[64,1280]{1,0:T(8,128)(2,1)S(1)} %collective-permute-done.refs_0_, bf16[128,1280]{1,0:T(8,128)(2,1)S(1)} %collective-permute-done.1.refs_1_, bf16[64,1280]{1,0:T(8,128)(2,1)S(1)} %collective-permute-done.2.refs_2_, bf16[128,1280]{1,0:T(8,128)(2,1)S(1)} %constant_dynamic-update-slice_fusion.refs_3_, ...), custom_call_target="tpu_custom_call" | custom-call | tf_op jit(solution)/shard_map/pallas_call | solution.py:258
  (18 shorter events, 0.1 us)
Async XLA Ops:
  1.1 6.6 %collective-permute-start = (bf16[64,1280]{1,0:T(8,128)(2,1)S(1)}, bf16[64,1280]{1,0:T(8,128)(2,1)S(1)}, u32[]{:S(2)}, u32[]{:S(2)}) collective-permute-start(bf16[64,1280]{1,0:T(8,128)(2,1)S(1)} %shard_map.28.refs_10_), channel_id=1, source_target_pairs={{0,2},{1,17},{2,0},{3,19},{4,6},{5,21},{6,4},{7,23},{8,10},{9,25},... | collective-permute-start | bytes 491528 | tf_op jit(solution)/shard_map/ppermute | solution.py:24
  4.1 12.6 %collective-permute-start.4 = (bf16[64,1280]{1,0:T(8,128)(2,1)S(1)}, bf16[64,1280]{1,0:T(8,128)(2,1)S(1)}, u32[]{:S(2)}, u32[]{:S(2)}) collective-permute-start(bf16[64,1280]{1,0:T(8,128)(2,1)S(1)} %shard_map.28.refs_10_), channel_id=1, source_target_pairs={{0,12},{1,13},{2,14},{3,15},{4,0},{5,1},{6,2},{7,3},{8,4},{9,5},{1... | collective-permute-start | bytes 491528 | tf_op jit(solution)/shard_map/ppermute | solution.py:24
  7.7 9.0 %collective-permute-start.3 = (bf16[64,1280]{1,0:T(8,128)(2,1)S(1)}, bf16[64,1280]{1,0:T(8,128)(2,1)S(1)}, u32[]{:S(2)}, u32[]{:S(2)}) collective-permute-start(bf16[64,1280]{1,0:T(8,128)(2,1)S(1)} %shard_map.28.refs_10_), channel_id=1, source_target_pairs={{0,4},{1,5},{2,6},{3,7},{4,8},{5,9},{6,10},{7,11},{8,12},{9,13},{1... | collective-permute-start | bytes 491528 | tf_op jit(solution)/shard_map/ppermute | solution.py:24
  7.7 13.5 %collective-permute-start.2 = (bf16[64,1280]{1,0:T(8,128)(2,1)S(1)}, bf16[64,1280]{1,0:T(8,128)(2,1)S(1)}, u32[]{:S(2)}, u32[]{:S(2)}) collective-permute-start(bf16[64,1280]{1,0:T(8,128)(2,1)S(1)} %shard_map.28.refs_10_), channel_id=1, source_target_pairs={{0,8},{1,9},{2,10},{3,11},{4,12},{5,13},{6,14},{7,15},{8,0},{9,1},... | collective-permute-start | bytes 491528 | tf_op jit(solution)/shard_map/ppermute | solution.py:24
  10.6 10.7 %collective-permute-start.1 = (bf16[128,1280]{1,0:T(8,128)(2,1)S(1)}, bf16[128,1280]{1,0:T(8,128)(2,1)S(1)}, u32[]{:S(2)}, u32[]{:S(2)}) collective-permute-start(bf16[128,1280]{1,0:T(8,128)(2,1)S(1)} %pad_maximum_fusion), channel_id=1, source_target_pairs={{0,16},{1,3},{2,18},{3,1},{4,20},{5,7},{6,22},{7,5},{8,24},{9,11},... | collective-permute-start | bytes 983048 | tf_op jit(solution)/shard_map/ppermute | solution.py:24
  16.8 7.5 %collective-permute-start.5 = (bf16[128,1280]{1,0:T(8,128)(2,1)S(1)}, bf16[128,1280]{1,0:T(8,128)(2,1)S(1)}, u32[]{:S(2)}, u32[]{:S(2)}) collective-permute-start(bf16[128,1280]{1,0:T(8,128)(2,1)S(1)} %constant_dynamic-update-slice_fusion.refs_3_), channel_id=1, source_target_pairs={{0,2},{1,17},{2,0},{3,19},{4,6},{5,21},{6,4},{7,23},{8,10},{9,25},... | collective-permute-start | bytes 983048 | tf_op jit(solution)/shard_map/ppermute | solution.py:24
  17.3 5.2 %collective-permute-start.21 = (bf16[64,1280]{1,0:T(8,128)(2,1)S(1)}, bf16[64,1280]{1,0:T(8,128)(2,1)S(1)}, u32[]{:S(2)}, u32[]{:S(2)}) collective-permute-start(bf16[64,1280]{1,0:T(8,128)(2,1)S(1)} %shard_map.28.refs_10_), channel_id=1, source_target_pairs={{0,1},{1,0},{2,3},{3,2},{4,5},{5,4},{6,7},{7,6},{8,9},{9,8},{10,11... | collective-permute-start | bytes 491528 | tf_op jit(solution)/shard_map/ppermute | solution.py:24
  17.3 5.8 %collective-permute-start.11 = (bf16[64,1280]{1,0:T(8,128)(2,1)S(1)}, bf16[64,1280]{1,0:T(8,128)(2,1)S(1)}, u32[]{:S(2)}, u32[]{:S(2)}) collective-permute-start(bf16[64,1280]{1,0:T(8,128)(2,1)S(1)} %collective-permute-done.refs_0_), channel_id=1, source_target_pairs={{0,1},{1,0},{2,3},{3,2},{4,5},{5,4},{6,7},{7,6},{8,9},{9,8},{10,11... | collective-permute-start | bytes 491528 | tf_op jit(solution)/shard_map/ppermute | solution.py:24
  21.2 2.0 %collective-permute-start.13 = (bf16[64,1280]{1,0:T(8,128)(2,1)S(1)}, bf16[64,1280]{1,0:T(8,128)(2,1)S(1)}, u32[]{:S(2)}, u32[]{:S(2)}) collective-permute-start(bf16[64,1280]{1,0:T(8,128)(2,1)S(1)} %collective-permute-done.2.refs_2_), channel_id=1, source_target_pairs={{0,1},{1,0},{2,3},{3,2},{4,5},{5,4},{6,7},{7,6},{8,9},{9,8},{10,11... | collective-permute-start | bytes 491528 | tf_op jit(solution)/shard_map/ppermute | solution.py:24
  21.2 5.3 %collective-permute-start.9 = (bf16[64,1280]{1,0:T(8,128)(2,1)S(1)}, bf16[64,1280]{1,0:T(8,128)(2,1)S(1)}, u32[]{:S(2)}, u32[]{:S(2)}) collective-permute-start(bf16[64,1280]{1,0:T(8,128)(2,1)S(1)} %collective-permute-done.2.refs_2_), channel_id=1, source_target_pairs={{0,16},{1,3},{2,18},{3,1},{4,20},{5,7},{6,22},{7,5},{8,24},{9,11},... | collective-permute-start | bytes 491528 | tf_op jit(solution)/shard_map/ppermute | solution.py:24
  22.5 11.7 %collective-permute-start.14 = (bf16[128,1280]{1,0:T(8,128)(2,1)S(1)}, bf16[128,1280]{1,0:T(8,128)(2,1)S(1)}, u32[]{:S(2)}, u32[]{:S(2)}) collective-permute-start(bf16[128,1280]{1,0:T(8,128)(2,1)S(1)} %constant_dynamic-update-slice_fusion.refs_3_), channel_id=1, source_target_pairs={{0,1},{1,0},{2,3},{3,2},{4,5},{5,4},{6,7},{7,6},{8,9},{9,8},{10,11... | collective-permute-start | bytes 983048 | tf_op jit(solution)/shard_map/ppermute | solution.py:24
  23.1 10.6 %collective-permute-start.10 = (bf16[64,1280]{1,0:T(8,128)(2,1)S(1)}, bf16[64,1280]{1,0:T(8,128)(2,1)S(1)}, u32[]{:S(2)}, u32[]{:S(2)}) collective-permute-start(bf16[64,1280]{1,0:T(8,128)(2,1)S(1)} %slice.4), channel_id=1, source_target_pairs={{0,8},{1,9},{2,10},{3,11},{4,12},{5,13},{6,14},{7,15},{8,0},{9,1},... | collective-permute-start | bytes 491528 | tf_op jit(solution)/shard_map/ppermute | solution.py:24
  23.2 12.0 %collective-permute-start.6 = (bf16[128,1280]{1,0:T(8,128)(2,1)S(1)}, bf16[128,1280]{1,0:T(8,128)(2,1)S(1)}, u32[]{:S(2)}, u32[]{:S(2)}) collective-permute-start(bf16[128,1280]{1,0:T(8,128)(2,1)S(1)} %constant_dynamic-update-slice_fusion.refs_3_), channel_id=1, source_target_pairs={{0,16},{1,3},{2,18},{3,1},{4,20},{5,7},{6,22},{7,5},{8,24},{9,11},... | collective-permute-start | bytes 983048 | tf_op jit(solution)/shard_map/ppermute | solution.py:24
  24.3 11.3 %collective-permute-start.7 = (bf16[128,1280]{1,0:T(8,128)(2,1)S(1)}, bf16[128,1280]{1,0:T(8,128)(2,1)S(1)}, u32[]{:S(2)}, u32[]{:S(2)}) collective-permute-start(bf16[128,1280]{1,0:T(8,128)(2,1)S(1)} %collective-permute-done.5.refs_4_), channel_id=1, source_target_pairs={{0,16},{1,3},{2,18},{3,1},{4,20},{5,7},{6,22},{7,5},{8,24},{9,11},... | collective-permute-start | bytes 983048 | tf_op jit(solution)/shard_map/ppermute | solution.py:24
  26.6 7.1 %collective-permute-start.8 = (bf16[64,1280]{1,0:T(8,128)(2,1)S(1)}, bf16[64,1280]{1,0:T(8,128)(2,1)S(1)}, u32[]{:S(2)}, u32[]{:S(2)}) collective-permute-start(bf16[64,1280]{1,0:T(8,128)(2,1)S(1)} %collective-permute-done.2.refs_2_), channel_id=1, source_target_pairs={{0,2},{1,17},{2,0},{3,19},{4,6},{5,21},{6,4},{7,23},{8,10},{9,25},... | collective-permute-start | bytes 491528 | tf_op jit(solution)/shard_map/ppermute | solution.py:24
  33.7 1.4 %collective-permute-start.19 = (bf16[64,1280]{1,0:T(8,128)(2,1)S(1)}, bf16[64,1280]{1,0:T(8,128)(2,1)S(1)}, u32[]{:S(2)}, u32[]{:S(2)}) collective-permute-start(bf16[64,1280]{1,0:T(8,128)(2,1)S(1)} %collective-permute-done.9.refs_8_), channel_id=1, source_target_pairs={{0,1},{1,0},{2,3},{3,2},{4,5},{5,4},{6,7},{7,6},{8,9},{9,8},{10,11... | collective-permute-start | bytes 491528 | tf_op jit(solution)/shard_map/ppermute | solution.py:24
  33.7 4.2 %collective-permute-start.12 = (bf16[128,1280]{1,0:T(8,128)(2,1)S(1)}, bf16[128,1280]{1,0:T(8,128)(2,1)S(1)}, u32[]{:S(2)}, u32[]{:S(2)}) collective-permute-start(bf16[128,1280]{1,0:T(8,128)(2,1)S(1)} %collective-permute-done.1.refs_1_), channel_id=1, source_target_pairs={{0,1},{1,0},{2,3},{3,2},{4,5},{5,4},{6,7},{7,6},{8,9},{9,8},{10,11... | collective-permute-start | bytes 983048 | tf_op jit(solution)/shard_map/ppermute | solution.py:24
  34.2 1.6 %collective-permute-start.18 = (bf16[64,1280]{1,0:T(8,128)(2,1)S(1)}, bf16[64,1280]{1,0:T(8,128)(2,1)S(1)}, u32[]{:S(2)}, u32[]{:S(2)}) collective-permute-start(bf16[64,1280]{1,0:T(8,128)(2,1)S(1)} %collective-permute-done.8.refs_7_), channel_id=1, source_target_pairs={{0,1},{1,0},{2,3},{3,2},{4,5},{5,4},{6,7},{7,6},{8,9},{9,8},{10,11... | collective-permute-start | bytes 491528 | tf_op jit(solution)/shard_map/ppermute | solution.py:24
  35.1 2.8 %collective-permute-start.15 = (bf16[128,1280]{1,0:T(8,128)(2,1)S(1)}, bf16[128,1280]{1,0:T(8,128)(2,1)S(1)}, u32[]{:S(2)}, u32[]{:S(2)}) collective-permute-start(bf16[128,1280]{1,0:T(8,128)(2,1)S(1)} %collective-permute-done.5.refs_4_), channel_id=1, source_target_pairs={{0,1},{1,0},{2,3},{3,2},{4,5},{5,4},{6,7},{7,6},{8,9},{9,8},{10,11... | collective-permute-start | bytes 983048 | tf_op jit(solution)/shard_map/ppermute | solution.py:24
  35.2 2.7 %collective-permute-start.16 = (bf16[128,1280]{1,0:T(8,128)(2,1)S(1)}, bf16[128,1280]{1,0:T(8,128)(2,1)S(1)}, u32[]{:S(2)}, u32[]{:S(2)}) collective-permute-start(bf16[128,1280]{1,0:T(8,128)(2,1)S(1)} %collective-permute-done.6.refs_5_), channel_id=1, source_target_pairs={{0,1},{1,0},{2,3},{3,2},{4,5},{5,4},{6,7},{7,6},{8,9},{9,8},{10,11... | collective-permute-start | bytes 983048 | tf_op jit(solution)/shard_map/ppermute | solution.py:24
  35.6 2.3 %collective-permute-start.17 = (bf16[128,1280]{1,0:T(8,128)(2,1)S(1)}, bf16[128,1280]{1,0:T(8,128)(2,1)S(1)}, u32[]{:S(2)}, u32[]{:S(2)}) collective-permute-start(bf16[128,1280]{1,0:T(8,128)(2,1)S(1)} %collective-permute-done.7.refs_6_), channel_id=1, source_target_pairs={{0,1},{1,0},{2,3},{3,2},{4,5},{5,4},{6,7},{7,6},{8,9},{9,8},{10,11... | collective-permute-start | bytes 983048 | tf_op jit(solution)/shard_map/ppermute | solution.py:24
  35.8 2.1 %collective-permute-start.20 = (bf16[64,1280]{1,0:T(8,128)(2,1)S(1)}, bf16[64,1280]{1,0:T(8,128)(2,1)S(1)}, u32[]{:S(2)}, u32[]{:S(2)}) collective-permute-start(bf16[64,1280]{1,0:T(8,128)(2,1)S(1)} %collective-permute-done.10.refs_9_), channel_id=1, source_target_pairs={{0,1},{1,0},{2,3},{3,2},{4,5},{5,4},{6,7},{7,6},{8,9},{9,8},{10,11... | collective-permute-start | bytes 491528 | tf_op jit(solution)/shard_map/ppermute | solution.py:24
